TPU v7x, 32 devices: a whole 2x2x4 slice. The times are simulated.
32 devices in a mesh: seq: 2 (over x), dp: 16 (over z, y, core).
Axes of the slice: x: 2, y: 2, z: 4, core: 2. Of those that a mesh axis runs over, the one named last changes fastest.
Arguments:
- latents: float32 [64, 256, 16], P('dp', 'seq'), may hold values from -6 to 6
- noise_target: float32 [64, 256, 16], P('dp', 'seq'), may hold values from -6 to 6
- pad_mask: int32 [64, 256], P('dp', 'seq'), may hold values from 0 to 1, as said below
- labels: int32 [64], P('dp'), may hold values from 0 to 1000
- timesteps: int32 [64], P('dp'), may hold values from 0 to 999
- embed_rows: float32 [1296, 1024], P(None, 'dp')
- first_embed: float32 [1296, 1024], P(None, 'dp'), may hold values from -24 to 24
- second_embed: float32 [1296, 1024], P(None, 'dp'), may hold values from 0.73728 to 11.79648
- class_table: float32 [1001, 1024], P(None, 'dp'), may hold values from -3 to 3
- first_table: float32 [1001, 1024], P(None, 'dp'), may hold values from -4 to 4
- second_table: float32 [1001, 1024], P(None, 'dp'), may hold values from 0.025 to 0.4
- qkv_weight: float32 [2, 1024, 3072], P(None, 'dp'), may hold values from -0.1875 to 0.1875
- first_qkv: float32 [2, 1024, 3072], P(None, 'dp'), may hold values from -14 to 14
- second_qkv: float32 [2, 1024, 3072], P(None, 'dp'), may hold values from 0.180224 to 2.94912
- proj_weight: float32 [2, 1024, 1024], P(None, 'dp'), may hold values from -0.75 to 0.75
- first_proj: float32 [2, 1024, 1024], P(None, 'dp'), may hold values from -14 to 14
- second_proj: float32 [2, 1024, 1024], P(None, 'dp'), may hold values from 0.180224 to 2.94912
- up_weight: float32 [2, 1024, 4096], P(None, 'dp'), may hold values from -0.1875 to 0.1875
- first_up: float32 [2, 1024, 4096], P(None, 'dp'), may hold values from -14 to 14
- second_up: float32 [2, 1024, 4096], P(None, 'dp'), may hold values from 0.180224 to 2.94912
- down_weight: float32 [2, 4096, 1024], P(None, 'dp'), may hold values from -0.09375 to 0.09375
- first_down: float32 [2, 4096, 1024], P(None, 'dp'), may hold values from -14 to 14
- second_down: float32 [2, 4096, 1024], P(None, 'dp'), may hold values from 0.180224 to 2.94912
- cond_weight: float32 [1024, 14336], P('dp'), may hold values from -0.1875 to 0.1875
- first_cond: float32 [1024, 14336], P('dp'), may hold values from -12 to 12
- second_cond: float32 [1024, 14336], P('dp'), may hold values from 0.1856 to 2.944
- head_weight: float32 [1024, 32], P('dp'), may hold values from -0.1875 to 0.1875
- first_head: float32 [1024, 32], P('dp'), may hold values from -224 to 224
- second_head: float32 [1024, 32], P('dp'), may hold values from 65.536 to 1032.192
- all_biases: float32 [35872], replicated, may hold values from -3 to 3
- first_bias: float32 [35872], replicated, may hold values from -24 to 24
- second_bias: float32 [35872], replicated, may hold values from 0.73728 to 11.79648
Outputs:
- loss_sum: float32 [], replicated
- loss_count: float32 [], replicated
- new_embed: float32 [1296, 1024], P(None, 'dp')
- new_first_embed: float32 [1296, 1024], P(None, 'dp')
- new_second_embed: float32 [1296, 1024], P(None, 'dp')
- new_table: float32 [1001, 1024], P(None, 'dp')
- new_first_table: float32 [1001, 1024], P(None, 'dp')
- new_second_table: float32 [1001, 1024], P(None, 'dp')
- new_qkv: float32 [2, 1024, 3072], P(None, 'dp')
- new_first_qkv: float32 [2, 1024, 3072], P(None, 'dp')
- new_second_qkv: float32 [2, 1024, 3072], P(None, 'dp')
- new_proj: float32 [2, 1024, 1024], P(None, 'dp')
- new_first_proj: float32 [2, 1024, 1024], P(None, 'dp')
- new_second_proj: float32 [2, 1024, 1024], P(None, 'dp')
- new_up: float32 [2, 1024, 4096], P(None, 'dp')
- new_first_up: float32 [2, 1024, 4096], P(None, 'dp')
- new_second_up: float32 [2, 1024, 4096], P(None, 'dp')
- new_down: float32 [2, 4096, 1024], P(None, 'dp')
- new_first_down: float32 [2, 4096, 1024], P(None, 'dp')
- new_second_down: float32 [2, 4096, 1024], P(None, 'dp')
- new_cond: float32 [1024, 14336], P('dp')
- new_first_cond: float32 [1024, 14336], P('dp')
- new_second_cond: float32 [1024, 14336], P('dp')
- new_head: float32 [1024, 32], P('dp')
- new_first_head: float32 [1024, 32], P('dp')
- new_second_head: float32 [1024, 32], P('dp')
- new_bias: float32 [35872], replicated
- new_first_bias: float32 [35872], replicated
- new_second_bias: float32 [35872], replicated
Inputs may be any that keep to these rules, and one draw needn't show every extreme that they name: `pad_mask`: each image's real tokens form a prefix of 32 or more tokens; among each 4 consecutive images one is real in all 256 tokens.
All inputs are finite; a program needn't handle non-finite values.
Results may differ from a plain program's by a relative error of at most 0.017.
Values may be sent and summed in bfloat16 or wider, within the bound.
A program may use at most 448 MiB of HBM per device.

v0:
```python
import math

import jax
import jax.numpy as jnp
from jax import lax
from jax.sharding import PartitionSpec as P

D = 1024
HEADS = 16
HEAD_DIM = 64
FF = 4096
NCLASS = 1001
FREQ = 256
OUT_CH = 32
PATCH_IN = 16
GRID = 16
LAYERS = 2
STEP = 10
NBIAS = 35872


BETA_ONE = 0.9
BETA_TWO = 0.999
EPSILON = 1e-08
DECAY = 0.01
RATE_MATRIX = 0.06
RATE_TABLE = 0.4
RATE_BIAS = 0.2


def matdot(left, right):
    return jnp.dot(left, right, preferred_element_type=jnp.float32)


def layer_norm(stream):
    row_mean = jnp.mean(stream, axis=-1, keepdims=True)
    centered = stream - row_mean
    variance = jnp.mean(centered * centered, axis=-1, keepdims=True)
    return centered * lax.rsqrt(variance + 1e-06)


def modulate(stream, shift_by, scale_by):
    return layer_norm(stream) * (1.0 + scale_by[:, None, :]) + shift_by[:, None, :]


def position_table(position_ids, feature_width, grid_side):
    quarter_width = feature_width // 4
    omegas = 1.0 / 10000.0 ** (jnp.arange(quarter_width, dtype=jnp.float32) / quarter_width)
    col_angle = (position_ids % grid_side).astype(jnp.float32)[:, None] * omegas[None, :]
    row_angle = (position_ids // grid_side).astype(jnp.float32)[:, None] * omegas[None, :]
    return jnp.concatenate(
        [jnp.sin(col_angle), jnp.cos(col_angle), jnp.sin(row_angle), jnp.cos(row_angle)], axis=1
    )


def time_features(timesteps, feature_width):
    half_width = feature_width // 2
    frequencies = jnp.exp(
        -math.log(10000.0) * jnp.arange(half_width, dtype=jnp.float32) / half_width
    )
    angles = timesteps.astype(jnp.float32)[:, None] * frequencies[None, :]
    return jnp.concatenate([jnp.cos(angles), jnp.sin(angles)], axis=1)


def column_sum(grad_bf):
    return jnp.sum(grad_bf.astype(jnp.float32), axis=0)


def split_six(modul):
    return [modul[:, piece * D : (piece + 1) * D] for piece in range(6)]


def layer_forward(stream, modul, weight_set, bias_part, pad_mask):
    w_qkv, w_proj, w_up, w_down = weight_set
    images, tok_rows, _ = stream.shape
    seq_parts = lax.axis_size("seq")
    local_heads = HEADS // seq_parts
    full_rows = tok_rows * seq_parts
    shift_one, scale_one, gate_one, shift_two, scale_two, gate_two = split_six(modul)
    a_one = (
        modulate(stream, shift_one, scale_one).astype(jnp.bfloat16).reshape(images * tok_rows, D)
    )
    qkv_all = (matdot(a_one, w_qkv) + bias_part[: 3 * D]).astype(jnp.bfloat16)
    qkv_all = qkv_all.reshape(images, tok_rows, 3, seq_parts, D // seq_parts)
    flags = jnp.broadcast_to(pad_mask[:, :, None, None, None], (images, tok_rows, 1, seq_parts, 1))
    heads_in, flags = (
        lax.all_to_all(qkv_all, "seq", split_axis=3, concat_axis=1, tiled=True),
        lax.all_to_all(flags, "seq", split_axis=3, concat_axis=1, tiled=True),
    )
    heads_in = heads_in.reshape(images, full_rows, 3, local_heads, HEAD_DIM)
    queries, key_rows, value_rows = (heads_in[:, :, 0], heads_in[:, :, 1], heads_in[:, :, 2])
    valid_keys = flags.reshape(images, full_rows)
    scores = jnp.einsum(
        "bqhd,bkhd->bhqk", queries, key_rows, preferred_element_type=jnp.float32
    ) * HEAD_DIM ** (-0.5)
    attn_probs = jax.nn.softmax(
        jnp.where(valid_keys[:, None, None, :] > 0, scores, -1000000000.0), axis=-1
    )
    heads_out = jnp.einsum(
        "bhqk,bkhd->bqhd",
        attn_probs.astype(jnp.bfloat16),
        value_rows,
        preferred_element_type=jnp.float32,
    )
    heads_out = heads_out.astype(jnp.bfloat16).reshape(images, full_rows, local_heads * HEAD_DIM)
    merged = lax.all_to_all(heads_out, "seq", split_axis=1, concat_axis=2, tiled=True).reshape(
        images * tok_rows, D
    )
    attn_out = (matdot(merged, w_proj) + bias_part[3 * D : 4 * D]).reshape(images, tok_rows, D)
    stream_one = stream + gate_one[:, None, :] * attn_out
    a_two = (
        modulate(stream_one, shift_two, scale_two)
        .astype(jnp.bfloat16)
        .reshape(images * tok_rows, D)
    )
    up_pre = matdot(a_two, w_up) + bias_part[4 * D : 4 * D + FF]
    activated = jax.nn.gelu(up_pre, approximate=True).astype(jnp.bfloat16)
    down_out = (matdot(activated, w_down) + bias_part[4 * D + FF :]).reshape(images, tok_rows, D)
    stream_two = stream_one + gate_two[:, None, :] * down_out
    saved = (
        a_one,
        queries,
        key_rows,
        value_rows,
        attn_probs,
        merged,
        attn_out,
        stream_one,
        a_two,
        up_pre,
        activated,
        down_out,
    )
    return (stream_two, saved)


def layer_backward(grad_in, stream, modul, weight_set, saved):
    w_qkv, w_proj, w_up, w_down = weight_set
    (
        a_one,
        queries,
        key_rows,
        value_rows,
        attn_probs,
        merged,
        attn_out,
        stream_one,
        a_two,
        up_pre,
        activated,
        down_out,
    ) = saved
    images, tok_rows, _ = stream.shape
    full_rows = queries.shape[1]
    local_heads = queries.shape[2]
    shift_one, scale_one, gate_one, shift_two, scale_two, gate_two = split_six(modul)
    d_gate_two = jnp.sum(grad_in * down_out, axis=1)
    d_down = (grad_in * gate_two[:, None, :]).astype(jnp.bfloat16).reshape(images * tok_rows, D)
    g_down = matdot(activated.T, d_down)
    d_activated = matdot(d_down, w_down.T)
    _, gelu_back = jax.vjp(lambda inner: jax.nn.gelu(inner, approximate=True), up_pre)
    d_up = gelu_back(d_activated)[0].astype(jnp.bfloat16)
    g_up = matdot(a_two.T, d_up)
    d_a_two = matdot(d_up, w_up.T).reshape(images, tok_rows, D)
    _, mod_back_two = jax.vjp(modulate, stream_one, shift_two, scale_two)
    d_stream_one, d_shift_two, d_scale_two = mod_back_two(d_a_two)
    d_stream_one = d_stream_one + grad_in
    d_gate_one = jnp.sum(d_stream_one * attn_out, axis=1)
    d_attn = (
        (d_stream_one * gate_one[:, None, :]).astype(jnp.bfloat16).reshape(images * tok_rows, D)
    )
    g_proj = matdot(merged.T, d_attn)
    d_merged = matdot(d_attn, w_proj.T).astype(jnp.bfloat16).reshape(images, tok_rows, D)
    d_heads = lax.all_to_all(d_merged, "seq", split_axis=2, concat_axis=1, tiled=True)
    d_heads = d_heads.reshape(images, full_rows, local_heads, HEAD_DIM)
    d_values = jnp.einsum(
        "bhqk,bqhd->bkhd",
        attn_probs.astype(jnp.bfloat16),
        d_heads,
        preferred_element_type=jnp.float32,
    )
    d_probs = jnp.einsum("bqhd,bkhd->bhqk", d_heads, value_rows, preferred_element_type=jnp.float32)
    d_scores = attn_probs * (d_probs - jnp.sum(attn_probs * d_probs, axis=-1, keepdims=True))
    d_scores = d_scores.astype(jnp.bfloat16)
    d_queries = jnp.einsum(
        "bhqk,bkhd->bqhd", d_scores, key_rows, preferred_element_type=jnp.float32
    ) * HEAD_DIM ** (-0.5)
    d_keys = jnp.einsum(
        "bhqk,bqhd->bkhd", d_scores, queries, preferred_element_type=jnp.float32
    ) * HEAD_DIM ** (-0.5)
    stacked = jnp.stack([d_queries, d_keys, d_values], axis=2).astype(jnp.bfloat16)
    stacked = stacked.reshape(images, full_rows, 3, 1, local_heads * HEAD_DIM)
    d_qkv = lax.all_to_all(stacked, "seq", split_axis=1, concat_axis=3, tiled=True).reshape(
        images * tok_rows, 3 * D
    )
    g_qkv = matdot(a_one.T, d_qkv)
    d_a_one = matdot(d_qkv, w_qkv.T).reshape(images, tok_rows, D)
    _, mod_back_one = jax.vjp(modulate, stream, shift_one, scale_one)
    d_stream, d_shift_one, d_scale_one = mod_back_one(d_a_one)
    d_stream = d_stream + d_stream_one
    d_modul = jnp.concatenate(
        [d_shift_one, d_scale_one, d_gate_one, d_shift_two, d_scale_two, d_gate_two], axis=1
    )
    d_bias = jnp.concatenate(
        [column_sum(d_qkv), column_sum(d_attn), column_sum(d_up), column_sum(d_down)]
    )
    return (d_stream, d_modul, (g_qkv, g_proj, g_up, g_down), d_bias)


def fetch_layer(qkv_weight, proj_weight, up_weight, down_weight, layer_at):
    return (
        lax.all_gather(qkv_weight[layer_at].astype(jnp.bfloat16), "dp", axis=0, tiled=True),
        lax.all_gather(proj_weight[layer_at].astype(jnp.bfloat16), "dp", axis=0, tiled=True),
        lax.all_gather(up_weight[layer_at].astype(jnp.bfloat16), "dp", axis=0, tiled=True),
        lax.all_gather(down_weight[layer_at].astype(jnp.bfloat16), "dp", axis=0, tiled=True),
    )


def fetch_again(qkv_weight, proj_weight, up_weight, down_weight, layer_at):
    return (
        lax.all_gather(qkv_weight[layer_at].astype(jnp.bfloat16), "dp", axis=0, tiled=True),
        lax.all_gather(proj_weight[layer_at].astype(jnp.bfloat16), "dp", axis=0, tiled=True),
        lax.all_gather(up_weight[layer_at].astype(jnp.bfloat16), "dp", axis=0, tiled=True),
        lax.all_gather(down_weight[layer_at].astype(jnp.bfloat16), "dp", axis=0, tiled=True),
    )


def adamw(weight, gradient, first, second, rate):
    first_new = BETA_ONE * first + (1.0 - BETA_ONE) * gradient
    second_new = BETA_TWO * second + (1.0 - BETA_TWO) * gradient * gradient
    first_hat = first_new / (1.0 - BETA_ONE**STEP)
    second_hat = second_new / (1.0 - BETA_TWO**STEP)
    return (
        weight - rate * (first_hat / (jnp.sqrt(second_hat) + EPSILON) + DECAY * weight),
        first_new,
        second_new,
    )


def body(
    latents,
    noise_target,
    pad_mask,
    labels,
    timesteps,
    embed_rows,
    first_embed,
    second_embed,
    class_table,
    first_table,
    second_table,
    qkv_weight,
    first_qkv,
    second_qkv,
    proj_weight,
    first_proj,
    second_proj,
    up_weight,
    first_up,
    second_up,
    down_weight,
    first_down,
    second_down,
    cond_weight,
    first_cond,
    second_cond,
    head_weight,
    first_head,
    second_head,
    all_biases,
    first_bias,
    second_bias,
):
    images, tok_rows, _ = latents.shape
    cond_cols = cond_weight.shape[1]
    embed_full, table_full, cond_full, head_full = (
        lax.all_gather(embed_rows.astype(jnp.bfloat16), "dp", axis=1, tiled=True),
        lax.all_gather(class_table.astype(jnp.bfloat16), "dp", axis=1, tiled=True),
        lax.all_gather(cond_weight.astype(jnp.bfloat16), "dp", axis=0, tiled=True),
        lax.all_gather(head_weight.astype(jnp.bfloat16), "dp", axis=0, tiled=True),
    )
    patch_part = embed_full[:PATCH_IN]
    freq_part = embed_full[PATCH_IN : PATCH_IN + FREQ]
    time_part = embed_full[PATCH_IN + FREQ :]
    seq_at = lax.axis_index("seq")
    position = position_table(seq_at * tok_rows + jnp.arange(tok_rows, dtype=jnp.int32), D, GRID)
    flat_in = latents.astype(jnp.bfloat16).reshape(images * tok_rows, PATCH_IN)
    stream = (matdot(flat_in, patch_part) + all_biases[:D]).reshape(images, tok_rows, D) + position[
        None
    ]
    features = time_features(timesteps, FREQ).astype(jnp.bfloat16)
    time_pre = matdot(features, freq_part) + all_biases[D : 2 * D]
    time_hidden = jax.nn.silu(time_pre).astype(jnp.bfloat16)
    time_embed = matdot(time_hidden, time_part) + all_biases[2 * D : 3 * D]
    onehot = (labels[:, None] == jnp.arange(NCLASS, dtype=jnp.int32)[None, :]).astype(jnp.float32)
    condition = time_embed + matdot(onehot.astype(jnp.bfloat16), table_full)
    cond_act = jax.nn.silu(condition).astype(jnp.bfloat16)
    modulation = matdot(cond_act, cond_full) + all_biases[3 * D : 3 * D + cond_cols]
    layer_bias = [
        all_biases[
            3 * D
            + cond_cols
            + layer_at * (5 * D + FF) : 3 * D
            + cond_cols
            + (layer_at + 1) * (5 * D + FF)
        ]
        for layer_at in range(LAYERS)
    ]
    inputs_kept = []
    weights_kept = []
    for layer_at in range(LAYERS):
        weight_set = fetch_layer(qkv_weight, proj_weight, up_weight, down_weight, layer_at)
        weights_kept.append(weight_set)
        inputs_kept.append(stream)
        stream, _ = layer_forward(
            stream,
            modulation[:, 6 * layer_at * D : 6 * (layer_at + 1) * D],
            weight_set,
            layer_bias[layer_at],
            pad_mask,
        )
    final_at = 6 * LAYERS * D
    _, final_back = jax.vjp(
        modulate,
        stream,
        modulation[:, final_at : final_at + D],
        modulation[:, final_at + D : final_at + 2 * D],
    )
    a_final = (
        modulate(
            stream,
            modulation[:, final_at : final_at + D],
            modulation[:, final_at + D : final_at + 2 * D],
        )
        .astype(jnp.bfloat16)
        .reshape(images * tok_rows, D)
    )
    head_out = matdot(a_final, head_full) + all_biases[NBIAS - OUT_CH :]
    split_out = head_out.reshape(images, tok_rows, 4, 2, OUT_CH // 8)
    predicted = split_out[:, :, :, 0, :].reshape(images, tok_rows, PATCH_IN)
    keep_rows = pad_mask.astype(jnp.float32)
    errors = predicted - noise_target
    loss_part = jnp.sum(keep_rows[:, :, None] * errors * errors)
    count_part = PATCH_IN * jnp.sum(keep_rows)
    d_pred = (2.0 * keep_rows[:, :, None] * errors).reshape(images, tok_rows, 4, 1, OUT_CH // 8)
    d_head = (
        jnp.concatenate([d_pred, jnp.zeros_like(d_pred)], axis=3)
        .reshape(images * tok_rows, OUT_CH)
        .astype(jnp.bfloat16)
    )
    g_head = matdot(a_final.T, d_head)
    d_a_final = matdot(d_head, head_full.T).reshape(images, tok_rows, D)
    d_stream, d_final_shift, d_final_scale = final_back(d_a_final)
    layer_sums = [None] * LAYERS
    layer_bias_grads = [None] * LAYERS
    modul_grads = [None] * LAYERS
    for layer_at in reversed(range(LAYERS)):
        weight_set = fetch_again(qkv_weight, proj_weight, up_weight, down_weight, layer_at)
        modul = modulation[:, 6 * layer_at * D : 6 * (layer_at + 1) * D]
        _, saved = layer_forward(
            inputs_kept[layer_at], modul, weight_set, layer_bias[layer_at], pad_mask
        )
        d_stream, d_modul, weight_grads, d_bias = layer_backward(
            d_stream, inputs_kept[layer_at], modul, weight_set, saved
        )
        layer_sums[layer_at] = (
            lax.psum_scatter(weight_grads[0], "dp", scatter_dimension=0, tiled=True),
            lax.psum_scatter(weight_grads[1], "dp", scatter_dimension=0, tiled=True),
            lax.psum_scatter(weight_grads[2], "dp", scatter_dimension=0, tiled=True),
            lax.psum_scatter(weight_grads[3], "dp", scatter_dimension=0, tiled=True),
        )
        layer_bias_grads[layer_at] = d_bias
        modul_grads[layer_at] = d_modul
    d_modulation = jnp.concatenate(modul_grads + [d_final_shift, d_final_scale], axis=1)
    d_modulation = lax.psum(d_modulation.astype(jnp.bfloat16), "seq")
    lead_flag = (seq_at == 0).astype(jnp.float32)
    d_cond_act = matdot(d_modulation, cond_full.T)
    _, silu_back = jax.vjp(jax.nn.silu, condition)
    d_condition = silu_back(d_cond_act)[0]
    d_time = d_condition.astype(jnp.bfloat16)
    d_time_hidden = matdot(d_time, time_part.T)
    _, time_back = jax.vjp(jax.nn.silu, time_pre)
    d_time_pre = time_back(d_time_hidden)[0].astype(jnp.bfloat16)
    d_patch = d_stream.astype(jnp.bfloat16).reshape(images * tok_rows, D)
    g_patch = matdot(flat_in.T, d_patch)
    g_cond = matdot(cond_act.T, d_modulation) * lead_flag
    g_table = jnp.dot(onehot.T, d_condition, precision=lax.Precision.HIGHEST) * lead_flag
    g_time = matdot(time_hidden.T, d_time)
    g_freq = matdot(features.T, d_time_pre)
    g_embed = jnp.concatenate([g_patch, g_freq * lead_flag, g_time * lead_flag], axis=0)
    s_embed, s_table, s_cond, s_head = (
        lax.psum_scatter(g_embed, "dp", scatter_dimension=1, tiled=True),
        lax.psum_scatter(g_table, "dp", scatter_dimension=1, tiled=True),
        lax.psum_scatter(g_cond, "dp", scatter_dimension=0, tiled=True),
        lax.psum_scatter(g_head, "dp", scatter_dimension=0, tiled=True),
    )
    s_qkv = jnp.stack([layer_sums[layer_at][0] for layer_at in range(LAYERS)])
    s_proj = jnp.stack([layer_sums[layer_at][1] for layer_at in range(LAYERS)])
    s_up = jnp.stack([layer_sums[layer_at][2] for layer_at in range(LAYERS)])
    s_down = jnp.stack([layer_sums[layer_at][3] for layer_at in range(LAYERS)])
    s_embed, s_table, s_cond, s_head, s_qkv, s_proj, s_up, s_down = (
        lax.psum(s_embed.astype(jnp.bfloat16), "seq").astype(jnp.float32),
        lax.psum(s_table.astype(jnp.bfloat16), "seq").astype(jnp.float32),
        lax.psum(s_cond.astype(jnp.bfloat16), "seq").astype(jnp.float32),
        lax.psum(s_head.astype(jnp.bfloat16), "seq").astype(jnp.float32),
        lax.psum(s_qkv.astype(jnp.bfloat16), "seq").astype(jnp.float32),
        lax.psum(s_proj.astype(jnp.bfloat16), "seq").astype(jnp.float32),
        lax.psum(s_up.astype(jnp.bfloat16), "seq").astype(jnp.float32),
        lax.psum(s_down.astype(jnp.bfloat16), "seq").astype(jnp.float32),
    )
    bias_grad = jnp.concatenate(
        [
            column_sum(d_patch),
            column_sum(d_time_pre) * lead_flag,
            column_sum(d_time) * lead_flag,
            column_sum(d_modulation) * lead_flag,
        ]
        + layer_bias_grads
        + [column_sum(d_head)]
    )
    bias_grad, loss_sum, loss_count = lax.psum((bias_grad, loss_part, count_part), ("seq", "dp"))
    new_embed, new_first_embed, new_second_embed = adamw(
        embed_rows, s_embed, first_embed, second_embed, RATE_MATRIX
    )
    new_table, new_first_table, new_second_table = adamw(
        class_table, s_table, first_table, second_table, RATE_TABLE
    )
    new_qkv, new_first_qkv, new_second_qkv = adamw(
        qkv_weight, s_qkv, first_qkv, second_qkv, RATE_MATRIX
    )
    new_proj, new_first_proj, new_second_proj = adamw(
        proj_weight, s_proj, first_proj, second_proj, RATE_MATRIX
    )
    new_up, new_first_up, new_second_up = adamw(up_weight, s_up, first_up, second_up, RATE_MATRIX)
    new_down, new_first_down, new_second_down = adamw(
        down_weight, s_down, first_down, second_down, RATE_MATRIX
    )
    new_cond, new_first_cond, new_second_cond = adamw(
        cond_weight, s_cond, first_cond, second_cond, RATE_MATRIX
    )
    new_head, new_first_head, new_second_head = adamw(
        head_weight, s_head, first_head, second_head, RATE_MATRIX
    )
    new_bias, new_first_bias, new_second_bias = adamw(
        all_biases, bias_grad, first_bias, second_bias, RATE_BIAS
    )
    return (
        loss_sum,
        loss_count,
        new_embed,
        new_first_embed,
        new_second_embed,
        new_table,
        new_first_table,
        new_second_table,
        new_qkv,
        new_first_qkv,
        new_second_qkv,
        new_proj,
        new_first_proj,
        new_second_proj,
        new_up,
        new_first_up,
        new_second_up,
        new_down,
        new_first_down,
        new_second_down,
        new_cond,
        new_first_cond,
        new_second_cond,
        new_head,
        new_first_head,
        new_second_head,
        new_bias,
        new_first_bias,
        new_second_bias,
    )


def solution(mesh):
    placed = (
        P("dp", "seq", None),
        P("dp", "seq", None),
        P("dp", "seq"),
        P("dp"),
        P("dp"),
        P(None, "dp"),
        P(None, "dp"),
        P(None, "dp"),
        P(None, "dp"),
        P(None, "dp"),
        P(None, "dp"),
        P(None, "dp", None),
        P(None, "dp", None),
        P(None, "dp", None),
        P(None, "dp", None),
        P(None, "dp", None),
        P(None, "dp", None),
        P(None, "dp", None),
        P(None, "dp", None),
        P(None, "dp", None),
        P(None, "dp", None),
        P(None, "dp", None),
        P(None, "dp", None),
        P("dp", None),
        P("dp", None),
        P("dp", None),
        P("dp", None),
        P("dp", None),
        P("dp", None),
        P(),
        P(),
        P(),
    )
    return jax.shard_map(
        body,
        mesh=mesh,
        in_specs=placed,
        out_specs=(
            P(),
            P(),
            P(None, "dp"),
            P(None, "dp"),
            P(None, "dp"),
            P(None, "dp"),
            P(None, "dp"),
            P(None, "dp"),
            P(None, "dp", None),
            P(None, "dp", None),
            P(None, "dp", None),
            P(None, "dp", None),
            P(None, "dp", None),
            P(None, "dp", None),
            P(None, "dp", None),
            P(None, "dp", None),
            P(None, "dp", None),
            P(None, "dp", None),
            P(None, "dp", None),
            P(None, "dp", None),
            P("dp", None),
            P("dp", None),
            P("dp", None),
            P("dp", None),
            P("dp", None),
            P("dp", None),
            P(),
            P(),
            P(),
        ),
        check_vma=False,
    )
```

profile of v0, /device:TPU:0, one launch (start us, length us, event | category | flops | bytes accessed | tf_op | source)
XLA Modules:
  0.0 3335.6 jit_solution(9779134227991097797)
XLA Ops:
  29.8 25.1 all-gather.23.cloned.1.call-done
  57.1 43.8 %all-gather.21.cloned.1.call-done = bf16[1296,1024]{0,1:T(8,128)(2,1)} async-done(((bf16[1296,64]{0,1:T(8,128)(2,1)}), bf16[1296,1024]{0,1:T(8,128)(2,1)}) %all-gather.21.cloned.1.call-update) | async-done | bytes 2654224 | tf_op jit(solution)/shard_map/all_gather | solution.py:277
  105.1 144.7 %all-gather.25.cloned.1.call-done = bf16[1024,14336]{1,0:T(8,128)(2,1)} async-done(((bf16[64,14336]{1,0:T(8,128)(2,1)}), bf16[1024,14336]{1,0:T(8,128)(2,1)}) %all-gather.25.cloned.1.call-update) | async-done | bytes 29360144 | tf_op jit(solution)/shard_map/all_gather | solution.py:279
  262.8 51.6 %all-gather.27.cloned.1.call-done = bf16[1,1024,3072]{2,1,0:T(8,128)(2,1)} async-done(((bf16[1,64,3072]{2,1,0:T(8,128)(2,1)}), bf16[1,1024,3072]{2,1,0:T(8,128)(2,1)}) %all-gather.27.cloned.1.call-update) | async-done | bytes 6291472 | tf_op jit(solution)/shard_map/all_gather | solution.py:212
  340.7 36.8 %all-to-all-done = bf16[4,128,3,2,512]{4,1,2,0,3:T(8,128)(2,1)} async-done(((bf16[4,128,3,2,512]{4,1,2,0,3:T(8,128)(2,1)}), bf16[4,128,3,2,512]{4,1,2,0,3:T(8,128)(2,1)}, u32[]{:S(2)}, u32[]{:S(2)}) %all-to-all-start) | async-done | bytes 3145760 | tf_op jit(solution)/shard_map/all_to_all | solution.py:87
  446.1 63.2 %all-gather.33.cloned.1.call-done = bf16[1,4096,1024]{2,1,0:T(8,128)(2,1)} async-done(((bf16[1,256,1024]{2,1,0:T(8,128)(2,1)}), bf16[1,4096,1024]{2,1,0:T(8,128)(2,1)}) %all-gather.33.cloned.1.call-update) | async-done | bytes 8388624 | tf_op jit(solution)/shard_map/all_gather | solution.py:215
  525.3 46.9 %all-gather.35.cloned.1.call-done = bf16[1,1024,3072]{2,1,0:T(8,128)(2,1)} async-done(((bf16[1,64,3072]{2,1,0:T(8,128)(2,1)}), bf16[1,1024,3072]{2,1,0:T(8,128)(2,1)}) %all-gather.35.cloned.1.call-update) | async-done | bytes 6291472 | tf_op jit(solution)/shard_map/all_gather | solution.py:212
  591.3 40.4 %all_to_all.164 = bf16[4,128,3,2,512]{4,1,2,0,3:T(8,128)(2,1)} all-to-all(bf16[4,128,3,2,512]{4,1,2,0,3:T(8,128)(2,1)S(1)} %copy.274), channel_id=1, replica_groups=mesh['seq'=2,'dp'=16] {'seq'}, dimensions={3} | all-to-all | bytes 6291456 | tf_op jit(solution)/shard_map/all_to_all | solution.py:87
  707.8 60.5 %all-gather.41.cloned.1.call-done = bf16[1,4096,1024]{2,1,0:T(8,128)(2,1)} async-done(((bf16[1,256,1024]{2,1,0:T(8,128)(2,1)}), bf16[1,4096,1024]{2,1,0:T(8,128)(2,1)}) %all-gather.41.cloned.1.call-update) | async-done | bytes 8388624 | tf_op jit(solution)/shard_map/all_gather | solution.py:215
  876.5 38.8 %all_to_all.166 = bf16[4,256,3,1,512]{4,0,3,2,1:T(4,128)(2,1)S(1)} all-to-all(bf16[4,256,3,1,512]{4,0,3,2,1:T(4,128)(2,1)S(1)} %pad_maximum_fusion.1), channel_id=1, replica_groups=mesh['seq'=2,'dp'=16] {'seq'}, dimensions={1} | all-to-all | bytes 6291456 | tf_op jit(solution)/shard_map/all_to_all | solution.py:193
  1029.7 34.1 %all-to-all-done.8 = bf16[4,256,3,1,512]{4,0,3,2,1:T(4,128)(2,1)} async-done(((bf16[4,256,3,1,512]{4,0,3,2,1:T(4,128)(2,1)}), bf16[4,256,3,1,512]{4,0,3,2,1:T(4,128)(2,1)}, u32[]{:S(2)}, u32[]{:S(2)}) %all-to-all-start.8) | async-done | bytes 3145760 | tf_op jit(solution)/shard_map/all_to_all | solution.py:193
  1238.0 23.0 broadcast_multiply_fusion
  1276.5 66.0 %reduce-scatter.17.cloned.1.call-done = f32[1001,64]{0,1:T(8,128)} async-done(((f32[1001,1024]{0,1:T(8,128)}), f32[1001,64]{0,1:T(8,128)}) %reduce-scatter.17.cloned.1.call-update) | async-done | bytes 256272 | tf_op jit(solution)/shard_map/reduce_scatter | solution.py:393
  1344.1 83.4 %reduce-scatter.37.cloned.1.call-done = f32[64,1296]{1,0:T(8,128)} async-done(((f32[1024,1296]{1,0:T(8,128)}), f32[64,1296]{1,0:T(8,128)}) %reduce-scatter.37.cloned.1.call-update) | async-done | bytes 331792
  1429.2 136.7 %reduce-scatter.21.cloned.1.call-done = f32[64,3072]{1,0:T(8,128)} async-done(((f32[1024,3072]{1,0:T(8,128)}), f32[64,3072]{1,0:T(8,128)}) %reduce-scatter.21.cloned.1.call-update) | async-done | bytes 786448 | tf_op jit(solution)/shard_map/reduce_scatter | solution.py:367
  1567.0 137.1 %reduce-scatter.19.cloned.1.call-done = f32[64,3072]{1,0:T(8,128)} async-done(((f32[1024,3072]{1,0:T(8,128)}), f32[64,3072]{1,0:T(8,128)}) %reduce-scatter.19.cloned.1.call-update) | async-done | bytes 786448 | tf_op jit(solution)/shard_map/reduce_scatter | solution.py:367
  1706.2 180.2 %reduce-scatter.33.cloned.1.call-done = f32[256,1024]{1,0:T(8,128)} async-done(((f32[4096,1024]{1,0:T(8,128)}), f32[256,1024]{1,0:T(8,128)}) %reduce-scatter.33.cloned.1.call-update) | async-done | bytes 1048592 | tf_op jit(solution)/shard_map/reduce_scatter | solution.py:370
  1887.8 180.8 %reduce-scatter.29.cloned.1.call-done = f32[64,4096]{1,0:T(8,128)} async-done(((f32[1024,4096]{1,0:T(8,128)}), f32[64,4096]{1,0:T(8,128)}) %reduce-scatter.29.cloned.1.call-update) | async-done | bytes 1048592 | tf_op jit(solution)/shard_map/reduce_scatter | solution.py:369
  2069.8 181.0 %reduce-scatter.27.cloned.1.call-done = f32[64,4096]{1,0:T(8,128)} async-done(((f32[1024,4096]{1,0:T(8,128)}), f32[64,4096]{1,0:T(8,128)}) %reduce-scatter.27.cloned.1.call-update) | async-done | bytes 1048592 | tf_op jit(solution)/shard_map/reduce_scatter | solution.py:369
  2253.1 179.9 %reduce-scatter.31.cloned.1.call-done = f32[256,1024]{1,0:T(8,128)} async-done(((f32[4096,1024]{1,0:T(8,128)}), f32[256,1024]{1,0:T(8,128)}) %reduce-scatter.31.cloned.1.call-update) | async-done | bytes 1048592 | tf_op jit(solution)/shard_map/reduce_scatter | solution.py:370
  2435.4 539.0 %reduce-scatter.35.cloned.1.call-done = f32[64,14336]{1,0:T(8,128)} async-done(((f32[1024,14336]{1,0:T(8,128)}), f32[64,14336]{1,0:T(8,128)}) %reduce-scatter.35.cloned.1.call-update) | async-done | bytes 3670032 | tf_op jit(solution)/shard_map/reduce_scatter | solution.py:394
  2979.9 39.7 %all-reduce.1 = (f32[]{:T(128)}, f32[]{:T(128)}) all-reduce(f32[]{:T(128)} %fusion.154, f32[]{:T(128)S(6)} %mul_shard_map.3), channel_id=1, replica_groups=mesh['seq'=2,'dp'=16] {'seq','dp'}, use_global_device_ids=true, to_apply=%region_15.16 | all-reduce | flops 2 | bytes 16 | tf_op jit(solution)/shard_map/psum | solution.py:421
  3040.4 119.3 %all-reduce.9.cloned.1.call-done = f32[35872]{0:T(1024)} async-done(((f32[35872]{0:T(1024)}), f32[35872]{0:T(1024)}) %all-reduce.9.cloned.1.call-update) | async-done | bytes 143504 | tf_op jit(solution)/shard_map/psum | solution.py:421
  3161.4 138.6 %all-reduce.11.cloned.1.call-done = (bf16[1296,64]{0,1:T(8,128)(2,1)}, bf16[1001,64]{0,1:T(8,128)(2,1)}, bf16[2,64,3072]{2,1,0:T(8,128)(2,1)}, bf16[2,64,1024]{2...) async-done(((bf16[1296,64]{0,1:T(8,128)(2,1)}, bf16[1001,64]{0,1:T(8,128)(2,1)}, ...) | async-done | bytes 5274768 | tf_op jit(solution)/shard_map/psum | solution.py:402
  (589 shorter events, 728.3 us)
Async XLA Ops:
  10.6 239.2 %all-gather.25.cloned.1.call-start = ((), (), s32[]{:S(2)}) async-start(), calls=%async_computation.23 | async-start | bytes 31195136 | tf_op jit(solution)/shard_map/all_gather | solution.py:279
  14.2 300.2 %all-gather.27.cloned.1.call-start = ((), (), s32[]{:S(2)}) async-start(), calls=%async_computation.36 | async-start | bytes 6684672 | tf_op jit(solution)/shard_map/all_gather | solution.py:212
  16.6 410.3 %all-gather.29.cloned.1.call-start = ((), (), s32[]{:S(2)}) async-start(), calls=%async_computation.37 | async-start | bytes 2228224 | tf_op jit(solution)/shard_map/all_gather | solution.py:213
  17.5 417.0 %all-gather.31.cloned.1.call-start = ((), (), s32[]{:S(2)}) async-start(), calls=%async_computation.38 | async-start | bytes 8912896 | tf_op jit(solution)/shard_map/all_gather | solution.py:214
  18.7 490.5 %all-gather.33.cloned.1.call-start = ((), (), s32[]{:S(2)}) async-start(), calls=%async_computation.39 | async-start | bytes 8912896 | tf_op jit(solution)/shard_map/all_gather | solution.py:215
  20.9 551.3 %all-gather.35.cloned.1.call-start = ((), (), s32[]{:S(2)}) async-start(), calls=%async_computation.40 | async-start | bytes 6684672 | tf_op jit(solution)/shard_map/all_gather | solution.py:212
  21.6 666.5 %all-gather.37.cloned.1.call-start = ((), (), s32[]{:S(2)}) async-start(), calls=%async_computation.41 | async-start | bytes 2228224 | tf_op jit(solution)/shard_map/all_gather | solution.py:213
  22.4 673.8 %all-gather.39.cloned.1.call-start = ((), (), s32[]{:S(2)}) async-start(), calls=%async_computation.42 | async-start | bytes 8912896 | tf_op jit(solution)/shard_map/all_gather | solution.py:214
  23.6 311.6 %all-to-all-start.1 = ((s32[4,128,1,2,1]{1,0,4,2,3:T(4,128)}), s32[4,128,1,2,1]{1,0,4,2,3:T(4,128)S(1)}, u32[]{:S(2)}, u32[]{:S(2)}) async-start(s32[4,128,1,2,1]{1,0,4,2,3:T(4,128)} %broadcast_in_dim.50), calls=%async_computation.1 | async-start | bytes 8192 | tf_op jit(solution)/shard_map/all_to_all | solution.py:88
  27.8 740.5 %all-gather.41.cloned.1.call-start = ((), (), s32[]{:S(2)}) async-start(), calls=%async_computation.43 | async-start | bytes 8912896 | tf_op jit(solution)/shard_map/all_gather | solution.py:215
  1096.4 177.4 %reduce-scatter.25.cloned.1.call-start = ((), (), s32[]{:S(2)}) async-start(), calls=%async_computation.29 | async-start | bytes 4456448 | tf_op jit(solution)/shard_map/reduce_scatter | solution.py:368
  1101.4 173.4 %reduce-scatter.23.cloned.1.call-start = ((), (), s32[]{:S(2)}) async-start(), calls=%async_computation.28 | async-start | bytes 4456448 | tf_op jit(solution)/shard_map/reduce_scatter | solution.py:368
  1106.2 236.3 %reduce-scatter.17.cloned.1.call-start = ((), (), s32[]{:S(2)}) async-start(), calls=%async_computation.25 | async-start | bytes 4456448 | tf_op jit(solution)/shard_map/reduce_scatter | solution.py:393
  1132.9 294.6 %reduce-scatter.37.cloned.1.call-start = ((), (), s32[]{:S(2)}) async-start(), calls=%async_computation.44 | async-start | bytes 6127616
  1147.1 418.7 %reduce-scatter.21.cloned.1.call-start = ((), (), s32[]{:S(2)}) async-start(), calls=%async_computation.27 | async-start | bytes 13369344 | tf_op jit(solution)/shard_map/reduce_scatter | solution.py:367
  1163.2 540.9 %reduce-scatter.19.cloned.1.call-start = ((), (), s32[]{:S(2)}) async-start(), calls=%async_computation.26 | async-start | bytes 13369344 | tf_op jit(solution)/shard_map/reduce_scatter | solution.py:367
  1179.1 707.4 %reduce-scatter.33.cloned.1.call-start = ((), (), s32[]{:S(2)}) async-start(), calls=%async_computation.33 | async-start | bytes 17825792 | tf_op jit(solution)/shard_map/reduce_scatter | solution.py:370
  1195.9 872.7 %reduce-scatter.29.cloned.1.call-start = ((), (), s32[]{:S(2)}) async-start(), calls=%async_computation.31 | async-start | bytes 17825792 | tf_op jit(solution)/shard_map/reduce_scatter | solution.py:369
  1207.9 1042.9 %reduce-scatter.27.cloned.1.call-start = ((), (), s32[]{:S(2)}) async-start(), calls=%async_computation.30 | async-start | bytes 17825792 | tf_op jit(solution)/shard_map/reduce_scatter | solution.py:369
  1220.0 1213.0 %reduce-scatter.31.cloned.1.call-start = ((), (), s32[]{:S(2)}) async-start(), calls=%async_computation.32 | async-start | bytes 17825792 | tf_op jit(solution)/shard_map/reduce_scatter | solution.py:370
  1237.1 1737.3 %reduce-scatter.35.cloned.1.call-start = ((), (), s32[]{:S(2)}) async-start(), calls=%async_computation.34 | async-start | bytes 62390272 | tf_op jit(solution)/shard_map/reduce_scatter | solution.py:394
  1261.0 1772.7 %reduce-scatter.39.cloned.1.call-start = ((), (), s32[]{:S(2)}) async-start(), calls=%async_computation.45 | async-start | bytes 557056
  1264.6 1895.1 %all-reduce.9.cloned.1.call-start = ((), (), s32[]{:S(2)}) async-start(), calls=%async_computation.35 | async-start | bytes 294912 | tf_op jit(solution)/shard_map/psum | solution.py:421
  1273.7 2026.3 %all-reduce.11.cloned.1.call-start = ((), (), s32[]{:S(2)}) async-start(), calls=%async_computation.46 | async-start | bytes 10584064 | tf_op jit(solution)/shard_map/psum | solution.py:402
  (147 other events, 5843.3 us)
Sparse Core Ops, SparseCore 0:
  10.8 44.0 all-gather.22
  57.8 43.1 all-gather.20
  103.1 146.6 all-gather.24
  252.5 61.8 all-gather.26
  317.0 39.9 all-gather.28
  359.6 73.6 all-gather.30
  436.0 73.1 all-gather.32
  512.1 60.0 all-gather.34
  617.5 74.8 all-gather.38
  695.2 73.0 all-gather.40
  1118.9 72.4 reduce-scatter.24
  1195.7 71.3 reduce-scatter.22
  1270.7 71.7 reduce-scatter.16
  1346.8 80.6 reduce-scatter.36
  1431.9 133.8 reduce-scatter.20
  1570.3 133.7 reduce-scatter.18
  1708.8 177.6 reduce-scatter.32
  1891.0 177.5 reduce-scatter.28
  2073.2 177.5 reduce-scatter.26
  2255.5 177.5 reduce-scatter.30
  2437.9 536.5 reduce-scatter.34
  2978.8 54.8 reduce-scatter.38
  3039.9 119.7 all-reduce.8
  3164.3 135.6 all-reduce.10
  (2 shorter events, 58.4 us)
where the time goes:
time: 3350 us; the launch traced here: 3340 us
  waiting for transfers between devices  2490 us (74%)
  matrix products  334 us (10%)
  blocking collectives  179 us (5%)
  local copies, waits for them, and re-layouts  176 us (5%)
  other arithmetic  117 us (3%)
    reduce_scatter x1, waiting for transfers between devices, body(): lax.psum_scatter(g_cond, 'dp', scatter_dimension=0, tiled=True)  539 us
    reduce_scatter x2, waiting for transfers between devices, body(): lax.psum_scatter(weight_grads[2], 'dp', scatter_dimension=0, tiled=True)  362 us
    reduce_scatter x2, waiting for transfers between devices, body(): lax.psum_scatter(weight_grads[3], 'dp', scatter_dimension=0, tiled=True)  360 us
    dot_general x37, matrix products, matdot(): return jnp.dot(left, right, preferred_element_type=jnp.float32)  284 us
    reduce_scatter x2, waiting for transfers between devices, body(): lax.psum_scatter(weight_grads[0], 'dp', scatter_dimension=0, tiled=True)  274 us
    all_gather x1, waiting for transfers between devices, body(): lax.all_gather(cond_weight.astype(jnp.bfloat16), 'dp', axis=0, tiled=True)  145 us
    psum x1, waiting for transfers between devices, body(): lax.psum(s_embed.astype(jnp.bfloat16), 'seq').astype(jnp.float32)  139 us
    all_gather x2, waiting for transfers between devices, fetch_layer(): lax.all_gather(down_weight[layer_at].astype(jnp.bfloat16), 'dp', axis=0,...  124 us
  transfers between devices with their start and end apart: 31, of which 23 were waited for; matrix products, arithmetic and copies ran while one was open for 11% of the time, Pallas kernels for 0%

commit v1 on v0

v1 whole, which is shorter than its diff:
```python
import math

import jax
import jax.numpy as jnp
from jax import lax
from jax.sharding import PartitionSpec as P

D = 1024
HEADS = 16
HEAD_DIM = 64
FF = 4096
NCLASS = 1001
FREQ = 256
OUT_CH = 32
PATCH_IN = 16
GRID = 16
LAYERS = 2
STEP = 10
NBIAS = 35872


BETA_ONE = 0.9
BETA_TWO = 0.999
EPSILON = 1e-08
DECAY = 0.01
RATE_MATRIX = 0.06
RATE_TABLE = 0.4
RATE_BIAS = 0.2


def matdot(left, right):
    return jnp.dot(left, right, preferred_element_type=jnp.float32)


def layer_norm(stream):
    row_mean = jnp.mean(stream, axis=-1, keepdims=True)
    centered = stream - row_mean
    variance = jnp.mean(centered * centered, axis=-1, keepdims=True)
    return centered * lax.rsqrt(variance + 1e-06)


def modulate(stream, shift_by, scale_by):
    return layer_norm(stream) * (1.0 + scale_by[:, None, :]) + shift_by[:, None, :]


def position_table(position_ids, feature_width, grid_side):
    quarter_width = feature_width // 4
    omegas = 1.0 / 10000.0 ** (jnp.arange(quarter_width, dtype=jnp.float32) / quarter_width)
    col_angle = (position_ids % grid_side).astype(jnp.float32)[:, None] * omegas[None, :]
    row_angle = (position_ids // grid_side).astype(jnp.float32)[:, None] * omegas[None, :]
    return jnp.concatenate(
        [jnp.sin(col_angle), jnp.cos(col_angle), jnp.sin(row_angle), jnp.cos(row_angle)], axis=1
    )


def time_features(timesteps, feature_width):
    half_width = feature_width // 2
    frequencies = jnp.exp(
        -math.log(10000.0) * jnp.arange(half_width, dtype=jnp.float32) / half_width
    )
    angles = timesteps.astype(jnp.float32)[:, None] * frequencies[None, :]
    return jnp.concatenate([jnp.cos(angles), jnp.sin(angles)], axis=1)


def column_sum(grad_bf):
    return jnp.sum(grad_bf.astype(jnp.float32), axis=0)


def split_six(modul):
    return [modul[:, piece * D : (piece + 1) * D] for piece in range(6)]


def layer_forward(stream, modul, weight_set, bias_part, pad_mask):
    w_qkv, w_proj, w_up, w_down = weight_set
    images, tok_rows, _ = stream.shape
    shift_one, scale_one, gate_one, shift_two, scale_two, gate_two = split_six(modul)
    a_one = (
        modulate(stream, shift_one, scale_one).astype(jnp.bfloat16).reshape(images * tok_rows, D)
    )
    qkv_all = (matdot(a_one, w_qkv) + bias_part[: 3 * D]).astype(jnp.bfloat16)
    heads_in = qkv_all.reshape(images, tok_rows, 3, HEADS, HEAD_DIM)
    queries, key_rows, value_rows = (heads_in[:, :, 0], heads_in[:, :, 1], heads_in[:, :, 2])
    scores = jnp.einsum(
        "bqhd,bkhd->bhqk", queries, key_rows, preferred_element_type=jnp.float32
    ) * HEAD_DIM ** (-0.5)
    attn_probs = jax.nn.softmax(
        jnp.where(pad_mask[:, None, None, :] > 0, scores, -1000000000.0), axis=-1
    )
    heads_out = jnp.einsum(
        "bhqk,bkhd->bqhd",
        attn_probs.astype(jnp.bfloat16),
        value_rows,
        preferred_element_type=jnp.float32,
    )
    merged = heads_out.astype(jnp.bfloat16).reshape(images * tok_rows, D)
    attn_out = (matdot(merged, w_proj) + bias_part[3 * D : 4 * D]).reshape(images, tok_rows, D)
    stream_one = stream + gate_one[:, None, :] * attn_out
    a_two = (
        modulate(stream_one, shift_two, scale_two)
        .astype(jnp.bfloat16)
        .reshape(images * tok_rows, D)
    )
    up_pre = matdot(a_two, w_up) + bias_part[4 * D : 4 * D + FF]
    activated = jax.nn.gelu(up_pre, approximate=True).astype(jnp.bfloat16)
    down_out = (matdot(activated, w_down) + bias_part[4 * D + FF :]).reshape(images, tok_rows, D)
    stream_two = stream_one + gate_two[:, None, :] * down_out
    saved = (
        a_one,
        queries,
        key_rows,
        value_rows,
        attn_probs,
        merged,
        attn_out,
        stream_one,
        a_two,
        up_pre,
        activated,
        down_out,
    )
    return (stream_two, saved)


def layer_backward(grad_in, stream, modul, weight_set, saved):
    w_qkv, w_proj, w_up, w_down = weight_set
    (
        a_one,
        queries,
        key_rows,
        value_rows,
        attn_probs,
        merged,
        attn_out,
        stream_one,
        a_two,
        up_pre,
        activated,
        down_out,
    ) = saved
    images, tok_rows, _ = stream.shape
    shift_one, scale_one, gate_one, shift_two, scale_two, gate_two = split_six(modul)
    d_gate_two = jnp.sum(grad_in * down_out, axis=1)
    d_down = (grad_in * gate_two[:, None, :]).astype(jnp.bfloat16).reshape(images * tok_rows, D)
    s_down = reduce_rows(matdot(activated.T, d_down))
    d_activated = matdot(d_down, w_down.T)
    _, gelu_back = jax.vjp(lambda inner: jax.nn.gelu(inner, approximate=True), up_pre)
    d_up = gelu_back(d_activated)[0].astype(jnp.bfloat16)
    s_up = reduce_rows(matdot(a_two.T, d_up))
    d_a_two = matdot(d_up, w_up.T).reshape(images, tok_rows, D)
    _, mod_back_two = jax.vjp(modulate, stream_one, shift_two, scale_two)
    d_stream_one, d_shift_two, d_scale_two = mod_back_two(d_a_two)
    d_stream_one = d_stream_one + grad_in
    d_gate_one = jnp.sum(d_stream_one * attn_out, axis=1)
    d_attn = (
        (d_stream_one * gate_one[:, None, :]).astype(jnp.bfloat16).reshape(images * tok_rows, D)
    )
    s_proj = reduce_rows(matdot(merged.T, d_attn))
    d_heads = matdot(d_attn, w_proj.T).astype(jnp.bfloat16)
    d_heads = d_heads.reshape(images, tok_rows, HEADS, HEAD_DIM)
    d_values = jnp.einsum(
        "bhqk,bqhd->bkhd",
        attn_probs.astype(jnp.bfloat16),
        d_heads,
        preferred_element_type=jnp.float32,
    )
    d_probs = jnp.einsum("bqhd,bkhd->bhqk", d_heads, value_rows, preferred_element_type=jnp.float32)
    d_scores = attn_probs * (d_probs - jnp.sum(attn_probs * d_probs, axis=-1, keepdims=True))
    d_scores = d_scores.astype(jnp.bfloat16)
    d_queries = jnp.einsum(
        "bhqk,bkhd->bqhd", d_scores, key_rows, preferred_element_type=jnp.float32
    ) * HEAD_DIM ** (-0.5)
    d_keys = jnp.einsum(
        "bhqk,bqhd->bkhd", d_scores, queries, preferred_element_type=jnp.float32
    ) * HEAD_DIM ** (-0.5)
    d_qkv = jnp.stack([d_queries, d_keys, d_values], axis=2).astype(jnp.bfloat16)
    d_qkv = d_qkv.reshape(images * tok_rows, 3 * D)
    s_qkv = reduce_rows(matdot(a_one.T, d_qkv))
    d_a_one = matdot(d_qkv, w_qkv.T).reshape(images, tok_rows, D)
    _, mod_back_one = jax.vjp(modulate, stream, shift_one, scale_one)
    d_stream, d_shift_one, d_scale_one = mod_back_one(d_a_one)
    d_stream = d_stream + d_stream_one
    d_modul = jnp.concatenate(
        [d_shift_one, d_scale_one, d_gate_one, d_shift_two, d_scale_two, d_gate_two], axis=1
    )
    d_bias = jnp.concatenate(
        [column_sum(d_qkv), column_sum(d_attn), column_sum(d_up), column_sum(d_down)]
    )
    return (d_stream, d_modul, (s_qkv, s_proj, s_up, s_down), d_bias)


def gather_rows(shard):
    return lax.all_gather(shard.astype(jnp.bfloat16), "dp", axis=0, tiled=True)


def reduce_rows(partial):
    owned = lax.psum_scatter(
        partial.astype(jnp.bfloat16), "dp", scatter_dimension=0, tiled=True
    )
    return lax.psum(owned, "seq").astype(jnp.float32)


def adamw(weight, gradient, first, second, rate):
    first_new = BETA_ONE * first + (1.0 - BETA_ONE) * gradient
    second_new = BETA_TWO * second + (1.0 - BETA_TWO) * gradient * gradient
    first_hat = first_new / (1.0 - BETA_ONE**STEP)
    second_hat = second_new / (1.0 - BETA_TWO**STEP)
    return (
        weight - rate * (first_hat / (jnp.sqrt(second_hat) + EPSILON) + DECAY * weight),
        first_new,
        second_new,
    )


def body(
    latents,
    noise_target,
    pad_mask,
    labels,
    timesteps,
    embed_rows,
    first_embed,
    second_embed,
    class_table,
    first_table,
    second_table,
    qkv_weight,
    first_qkv,
    second_qkv,
    proj_weight,
    first_proj,
    second_proj,
    up_weight,
    first_up,
    second_up,
    down_weight,
    first_down,
    second_down,
    cond_weight,
    first_cond,
    second_cond,
    head_weight,
    first_head,
    second_head,
    all_biases,
    first_bias,
    second_bias,
):
    seq_parts = lax.axis_size("seq")
    dp_parts = lax.axis_size("dp")
    seq_at = lax.axis_index("seq")
    dp_at = lax.axis_index("dp")
    group, _, _ = latents.shape
    images = group // seq_parts
    everyone = group * dp_parts
    own_cols = embed_rows.shape[1]
    cond_cols = cond_weight.shape[1]
    bias_base = 3 * D + cond_cols
    packed = jnp.concatenate(
        [latents, noise_target, pad_mask.astype(jnp.float32)[:, :, None]], axis=2
    )
    packed = lax.all_to_all(packed, "seq", split_axis=0, concat_axis=1, tiled=True)
    tok_rows = packed.shape[1]
    latents, noise_target, keep_rows = (
        packed[:, :, :PATCH_IN],
        packed[:, :, PATCH_IN : 2 * PATCH_IN],
        packed[:, :, 2 * PATCH_IN],
    )
    ids = lax.all_gather(jnp.stack([labels, timesteps]), "dp", axis=1, tiled=True)
    small = jnp.concatenate(
        [embed_rows[: PATCH_IN + FREQ], head_weight.T], axis=0
    ).astype(jnp.bfloat16)
    small = lax.all_gather(small, "dp", axis=1, tiled=True)
    patch_part = small[:PATCH_IN]
    freq_part = small[PATCH_IN : PATCH_IN + FREQ]
    head_rows = small[PATCH_IN + FREQ :]
    time_own = embed_rows[PATCH_IN + FREQ :].astype(jnp.bfloat16)
    cond_own = cond_weight.astype(jnp.bfloat16)

    features = time_features(ids[1], FREQ).astype(jnp.bfloat16)
    time_pre = matdot(features, freq_part) + all_biases[D : 2 * D]
    time_hidden = jax.nn.silu(time_pre).astype(jnp.bfloat16)
    second_bias_own = lax.dynamic_slice(all_biases, (2 * D + dp_at * own_cols,), (own_cols,))
    onehot = (ids[0][:, None] == jnp.arange(NCLASS, dtype=jnp.int32)[None, :]).astype(jnp.float32)
    condition = (
        matdot(time_hidden, time_own)
        + second_bias_own
        + matdot(onehot.astype(jnp.bfloat16), class_table.astype(jnp.bfloat16))
    )
    cond_act = jax.nn.silu(condition).astype(jnp.bfloat16)
    plane_act = lax.dynamic_index_in_dim(
        cond_act.reshape(dp_parts, seq_parts, images, own_cols), seq_at, 1, keepdims=False
    ).reshape(dp_parts * images, own_cols)
    modulation = lax.psum_scatter(
        matdot(plane_act, cond_own), "dp", scatter_dimension=0, tiled=True
    )
    modulation = modulation + all_biases[3 * D : bias_base]

    position = position_table(jnp.arange(tok_rows, dtype=jnp.int32), D, GRID)
    flat_in = latents.astype(jnp.bfloat16).reshape(images * tok_rows, PATCH_IN)
    stream = (matdot(flat_in, patch_part) + all_biases[:D]).reshape(images, tok_rows, D) + position[
        None
    ]
    layer_bias = [
        all_biases[bias_base + at * (5 * D + FF) : bias_base + (at + 1) * (5 * D + FF)]
        for at in range(LAYERS)
    ]
    inputs_kept = []
    weights_kept = []
    saved_kept = []
    for at in range(LAYERS):
        weight_set = (
            gather_rows(qkv_weight[at]),
            gather_rows(proj_weight[at]),
            gather_rows(up_weight[at]),
            gather_rows(down_weight[at]),
        )
        weights_kept.append(weight_set)
        inputs_kept.append(stream)
        stream, saved = layer_forward(
            stream,
            modulation[:, 6 * at * D : 6 * (at + 1) * D],
            weight_set,
            layer_bias[at],
            keep_rows,
        )
        saved_kept.append(saved)
    final_at = 6 * LAYERS * D
    final_shift = modulation[:, final_at : final_at + D]
    final_scale = modulation[:, final_at + D : final_at + 2 * D]
    moved, final_back = jax.vjp(modulate, stream, final_shift, final_scale)
    a_final = moved.astype(jnp.bfloat16).reshape(images * tok_rows, D)
    head_out = lax.dot_general(
        a_final, head_rows, (((1,), (1,)), ((), ())), preferred_element_type=jnp.float32
    ) + all_biases[NBIAS - OUT_CH :]
    split_out = head_out.reshape(images, tok_rows, 4, 2, OUT_CH // 8)
    predicted = split_out[:, :, :, 0, :].reshape(images, tok_rows, PATCH_IN)
    errors = predicted - noise_target
    loss_part = jnp.sum(keep_rows[:, :, None] * errors * errors)
    count_part = PATCH_IN * jnp.sum(keep_rows)
    d_pred = (2.0 * keep_rows[:, :, None] * errors).reshape(images, tok_rows, 4, 1, OUT_CH // 8)
    d_head = (
        jnp.concatenate([d_pred, jnp.zeros_like(d_pred)], axis=3)
        .reshape(images * tok_rows, OUT_CH)
        .astype(jnp.bfloat16)
    )
    g_head = matdot(a_final.T, d_head)
    d_a_final = matdot(d_head, head_rows).reshape(images, tok_rows, D)
    d_stream, d_final_shift, d_final_scale = final_back(d_a_final)
    layer_sums = [None] * LAYERS
    layer_bias_grads = [None] * LAYERS
    modul_grads = [None] * LAYERS
    for at in reversed(range(LAYERS)):
        d_stream, modul_grads[at], layer_sums[at], layer_bias_grads[at] = layer_backward(
            d_stream,
            inputs_kept[at],
            modulation[:, 6 * at * D : 6 * (at + 1) * D],
            weights_kept[at],
            saved_kept[at],
        )
    d_mod_own = jnp.concatenate(modul_grads + [d_final_shift, d_final_scale], axis=1).astype(
        jnp.bfloat16
    )
    d_modulation = lax.all_gather(d_mod_own, ("dp", "seq"), axis=0, tiled=True)
    d_cond_act = lax.dot_general(
        d_modulation, cond_own, (((1,), (1,)), ((), ())), preferred_element_type=jnp.float32
    )
    _, silu_back = jax.vjp(jax.nn.silu, condition)
    d_condition = silu_back(d_cond_act)[0]
    d_time = d_condition.astype(jnp.bfloat16)
    d_time_hidden = lax.psum_scatter(
        lax.dot_general(
            d_time, time_own, (((1,), (1,)), ((), ())), preferred_element_type=jnp.float32
        ),
        "dp",
        scatter_dimension=1,
        tiled=True,
    )
    time_pre_own = lax.dynamic_slice(time_pre, (0, dp_at * own_cols), (everyone, own_cols))
    _, time_back = jax.vjp(jax.nn.silu, time_pre_own)
    d_time_pre = time_back(d_time_hidden)[0].astype(jnp.bfloat16)
    d_patch = d_stream.astype(jnp.bfloat16).reshape(images * tok_rows, D)
    g_patch = matdot(flat_in.T, d_patch)
    s_cond = matdot(cond_act.T, d_modulation)
    s_table = jnp.dot(onehot.T, d_condition, precision=lax.Precision.HIGHEST)
    g_time = matdot(time_hidden.T, d_time)
    g_freq = matdot(features.T, d_time_pre)

    lead_flag = (seq_at == 0).astype(jnp.float32)
    own_place = dp_at * own_cols
    first_time_bias = lax.dynamic_update_slice(
        jnp.zeros((D,), jnp.float32), column_sum(d_time_pre) * lead_flag, (own_place,)
    )
    second_time_bias = lax.dynamic_update_slice(
        jnp.zeros((D,), jnp.float32), column_sum(d_time) * lead_flag, (own_place,)
    )
    bias_grad = jnp.concatenate(
        [column_sum(d_patch), first_time_bias, second_time_bias, column_sum(d_mod_own)]
        + layer_bias_grads
        + [column_sum(d_head)]
    )
    bias_grad, g_patch, g_head, loss_sum, loss_count = lax.psum(
        (bias_grad, g_patch, g_head, loss_part, count_part), ("seq", "dp")
    )
    s_patch = lax.dynamic_slice(g_patch, (0, own_place), (PATCH_IN, own_cols))
    s_head = lax.dynamic_slice(g_head, (own_place, 0), (own_cols, OUT_CH))
    s_embed = jnp.concatenate([s_patch, g_freq, g_time], axis=0)
    s_qkv = jnp.stack([layer_sums[at][0] for at in range(LAYERS)])
    s_proj = jnp.stack([layer_sums[at][1] for at in range(LAYERS)])
    s_up = jnp.stack([layer_sums[at][2] for at in range(LAYERS)])
    s_down = jnp.stack([layer_sums[at][3] for at in range(LAYERS)])
    new_embed, new_first_embed, new_second_embed = adamw(
        embed_rows, s_embed, first_embed, second_embed, RATE_MATRIX
    )
    new_table, new_first_table, new_second_table = adamw(
        class_table, s_table, first_table, second_table, RATE_TABLE
    )
    new_qkv, new_first_qkv, new_second_qkv = adamw(
        qkv_weight, s_qkv, first_qkv, second_qkv, RATE_MATRIX
    )
    new_proj, new_first_proj, new_second_proj = adamw(
        proj_weight, s_proj, first_proj, second_proj, RATE_MATRIX
    )
    new_up, new_first_up, new_second_up = adamw(up_weight, s_up, first_up, second_up, RATE_MATRIX)
    new_down, new_first_down, new_second_down = adamw(
        down_weight, s_down, first_down, second_down, RATE_MATRIX
    )
    new_cond, new_first_cond, new_second_cond = adamw(
        cond_weight, s_cond, first_cond, second_cond, RATE_MATRIX
    )
    new_head, new_first_head, new_second_head = adamw(
        head_weight, s_head, first_head, second_head, RATE_MATRIX
    )
    new_bias, new_first_bias, new_second_bias = adamw(
        all_biases, bias_grad, first_bias, second_bias, RATE_BIAS
    )
    return (
        loss_sum,
        loss_count,
        new_embed,
        new_first_embed,
        new_second_embed,
        new_table,
        new_first_table,
        new_second_table,
        new_qkv,
        new_first_qkv,
        new_second_qkv,
        new_proj,
        new_first_proj,
        new_second_proj,
        new_up,
        new_first_up,
        new_second_up,
        new_down,
        new_first_down,
        new_second_down,
        new_cond,
        new_first_cond,
        new_second_cond,
        new_head,
        new_first_head,
        new_second_head,
        new_bias,
        new_first_bias,
        new_second_bias,
    )


def solution(mesh):
    placed = (
        P("dp", "seq", None),
        P("dp", "seq", None),
        P("dp", "seq"),
        P("dp"),
        P("dp"),
        P(None, "dp"),
        P(None, "dp"),
        P(None, "dp"),
        P(None, "dp"),
        P(None, "dp"),
        P(None, "dp"),
        P(None, "dp", None),
        P(None, "dp", None),
        P(None, "dp", None),
        P(None, "dp", None),
        P(None, "dp", None),
        P(None, "dp", None),
        P(None, "dp", None),
        P(None, "dp", None),
        P(None, "dp", None),
        P(None, "dp", None),
        P(None, "dp", None),
        P(None, "dp", None),
        P("dp", None),
        P("dp", None),
        P("dp", None),
        P("dp", None),
        P("dp", None),
        P("dp", None),
        P(),
        P(),
        P(),
    )
    return jax.shard_map(
        body,
        mesh=mesh,
        in_specs=placed,
        out_specs=(
            P(),
            P(),
            P(None, "dp"),
            P(None, "dp"),
            P(None, "dp"),
            P(None, "dp"),
            P(None, "dp"),
            P(None, "dp"),
            P(None, "dp", None),
            P(None, "dp", None),
            P(None, "dp", None),
            P(None, "dp", None),
            P(None, "dp", None),
            P(None, "dp", None),
            P(None, "dp", None),
            P(None, "dp", None),
            P(None, "dp", None),
            P(None, "dp", None),
            P(None, "dp", None),
            P(None, "dp", None),
            P("dp", None),
            P("dp", None),
            P("dp", None),
            P("dp", None),
            P("dp", None),
            P("dp", None),
            P(),
            P(),
            P(),
        ),
        check_vma=False,
    )
```

time: 3350 us -> 1970 us (0.59)
  waiting for transfers between devices: 2490 us -> 1360 us
  blocking collectives: 179 us -> 82 us
  matrix products: 334 us -> 270 us
  local copies, waits for them, and re-layouts: 176 us -> 126 us
    reduce_scatter x10 -> x8, waiting for transfers between devices: 1600 us -> 668 us  [reduce_rows(): lax.psum_scatter(partial.astype(jnp.bfloat16), 'dp', scatter_dimension=0,...]
    all_to_all x4 -> x0, blocking collectives: 114 us -> none  [the longest x1 40.4 us: layer_forward(): lax.all_to_all(qkv_all, 'seq', split_axis=3, concat_axis=1, tiled=True)]
    all_to_all x5 -> x1, waiting for transfers between devices: 84.8 us -> 0.06 us  [body(): lax.all_to_all(packed, 'seq', split_axis=0, concat_axis=1, tiled=True)]
    psum x3 -> x2, waiting for transfers between devices: 267 us -> 208 us  [the longest x1 125 us: body(): lax.psum((bias_grad, g_patch, g_head, loss_part, count_part), ('seq', 'dp'))]
    dot_general x37 -> x35, matrix products: 284 us -> 226 us  [matdot(): return jnp.dot(left, right, preferred_element_type=jnp.float32)]
    all_to_all x10 -> x2, local copies, waits for them, and re-layouts: 38.1 us -> 0.11 us  [body(): lax.all_to_all(packed, 'seq', split_axis=0, concat_axis=1, tiled=True)]
    unnamed x28 -> x23, waiting for transfers between devices: 100 us -> 76.1 us
    all_gather x11 -> x9, waiting for transfers between devices: 436 us -> 412 us  [the longest x8 358 us: gather_rows(): return lax.all_gather(shard.astype(jnp.bfloat16), 'dp', axis=0, tiled=True)]
  transfers between devices with their start and end apart: 31 -> 22, of which waited for: 23 -> 18; matrix products, arithmetic and copies ran while one was open for 11% -> 13% of each run, Pallas kernels for 0% -> 0%
where the time goes in v1:
time: 1970 us; the launch traced here: 1960 us
  waiting for transfers between devices  1360 us (69%)
  matrix products  270 us (14%)
  local copies, waits for them, and re-layouts  126 us (6%)
  other arithmetic  96.6 us (5%)
  blocking collectives  82 us (4%)
    reduce_scatter x8, waiting for transfers between devices, reduce_rows(): lax.psum_scatter(partial.astype(jnp.bfloat16), 'dp', scatter_dimension=0,...  668 us
    all_gather x8, waiting for transfers between devices, gather_rows(): return lax.all_gather(shard.astype(jnp.bfloat16), 'dp', axis=0, tiled=True)  358 us
    dot_general x35, matrix products, matdot(): return jnp.dot(left, right, preferred_element_type=jnp.float32)  226 us
    psum x1, waiting for transfers between devices, body(): lax.psum((bias_grad, g_patch, g_head, loss_part, count_part), ('seq', 'dp'))  125 us
    psum x1, waiting for transfers between devices, reduce_rows(): return lax.psum(owned, 'seq').astype(jnp.float32)  82.9 us
    unnamed x23, waiting for transfers between devices  76.1 us
    unnamed x329, local copies, waits for them, and re-layouts  60.5 us
    all_gather x1, waiting for transfers between devices, body(): d_modulation = lax.all_gather(d_mod_own, ('dp', 'seq'), axis=0, tiled=True)  54.2 us
  transfers between devices with their start and end apart: 22, of which 18 were waited for; matrix products, arithmetic and copies ran while one was open for 13% of the time, Pallas kernels for 0%

profile of v1, /device:TPU:0, one launch (start us, length us, event | category | flops | bytes accessed | tf_op | source)
XLA Modules:
  0.0 1962.0 jit_solution(15313687998711631161)
XLA Ops:
  10.3 23.1 %all-gather.8 = s32[16,4,2]{1,2,0:T(2,128)S(1)} all-gather(s32[1,4,2]{1,2,0:T(2,128)S(1)} %add_bitcast_fusion), channel_id=1, replica_groups=mesh['seq'=2,'dp'=16] {'dp'}, dimensions={0}, use_global_device_ids=true | all-gather | bytes 544 | tf_op jit(solution)/shard_map/all_gather | solution.py:268
  34.7 19.6 all_gather.33
  83.2 73.3 %all-reduce.9.cloned.1.call-done = f32[32,14336]{1,0:T(8,128)} async-done(((f32[32,14336]{1,0:T(8,128)}), f32[32,14336]{1,0:T(8,128)}) %all-reduce.9.cloned.1.call-update) | async-done | bytes 1835024
  159.2 61.2 %all-gather.20.cloned.1.call-done = bf16[1,1024,3072]{2,1,0:T(8,128)(2,1)} async-done(((bf16[1,64,3072]{2,1,0:T(8,128)(2,1)}), bf16[1,1024,3072]{2,1,0:T(8,128)(2,1)}) %all-gather.20.cloned.1.call-update) | async-done | bytes 6291472 | tf_op jit(solution)/shard_map/all_gather | solution.py:192
  278.5 61.0 %all-gather.24.cloned.1.call-done = bf16[1,1024,4096]{2,1,0:T(8,128)(2,1)} async-done(((bf16[1,64,4096]{2,1,0:T(8,128)(2,1)}), bf16[1,1024,4096]{2,1,0:T(8,128)(2,1)}) %all-gather.24.cloned.1.call-update) | async-done | bytes 8388624 | tf_op jit(solution)/shard_map/all_gather | solution.py:192
  351.0 64.2 %all-gather.26.cloned.1.call-done = bf16[1,4096,1024]{2,1,0:T(8,128)(2,1)} async-done(((bf16[1,256,1024]{2,1,0:T(8,128)(2,1)}), bf16[1,4096,1024]{2,1,0:T(8,128)(2,1)}) %all-gather.26.cloned.1.call-update) | async-done | bytes 8388624 | tf_op jit(solution)/shard_map/all_gather | solution.py:192
  415.2 14.4 fusion.225
  433.5 44.6 %all-gather.28.cloned.1.call-done = bf16[1,1024,3072]{2,1,0:T(8,128)(2,1)} async-done(((bf16[1,64,3072]{2,1,0:T(8,128)(2,1)}), bf16[1,1024,3072]{2,1,0:T(8,128)(2,1)}) %all-gather.28.cloned.1.call-update) | async-done | bytes 6291472 | tf_op jit(solution)/shard_map/all_gather | solution.py:192
  534.4 62.8 %all-gather.32.cloned.1.call-done = bf16[1,1024,4096]{2,1,0:T(8,128)(2,1)} async-done(((bf16[1,64,4096]{2,1,0:T(8,128)(2,1)}), bf16[1,1024,4096]{2,1,0:T(8,128)(2,1)}) %all-gather.32.cloned.1.call-update) | async-done | bytes 8388624 | tf_op jit(solution)/shard_map/all_gather | solution.py:192
  608.7 64.4 %all-gather.34.cloned.1.call-done = bf16[1,4096,1024]{2,1,0:T(8,128)(2,1)} async-done(((bf16[1,256,1024]{2,1,0:T(8,128)(2,1)}), bf16[1,4096,1024]{2,1,0:T(8,128)(2,1)}) %all-gather.34.cloned.1.call-update) | async-done | bytes 8388624 | tf_op jit(solution)/shard_map/all_gather | solution.py:192
  673.2 13.9 fusion.221
  703.0 14.9 convert_reduce_fusion
  853.0 54.2 %all-gather.36.cloned.1.call-done = bf16[32,2,14336]{2,1,0:T(2,128)(2,1)} async-done(((bf16[1,2,14336]{2,1,0:T(2,128)(2,1)}), bf16[32,2,14336]{2,1,0:T(2,128)(2,1)}) %all-gather.36.cloned.1.call-update) | async-done | bytes 1835024 | tf_op jit(solution)/shard_map/all_gather | solution.py:363
  961.8 13.2 convolution_convert_fusion.1
  997.9 39.3 %all-reduce.2 = (f32[]{:T(128)}, f32[]{:T(128)}) all-reduce(f32[]{:T(128)} %fusion.175, f32[]{:T(128)S(6)} %mul_shard_map.3), channel_id=1, replica_groups=mesh['seq'=2,'dp'=16] {'seq','dp'}, use_global_device_ids=true, to_apply=%region_16.17 | all-reduce | flops 2 | bytes 16 | tf_op jit(solution)/shard_map/psum | solution.py:401
  1045.4 55.9 %reduce-scatter.16.cloned.1.call-done = bf16[64,1024]{1,0:T(8,128)(2,1)} async-done(((bf16[1024,1024]{1,0:T(8,128)(2,1)}), bf16[64,1024]{1,0:T(8,128)(2,1)}) %reduce-scatter.16.cloned.1.call-update) | async-done | bytes 131088 | tf_op jit(solution)/shard_map/reduce_scatter | solution.py:196
  1101.4 88.5 %reduce-scatter.14.cloned.1.call-done = bf16[64,3072]{1,0:T(8,128)(2,1)} async-done(((bf16[1024,3072]{1,0:T(8,128)(2,1)}), bf16[64,3072]{1,0:T(8,128)(2,1)}) %reduce-scatter.14.cloned.1.call-update) | async-done | bytes 393232 | tf_op jit(solution)/shard_map/reduce_scatter | solution.py:196
  1189.9 88.5 %reduce-scatter.12.cloned.1.call-done = bf16[64,3072]{1,0:T(8,128)(2,1)} async-done(((bf16[1024,3072]{1,0:T(8,128)(2,1)}), bf16[64,3072]{1,0:T(8,128)(2,1)}) %reduce-scatter.12.cloned.1.call-update) | async-done | bytes 393232 | tf_op jit(solution)/shard_map/reduce_scatter | solution.py:196
  1278.4 108.5 %reduce-scatter.26.cloned.1.call-done = bf16[256,1024]{1,0:T(8,128)(2,1)} async-done(((bf16[4096,1024]{1,0:T(8,128)(2,1)}), bf16[256,1024]{1,0:T(8,128)(2,1)}) %reduce-scatter.26.cloned.1.call-update) | async-done | bytes 524304 | tf_op jit(solution)/shard_map/reduce_scatter | solution.py:196
  1386.9 108.8 %reduce-scatter.24.cloned.1.call-done = bf16[256,1024]{1,0:T(8,128)(2,1)} async-done(((bf16[4096,1024]{1,0:T(8,128)(2,1)}), bf16[256,1024]{1,0:T(8,128)(2,1)}) %reduce-scatter.24.cloned.1.call-update) | async-done | bytes 524304 | tf_op jit(solution)/shard_map/reduce_scatter | solution.py:196
  1495.7 108.9 %reduce-scatter.20.cloned.1.call-done = bf16[64,4096]{1,0:T(8,128)(2,1)} async-done(((bf16[1024,4096]{1,0:T(8,128)(2,1)}), bf16[64,4096]{1,0:T(8,128)(2,1)}) %reduce-scatter.20.cloned.1.call-update) | async-done | bytes 524304 | tf_op jit(solution)/shard_map/reduce_scatter | solution.py:196
  1604.5 109.0 %reduce-scatter.22.cloned.1.call-done = bf16[64,4096]{1,0:T(8,128)(2,1)} async-done(((bf16[1024,4096]{1,0:T(8,128)(2,1)}), bf16[64,4096]{1,0:T(8,128)(2,1)}) %reduce-scatter.22.cloned.1.call-update) | async-done | bytes 524304 | tf_op jit(solution)/shard_map/reduce_scatter | solution.py:196
  1722.4 125.1 %all-reduce.11.cloned.1.call-done = (f32[16,1024]{1,0:T(8,128)}, f32[1024,32]{0,1:T(8,128)}, f32[35872]{0:T(1024)}) async-done(((f32[16,1024]{1,0:T(8,128)}, f32[1024,32]{0,1:T(8,128)}, f32[35872]{0:T(1024)}), (f32[16,1024]{1,0:T(8,128)}, f32[1024,32]{0,1:T(8,128)}, f32[35872]{0:T(1024)})) %all-reduce.11.cloned.1.call-update) | async-done | bytes 340112 | tf_op jit(solution)/shard_map/psum | solution.py:401
  1855.1 82.9 %all-reduce.13.cloned.1.call-done = (bf16[1,64,3072]{2,1,0:T(8,128)(2,1)}, bf16[1,64,3072]{2,1,0:T(8,128)(2,1)}, bf16[1,64,1024]{2,1,0:T(8,128)(2,1)}, bf16[1,64...) async-done(((bf16[1,64,3072]{2,1,0:T(8,128)(2,1)}, ...) | async-done | bytes 3145744 | tf_op jit(solution)/shard_map/psum | solution.py:199
  (575 shorter events, 443.7 us)
Async XLA Ops:
  7.2 149.2 %all-reduce.9.cloned.1.call-start = ((), (), s32[]{:S(2)}) async-start(), calls=%async_computation.28 | async-start | bytes 3670016
  61.0 159.4 %all-gather.20.cloned.1.call-start = ((), (), s32[]{:S(2)}) async-start(), calls=%async_computation.18 | async-start | bytes 6684672 | tf_op jit(solution)/shard_map/all_gather | solution.py:192
  63.4 203.2 %all-gather.22.cloned.1.call-start = ((), (), s32[]{:S(2)}) async-start(), calls=%async_computation.19 | async-start | bytes 2228224 | tf_op jit(solution)/shard_map/all_gather | solution.py:192
  64.3 275.2 %all-gather.24.cloned.1.call-start = ((), (), s32[]{:S(2)}) async-start(), calls=%async_computation.20 | async-start | bytes 8912896 | tf_op jit(solution)/shard_map/all_gather | solution.py:192
  65.5 349.7 %all-gather.26.cloned.1.call-start = ((), (), s32[]{:S(2)}) async-start(), calls=%async_computation.21 | async-start | bytes 8912896 | tf_op jit(solution)/shard_map/all_gather | solution.py:192
  67.7 410.3 %all-gather.28.cloned.1.call-start = ((), (), s32[]{:S(2)}) async-start(), calls=%async_computation.22 | async-start | bytes 6684672 | tf_op jit(solution)/shard_map/all_gather | solution.py:192
  68.3 455.7 %all-gather.30.cloned.1.call-start = ((), (), s32[]{:S(2)}) async-start(), calls=%async_computation.23 | async-start | bytes 2228224 | tf_op jit(solution)/shard_map/all_gather | solution.py:192
  69.1 528.2 %all-gather.32.cloned.1.call-start = ((), (), s32[]{:S(2)}) async-start(), calls=%async_computation.24 | async-start | bytes 8912896 | tf_op jit(solution)/shard_map/all_gather | solution.py:192
  70.5 7.5 all-to-all-start
  73.8 599.3 %all-gather.34.cloned.1.call-start = ((), (), s32[]{:S(2)}) async-start(), calls=%async_computation.25 | async-start | bytes 8912896 | tf_op jit(solution)/shard_map/all_gather | solution.py:192
  74.6 832.6 %all-gather.36.cloned.1.call-start = ((), (), s32[]{:S(2)}) async-start(), calls=%async_computation.26 | async-start | bytes 1892352 | tf_op jit(solution)/shard_map/all_gather | solution.py:363
  853.0 189.5 %reduce-scatter.28.cloned.1.call-start = ((), (), s32[]{:S(2)}) async-start(), calls=%async_computation.27 | async-start | bytes 557056
  915.7 129.7 %reduce-scatter.18.cloned.1.call-start = ((), (), s32[]{:S(2)}) async-start(), calls=%async_computation.13 | async-start | bytes 2228224 | tf_op jit(solution)/shard_map/reduce_scatter | solution.py:196
  919.6 181.8 %reduce-scatter.16.cloned.1.call-start = ((), (), s32[]{:S(2)}) async-start(), calls=%async_computation.12 | async-start | bytes 2228224 | tf_op jit(solution)/shard_map/reduce_scatter | solution.py:196
  924.3 265.5 %reduce-scatter.14.cloned.1.call-start = ((), (), s32[]{:S(2)}) async-start(), calls=%async_computation.11 | async-start | bytes 6684672 | tf_op jit(solution)/shard_map/reduce_scatter | solution.py:196
  934.4 343.9 %reduce-scatter.12.cloned.1.call-start = ((), (), s32[]{:S(2)}) async-start(), calls=%async_computation.10 | async-start | bytes 6684672 | tf_op jit(solution)/shard_map/reduce_scatter | solution.py:196
  946.3 440.6 %reduce-scatter.26.cloned.1.call-start = ((), (), s32[]{:S(2)}) async-start(), calls=%async_computation.17 | async-start | bytes 8912896 | tf_op jit(solution)/shard_map/reduce_scatter | solution.py:196
  960.6 535.0 %reduce-scatter.24.cloned.1.call-start = ((), (), s32[]{:S(2)}) async-start(), calls=%async_computation.16 | async-start | bytes 8912896 | tf_op jit(solution)/shard_map/reduce_scatter | solution.py:196
  975.0 629.5 %reduce-scatter.20.cloned.1.call-start = ((), (), s32[]{:S(2)}) async-start(), calls=%async_computation.14 | async-start | bytes 8912896 | tf_op jit(solution)/shard_map/reduce_scatter | solution.py:196
  985.3 728.3 %reduce-scatter.22.cloned.1.call-start = ((), (), s32[]{:S(2)}) async-start(), calls=%async_computation.15 | async-start | bytes 8912896 | tf_op jit(solution)/shard_map/reduce_scatter | solution.py:196
  995.6 851.8 %all-reduce.11.cloned.1.call-start = ((), (), s32[]{:S(2)}) async-start(), calls=%async_computation.29 | async-start | bytes 688128 | tf_op jit(solution)/shard_map/psum | solution.py:401
  1044.4 669.2 %copy-start.26 = (bf16[64,14336]{1,0:T(8,128)(2,1)S(1)}, bf16[64,14336]{1,0:T(8,128)(2,1)}, u32[]{:S(2)}) copy-start(bf16[64,14336]{1,0:T(8,128)(2,1)} %copy-done.25) | copy-start | bytes 5505028
  1044.4 669.2 %copy-start.105 = (bf16[64,64]{1,0:T(8,128)(2,1)S(1)}, bf16[64,64]{1,0:T(8,128)(2,1)}, u32[]{:S(2)}) copy-start(bf16[64,64]{1,0:T(8,128)(2,1)} %copy-done.104) | copy-start | bytes 24580
  1044.4 893.6 %all-reduce.13.cloned.1.call-start = ((), (), s32[]{:S(2)}) async-start(), calls=%async_computation.30 | async-start | bytes 6291456 | tf_op jit(solution)/shard_map/psum | solution.py:199
  (144 other events, 3821.3 us)
Sparse Core Ops, SparseCore 0:
  61.1 95.2 all-reduce.8
  159.3 61.0 all-gather.19
  223.1 39.9 all-gather.21
  265.7 73.6 all-gather.23
  342.0 73.1 all-gather.25
  417.9 60.0 all-gather.27
  480.8 39.9 all-gather.29
  523.6 73.6 all-gather.31
  600.0 73.1 all-gather.33
  853.1 54.0 all-gather.35
  915.8 54.7 reduce-scatter.27
  975.2 61.1 reduce-scatter.17
  1040.7 60.5 reduce-scatter.15
  1105.7 84.1 reduce-scatter.13
  1193.6 84.6 reduce-scatter.11
  1282.8 103.9 reduce-scatter.25
  1391.3 104.3 reduce-scatter.23
  1500.1 104.3 reduce-scatter.19
  1609.1 104.3 reduce-scatter.21
  1720.7 126.7 all-reduce.10
  1850.2 87.8 all-reduce.12

commit v2 on v1

--- a/solution.py
+++ b/solution.py
@@ -1,8 +1,11 @@
+import functools
 import math
 
 import jax
 import jax.numpy as jnp
 from jax import lax
+from jax.experimental import pallas as pl
+from jax.experimental.pallas import tpu as pltpu
 from jax.sharding import PartitionSpec as P
 
 D = 1024
@@ -68,6 +71,381 @@
 
 def split_six(modul):
     return [modul[:, piece * D : (piece + 1) * D] for piece in range(6)]
+
+
+MESH = pl.DeviceIdType.MESH
+TILE = 256
+PARTS = 4
+
+
+def scatter_kernel(
+    per_layer,
+    total,
+    lines,
+    *refs,
+):
+    count = 8 * LAYERS
+    sources = [refs[8 * layer : 8 * layer + 8] for layer in range(LAYERS)]
+    (
+    out_ref,
+    lhs_buf,
+    act_buf,
+    wide_buf,
+    down_buf,
+    load_sem,
+    made,
+    core_in,
+    x_out,
+    x_in,
+    p_keep,
+    yq_out,
+    yq_in,
+    q_keep,
+    yp_out,
+    yp_in,
+    p_line,
+    zq_out,
+    zq_in,
+    zp_out,
+    zp_in,
+    xq_out,
+    xq_in,
+    xp_out,
+    xp_in,
+    core_sem,
+    x_sem,
+    yq_sem,
+    yp_sem,
+    zq_sem,
+    zp_sem,
+    xq_sem,
+    xp_sem,
+    ) = refs[count:]
+    seq = lax.axis_index("seq")
+    dp = lax.axis_index("dp")
+    core = lax.rem(dp, 2)
+    why = lax.rem(dp // 2, 2)
+    zed = dp // 4
+    core_peer = {"seq": seq, "dp": dp + 1 - 2 * core}
+    x_peer = {"seq": 1 - seq, "dp": dp}
+    y_peer = {"seq": seq, "dp": dp + 2 - 4 * why}
+
+    def z_place(step):
+        return lax.rem(zed + step, lines)
+
+    def z_peer(step):
+        return {"seq": seq, "dp": z_place(step) * 4 + 2 * why + core}
+
+    barrier = pltpu.get_barrier_semaphore()
+    for peer in [core_peer, x_peer, y_peer] + [z_peer(step) for step in range(1, lines)]:
+        pl.semaphore_signal(barrier, inc=1, device_id=peer, device_id_type=MESH)
+    pl.semaphore_wait(barrier, 2 + lines)
+
+    def remote(source, target, sems, peer):
+        return pltpu.make_async_remote_copy(
+            src_ref=source,
+            dst_ref=target,
+            send_sem=sems.at[0],
+            recv_sem=sems.at[1],
+            device_id=peer,
+            device_id_type=MESH,
+        )
+
+    def core_copy(slot):
+        return remote(made.at[slot, 1 - core], core_in.at[slot], core_sem.at[slot], core_peer)
+
+    def x_copy(slot):
+        return remote(x_out.at[slot], x_in.at[slot], x_sem.at[slot], x_peer)
+
+    def yq_copy(slot):
+        return remote(yq_out.at[slot], yq_in.at[slot], yq_sem.at[slot], y_peer)
+
+    def yp_copy(slot):
+        return remote(yp_out.at[slot], yp_in.at[slot], yp_sem.at[slot], y_peer)
+
+    def zq_copy(slot, step):
+        return remote(
+            zq_out.at[slot, z_place(step)],
+            zq_in.at[slot, step - 1],
+            zq_sem.at[slot, step - 1],
+            z_peer(step),
+        )
+
+    def zp_copy(slot, step):
+        return remote(
+            zp_out.at[slot, z_place(step)],
+            zp_in.at[slot, step - 1],
+            zp_sem.at[slot, step - 1],
+            z_peer(step),
+        )
+
+    def xq_copy(slot):
+        return remote(xq_out.at[slot], xq_in.at[slot], xq_sem.at[slot], x_peer)
+
+    def xp_copy(slot):
+        return remote(xp_out.at[slot], xp_in.at[slot], xp_sem.at[slot], x_peer)
+
+    def loads(unit, slot):
+        found = []
+        for layer in range(LAYERS):
+            merged, a_one, a_two, act, d_attn, d_qkv, d_up, d_down = sources[layer]
+            at = unit - layer * per_layer
+
+            def slab(ref, index, size):
+                return ref.at[:, pl.ds(pl.multiple_of(index * size, size), size)]
+
+            wide_to = wide_buf.at[slot], load_sem.at[1, slot]
+            lhs_to = lhs_buf.at[slot], load_sem.at[0, slot]
+            found += [
+                (at == 0, (merged, *lhs_to), (d_attn, *wide_to)),
+                (
+                    jnp.logical_and(at >= 1, at < 4),
+                    (a_one, *lhs_to),
+                    (slab(d_qkv, at - 1, D), *wide_to),
+                ),
+                (
+                    jnp.logical_and(at >= 4, at < 8),
+                    (a_two, *lhs_to),
+                    (slab(d_up, at - 4, D), *wide_to),
+                ),
+                (
+                    jnp.logical_and(at >= 8, at < per_layer),
+                    (slab(d_down, at - 8, TILE), down_buf.at[slot], load_sem.at[2, slot]),
+                ),
+                (at == 8, (act, act_buf, load_sem.at[3, 0])),
+            ]
+        return found
+
+    def prefetch(unit):
+        for due, *moves in loads(unit, lax.rem(unit, 2)):
+
+            @pl.when(due)
+            def _():
+                for move in moves:
+                    pltpu.make_async_copy(*move).start()
+
+    def fetched(unit):
+        for due, *moves in loads(unit, lax.rem(unit, 2)):
+
+            @pl.when(due)
+            def _():
+                for move in moves:
+                    pltpu.make_async_copy(*move).wait()
+
+    def dot_rows(left, right):
+        return lax.dot_general(
+            left, right, (((0,), (0,)), ((), ())), preferred_element_type=jnp.float32
+        )
+
+    def compute(unit):
+        at = lax.rem(unit, per_layer)
+        slot = lax.rem(unit, 2)
+        fetched(unit)
+
+        @pl.when(at < 8)
+        def _():
+            def rows(pair, carry):
+                left = lhs_buf[slot, :, pl.ds(pl.multiple_of(pair * 128, 128), 128)]
+                block = dot_rows(left, wide_buf[slot]).astype(jnp.bfloat16)
+                for own in range(2):
+                    for part in range(PARTS):
+                        made[slot, own, part, pair // 2, lax.rem(pair, 2)] = block[
+                            own * 64 : own * 64 + 64, part * TILE : part * TILE + TILE
+                        ]
+                return carry
+
+            lax.fori_loop(0, 2 * lines, rows, 0)
+
+        @pl.when(at >= 8)
+        def _():
+            def rows(pair, carry):
+                left = act_buf[:, pl.ds(pl.multiple_of(pair * 512, 512), 512)]
+                block = dot_rows(left, down_buf[slot]).astype(jnp.bfloat16)
+                for own in range(2):
+                    for part in range(PARTS):
+                        first = own * 256 + part * 64
+                        made[slot, own, part, pair // 2, lax.rem(pair, 2)] = block[
+                            first : first + 64
+                        ]
+                return carry
+
+            lax.fori_loop(0, 2 * lines, rows, 0)
+
+    def wide_sum(one, other):
+        return one.astype(jnp.float32) + other.astype(jnp.float32)
+
+    def stage_two(slot):
+        core_copy(slot).wait()
+
+        def rows(line, carry):
+            for side in range(2):
+                x_out[slot, line, side] = wide_sum(
+                    made[slot, core, 1 - seq, line, side], core_in[slot, 1 - seq, line, side]
+                ).astype(jnp.bfloat16)
+                p_keep[slot, line, side] = wide_sum(
+                    made[slot, core, seq, line, side], core_in[slot, seq, line, side]
+                ).astype(jnp.bfloat16)
+            for part in range(2):
+                yq_out[slot, line, part] = wide_sum(
+                    made[slot, core, 2 + part, line, 1 - why],
+                    core_in[slot, 2 + part, line, 1 - why],
+                ).astype(jnp.bfloat16)
+                q_keep[slot, line, part] = wide_sum(
+                    made[slot, core, 2 + part, line, why], core_in[slot, 2 + part, line, why]
+                ).astype(jnp.bfloat16)
+            return carry
+
+        lax.fori_loop(0, lines, rows, 0)
+        x_copy(slot).start()
+        yq_copy(slot).start()
+
+    def stage_three(slot):
+        x_copy(slot).wait()
+        yq_copy(slot).wait()
+
+        def rows(line, carry):
+            yp_out[slot, line] = wide_sum(
+                p_keep[slot, line, 1 - why], x_in[slot, line, 1 - why]
+            ).astype(jnp.bfloat16)
+            p_line[slot, line] = wide_sum(p_keep[slot, line, why], x_in[slot, line, why]).astype(
+                jnp.bfloat16
+            )
+            for part in range(2):
+                zq_out[slot, line, part] = wide_sum(
+                    q_keep[slot, line, part], yq_in[slot, line, part]
+                ).astype(jnp.bfloat16)
+            return carry
+
+        lax.fori_loop(0, lines, rows, 0)
+        yp_copy(slot).start()
+        for step in range(1, lines):
+            zq_copy(slot, step).start()
+
+    def stage_four(slot):
+        yp_copy(slot).wait()
+        for step in range(1, lines):
+            zq_copy(slot, step).wait()
+
+        def rows(line, carry):
+            zp_out[slot, line] = wide_sum(p_line[slot, line], yp_in[slot, line]).astype(
+                jnp.bfloat16
+            )
+            return carry
+
+        lax.fori_loop(0, lines, rows, 0)
+        total_q = zq_out[slot, zed].astype(jnp.float32)
+        for step in range(1, lines):
+            total_q = total_q + zq_in[slot, step - 1].astype(jnp.float32)
+        xq_out[slot] = total_q.astype(jnp.bfloat16)
+        for step in range(1, lines):
+            zp_copy(slot, step).start()
+        xq_copy(slot).start()
+
+    def stage_five(unit, slot):
+        for step in range(1, lines):
+            zp_copy(slot, step).wait()
+        xq_copy(slot).wait()
+        total_p = zp_out[slot, zed].astype(jnp.float32)
+        for step in range(1, lines):
+            total_p = total_p + zp_in[slot, step - 1].astype(jnp.float32)
+        rounded = total_p.astype(jnp.bfloat16)
+        xp_out[slot] = rounded
+        xp_copy(slot).start()
+        out_ref[unit, seq] = rounded.astype(jnp.float32)
+        for part in range(2):
+            out_ref[unit, 2 + part] = wide_sum(xq_out[slot, part], xq_in[slot, part])
+
+    def stage_six(unit, slot):
+        xp_copy(slot).wait()
+        out_ref[unit, 1 - seq] = xp_in[slot].astype(jnp.float32)
+
+    prefetch(jnp.int32(0))
+
+    def turn(at, carry):
+        def when_due(behind, run):
+            unit = at - behind
+
+            @pl.when(jnp.logical_and(unit >= 0, unit < total))
+            def _():
+                run(unit, lax.rem(unit, 2))
+
+        prefetch(at + 1)
+        when_due(5, stage_six)
+        when_due(4, stage_five)
+        when_due(3, lambda unit, slot: stage_four(slot))
+        when_due(2, lambda unit, slot: stage_three(slot))
+        when_due(1, lambda unit, slot: stage_two(slot))
+
+        @pl.when(at < total)
+        def _():
+            compute(at)
+            core_copy(lax.rem(at, 2)).start()
+
+        return carry
+
+    lax.fori_loop(0, total + 5, turn, 0)
+
+
+def scatter_sums(operands, lines):
+    toks, hidden = operands[3].shape
+    width = D
+    per_layer = 12
+    total = LAYERS * per_layer
+    bf = jnp.bfloat16
+    dma = pltpu.SemaphoreType.DMA
+
+    def buf(*shape):
+        return pltpu.VMEM((2,) + shape, bf)
+
+    scratch = [
+        buf(toks, width),
+        pltpu.VMEM((toks, hidden), bf),
+        buf(toks, width),
+        buf(toks, TILE),
+        dma((4, 2)),
+        buf(2, PARTS, lines, 2, 64, TILE),
+        buf(PARTS, lines, 2, 64, TILE),
+        buf(lines, 2, 64, TILE),
+        buf(lines, 2, 64, TILE),
+        buf(lines, 2, 64, TILE),
+        buf(lines, 2, 64, TILE),
+        buf(lines, 2, 64, TILE),
+        buf(lines, 2, 64, TILE),
+        buf(lines, 64, TILE),
+        buf(lines, 64, TILE),
+        buf(lines, 64, TILE),
+        buf(lines, 2, 64, TILE),
+        buf(lines - 1, 2, 64, TILE),
+        buf(lines, 64, TILE),
+        buf(lines - 1, 64, TILE),
+        buf(2, 64, TILE),
+        buf(2, 64, TILE),
+        buf(64, TILE),
+        buf(64, TILE),
+        dma((2, 2)),
+        dma((2, 2)),
+        dma((2, 2)),
+        dma((2, 2)),
+        dma((2, lines - 1, 2)),
+        dma((2, lines - 1, 2)),
+        dma((2, 2)),
+        dma((2, 2)),
+    ]
+    return pl.pallas_call(
+        functools.partial(scatter_kernel, per_layer, total, lines),
+        out_shape=jax.ShapeDtypeStruct((total, PARTS, 64, TILE), jnp.float32),
+        in_specs=[pl.BlockSpec(memory_space=pl.ANY)] * len(operands),
+        out_specs=pl.BlockSpec(memory_space=pltpu.VMEM),
+        scratch_shapes=scratch,
+        compiler_params=pltpu.CompilerParams(
+            collective_id=1, has_side_effects=True, vmem_limit_bytes=56 * 1024 * 1024
+        ),
+        cost_estimate=pl.CostEstimate(
+            flops=2 * total * toks * width * width,
+            bytes_accessed=total * 4 * 1024 * 1024,
+            transcendentals=0,
+        ),
+    )(*operands)
 
 
 def layer_forward(stream, modul, weight_set, bias_part, pad_mask):
@@ -141,11 +519,9 @@
     shift_one, scale_one, gate_one, shift_two, scale_two, gate_two = split_six(modul)
     d_gate_two = jnp.sum(grad_in * down_out, axis=1)
     d_down = (grad_in * gate_two[:, None, :]).astype(jnp.bfloat16).reshape(images * tok_rows, D)
-    s_down = reduce_rows(matdot(activated.T, d_down))
     d_activated = matdot(d_down, w_down.T)
     _, gelu_back = jax.vjp(lambda inner: jax.nn.gelu(inner, approximate=True), up_pre)
     d_up = gelu_back(d_activated)[0].astype(jnp.bfloat16)
-    s_up = reduce_rows(matdot(a_two.T, d_up))
     d_a_two = matdot(d_up, w_up.T).reshape(images, tok_rows, D)
     _, mod_back_two = jax.vjp(modulate, stream_one, shift_two, scale_two)
     d_stream_one, d_shift_two, d_scale_two = mod_back_two(d_a_two)
@@ -154,7 +530,6 @@
     d_attn = (
         (d_stream_one * gate_one[:, None, :]).astype(jnp.bfloat16).reshape(images * tok_rows, D)
     )
-    s_proj = reduce_rows(matdot(merged.T, d_attn))
     d_heads = matdot(d_attn, w_proj.T).astype(jnp.bfloat16)
     d_heads = d_heads.reshape(images, tok_rows, HEADS, HEAD_DIM)
     d_values = jnp.einsum(
@@ -174,7 +549,6 @@
     ) * HEAD_DIM ** (-0.5)
     d_qkv = jnp.stack([d_queries, d_keys, d_values], axis=2).astype(jnp.bfloat16)
     d_qkv = d_qkv.reshape(images * tok_rows, 3 * D)
-    s_qkv = reduce_rows(matdot(a_one.T, d_qkv))
     d_a_one = matdot(d_qkv, w_qkv.T).reshape(images, tok_rows, D)
     _, mod_back_one = jax.vjp(modulate, stream, shift_one, scale_one)
     d_stream, d_shift_one, d_scale_one = mod_back_one(d_a_one)
@@ -185,7 +559,8 @@
     d_bias = jnp.concatenate(
         [column_sum(d_qkv), column_sum(d_attn), column_sum(d_up), column_sum(d_down)]
     )
-    return (d_stream, d_modul, (s_qkv, s_proj, s_up, s_down), d_bias)
+    factors = (merged, a_one, a_two, activated, d_attn, d_qkv, d_up, d_down)
+    return (d_stream, d_modul, factors, d_bias)
 
 
 def gather_rows(shard):
@@ -197,6 +572,41 @@
         partial.astype(jnp.bfloat16), "dp", scatter_dimension=0, tiled=True
     )
     return lax.psum(owned, "seq").astype(jnp.float32)
+
+
+def weight_sums(factors):
+    dp_parts = lax.axis_size("dp")
+    by_kernel = (
+        lax.axis_size("seq") == 2
+        and dp_parts % 4 == 0
+        and D // dp_parts == 64
+        and FF // dp_parts == PARTS * 64
+    )
+    if not by_kernel:
+        return [
+            (
+                reduce_rows(matdot(a_one.T, d_qkv)),
+                reduce_rows(matdot(merged.T, d_attn)),
+                reduce_rows(matdot(a_two.T, d_up)),
+                reduce_rows(matdot(activated.T, d_down)),
+            )
+            for merged, a_one, a_two, activated, d_attn, d_qkv, d_up, d_down in factors
+        ]
+    units = scatter_sums([each for layer in factors for each in layer], dp_parts // 4)
+    units = units.reshape(LAYERS, 12, PARTS, 64, TILE)
+
+    def by_columns(some):
+        return some.transpose(2, 0, 1, 3).reshape(64, some.shape[0] * D)
+
+    return [
+        (
+            by_columns(layer[1:4]),
+            by_columns(layer[:1]),
+            by_columns(layer[4:8]),
+            layer[8:].transpose(1, 2, 0, 3).reshape(PARTS * 64, D),
+        )
+        for layer in units
+    ]
 
 
 def adamw(weight, gradient, first, second, rate):
@@ -346,11 +756,11 @@
     g_head = matdot(a_final.T, d_head)
     d_a_final = matdot(d_head, head_rows).reshape(images, tok_rows, D)
     d_stream, d_final_shift, d_final_scale = final_back(d_a_final)
-    layer_sums = [None] * LAYERS
+    layer_factors = [None] * LAYERS
     layer_bias_grads = [None] * LAYERS
     modul_grads = [None] * LAYERS
     for at in reversed(range(LAYERS)):
-        d_stream, modul_grads[at], layer_sums[at], layer_bias_grads[at] = layer_backward(
+        d_stream, modul_grads[at], layer_factors[at], layer_bias_grads[at] = layer_backward(
             d_stream,
             inputs_kept[at],
             modulation[:, 6 * at * D : 6 * (at + 1) * D],
@@ -404,6 +814,7 @@
     s_patch = lax.dynamic_slice(g_patch, (0, own_place), (PATCH_IN, own_cols))
     s_head = lax.dynamic_slice(g_head, (own_place, 0), (own_cols, OUT_CH))
     s_embed = jnp.concatenate([s_patch, g_freq, g_time], axis=0)
+    layer_sums = weight_sums(layer_factors)
     s_qkv = jnp.stack([layer_sums[at][0] for at in range(LAYERS)])
     s_proj = jnp.stack([layer_sums[at][1] for at in range(LAYERS)])
     s_up = jnp.stack([layer_sums[at][2] for at in range(LAYERS)])

time: 1970 us -> 1460 us (0.74)
  waiting for transfers between devices: 1360 us -> 603 us
  Pallas kernels: 0 us -> 255 us
  matrix products: 270 us -> 210 us
  local copies, waits for them, and re-layouts: 126 us -> 184 us
    reduce_scatter x8 -> x0, waiting for transfers between devices: 668 us -> none  [reduce_rows(): lax.psum_scatter(partial.astype(jnp.bfloat16), 'dp', scatter_dimension=0,...]
    pallas_call x0 -> x1, Pallas kernels: none -> 255 us  [scatter_sums(): pl.pallas_call(functools.partial(scatter_kernel, per_layer, total, lines)...]
    psum x1 -> x0, waiting for transfers between devices: 82.9 us -> none  [reduce_rows(): return lax.psum(owned, 'seq').astype(jnp.float32)]
    dot_general x35 -> x27, matrix products: 226 us -> 168 us  [matdot(): return jnp.dot(left, right, preferred_element_type=jnp.float32)]
    all_gather x1, waiting for transfers between devices: 54.2 us -> 0.01 us  [body(): d_modulation = lax.all_gather(d_mod_own, ('dp', 'seq'), axis=0, tiled=True)]
    unnamed x23 -> x14, waiting for transfers between devices: 76.1 us -> 121 us
    convert_element_type x4 -> x6, local copies, waits for them, and re-layouts: 7.2 us -> 37 us  [layer_backward(): jnp.stack([d_queries, d_keys, d_values], axis=2).astype(jnp.bfloat16)]
    unnamed x329 -> x323, local copies, waits for them, and re-layouts: 60.5 us -> 56.1 us
  transfers between devices with their start and end apart: 22 -> 13, of which waited for: 18 -> 10; matrix products, arithmetic and copies ran while one was open for 13% -> 16% of each run, Pallas kernels for 0% -> 0%
where the time goes in v2:
time: 1460 us; the launch traced here: 1450 us
  waiting for transfers between devices  603 us (41%)
  Pallas kernels  255 us (17%)
  matrix products  210 us (14%)
  local copies, waits for them, and re-layouts  184 us (13%)
  other arithmetic  95.5 us (7%)
  blocking collectives  83.4 us (6%)
  between operations  18.2 us (1%)
    all_gather x8, waiting for transfers between devices, gather_rows(): return lax.all_gather(shard.astype(jnp.bfloat16), 'dp', axis=0, tiled=True)  351 us
    pallas_call x1, Pallas kernels, scatter_sums(): pl.pallas_call(functools.partial(scatter_kernel, per_layer, total, lines)...  255 us
    dot_general x27, matrix products, matdot(): return jnp.dot(left, right, preferred_element_type=jnp.float32)  168 us
    psum x1, waiting for transfers between devices, body(): lax.psum((bias_grad, g_patch, g_head, loss_part, count_part), ('seq', 'dp'))  131 us
    unnamed x14, waiting for transfers between devices  121 us
    unnamed x323, local copies, waits for them, and re-layouts  56.1 us
    psum x1, blocking collectives, body(): lax.psum((bias_grad, g_patch, g_head, loss_part, count_part), ('seq', 'dp'))  40.8 us
    convert_element_type x6, local copies, waits for them, and re-layouts, layer_backward(): jnp.stack([d_queries, d_keys, d_values], axis=2).astype(jnp.bfloat16)  37 us
  transfers between devices with their start and end apart: 13, of which 10 were waited for; matrix products, arithmetic and copies ran while one was open for 16% of the time, Pallas kernels for 0%

profile of v2, /device:TPU:0, one launch (start us, length us, event | category | flops | bytes accessed | tf_op | source)
XLA Modules:
  0.0 1452.6 jit_solution(17662219072325314168)
XLA Ops:
  10.3 23.1 %all-gather.8 = s32[16,4,2]{1,2,0:T(2,128)S(1)} all-gather(s32[1,4,2]{1,2,0:T(2,128)S(1)} %add_bitcast_fusion), channel_id=1, replica_groups=mesh['seq'=2,'dp'=16] {'dp'}, dimensions={0}, use_global_device_ids=true | all-gather | bytes 544 | tf_op jit(solution)/shard_map/all_gather | solution.py:678
  34.7 19.6 %all_gather.33 = bf16[304,1024]{0,1:T(8,128)(2,1)S(1)} all-gather(bf16[304,64]{0,1:T(8,128)(2,1)S(1)} %pad_maximum_fusion.2), channel_id=1, replica_groups=mesh['seq'=2,'dp'=16] {'dp'}, dimensions={1}, use_global_device_ids=true | all-gather | bytes 661504 | tf_op jit(solution)/shard_map/all_gather | solution.py:682
  83.9 72.5 %all-reduce.7.cloned.1.call-done = f32[32,14336]{1,0:T(8,128)} async-done(((f32[32,14336]{1,0:T(8,128)}), f32[32,14336]{1,0:T(8,128)}) %all-reduce.7.cloned.1.call-update) | async-done | bytes 1835024
  159.2 61.2 %all-gather.20.cloned.1.call-done = bf16[1,1024,3072]{2,1,0:T(8,128)(2,1)} async-done(((bf16[1,64,3072]{2,1,0:T(8,128)(2,1)}), bf16[1,1024,3072]{2,1,0:T(8,128)(2,1)}) %all-gather.20.cloned.1.call-update) | async-done | bytes 6291472 | tf_op jit(solution)/shard_map/all_gather | solution.py:567
  228.6 9.1 reshape.645
  280.7 58.8 %all-gather.24.cloned.1.call-done = bf16[1,1024,4096]{2,1,0:T(8,128)(2,1)} async-done(((bf16[1,64,4096]{2,1,0:T(8,128)(2,1)}), bf16[1,1024,4096]{2,1,0:T(8,128)(2,1)}) %all-gather.24.cloned.1.call-update) | async-done | bytes 8388624 | tf_op jit(solution)/shard_map/all_gather | solution.py:567
  339.4 14.5 multiply_convert_fusion.3
  353.9 61.3 %all-gather.26.cloned.1.call-done = bf16[1,4096,1024]{2,1,0:T(8,128)(2,1)} async-done(((bf16[1,256,1024]{2,1,0:T(8,128)(2,1)}), bf16[1,4096,1024]{2,1,0:T(8,128)(2,1)}) %all-gather.26.cloned.1.call-update) | async-done | bytes 8388624 | tf_op jit(solution)/shard_map/all_gather | solution.py:567
  415.2 11.7 fusion.217
  430.7 47.3 %all-gather.28.cloned.1.call-done = bf16[1,1024,3072]{2,1,0:T(8,128)(2,1)} async-done(((bf16[1,64,3072]{2,1,0:T(8,128)(2,1)}), bf16[1,1024,3072]{2,1,0:T(8,128)(2,1)}) %all-gather.28.cloned.1.call-update) | async-done | bytes 6291472 | tf_op jit(solution)/shard_map/all_gather | solution.py:567
  536.2 61.1 %all-gather.32.cloned.1.call-done = bf16[1,1024,4096]{2,1,0:T(8,128)(2,1)} async-done(((bf16[1,64,4096]{2,1,0:T(8,128)(2,1)}), bf16[1,1024,4096]{2,1,0:T(8,128)(2,1)}) %all-gather.32.cloned.1.call-update) | async-done | bytes 8388624 | tf_op jit(solution)/shard_map/all_gather | solution.py:567
  597.2 14.5 multiply_convert_fusion.2
  611.8 61.4 %all-gather.34.cloned.1.call-done = bf16[1,4096,1024]{2,1,0:T(8,128)(2,1)} async-done(((bf16[1,256,1024]{2,1,0:T(8,128)(2,1)}), bf16[1,4096,1024]{2,1,0:T(8,128)(2,1)}) %all-gather.34.cloned.1.call-update) | async-done | bytes 8388624 | tf_op jit(solution)/shard_map/all_gather | solution.py:567
  673.2 11.7 fusion.213
  700.4 14.7 %convert_reduce_fusion = (f32[4096]{0:T(1024)}, bf16[512,4096]{1,0:T(8,128)(2,1)S(1)}) fusion(f32[512,4096]{1,0:T(8,128)} %get-tuple-element.205, f32[4096]{0:T(1024)S(1)} %get-tuple-element.144, bf16[512,1024]{1,0:T(8,128)(2,1)S(1)} %bitcast.424, bf16[1,4096,1024]{2,1,0:T(8,128)(2,1)} %all-gather.34.cloned.1.call-done), kind=kOutput, calls=%fused_computation.36 | convolution fusion | flops 4343197696 | bytes 22052864 | tf_op jit(solution)/shard_map/dot_general | solution.py:35
  774.3 13.9 convert_reduce_fusion.1
  788.2 11.1 multiply_reduce_fusion.10
  855.4 8.7 reshape.641.refs_13_
  864.2 8.7 reshape.640.refs_5_
  872.9 255.0 %shard_map.527 = f32[24,4,64,256]{3,2,1,0:T(8,128)} custom-call(bf16[512,1024]{1,0:T(8,128)(2,1)} %copy.232.refs_0_, bf16[512,1024]{1,0:T(8,128)(2,1)} %fusion.80.refs_1_, bf16[512,1024]{1,0:T(8,128)(2,1)} %fusion.62.refs_2_, bf16[512,4096]{1,0:T(8,128)(2,1)} %get-tuple-element.198.refs_3_, bf16[512,1024]{1,0:T(8,128)(2,1)} %bitcast.423, ...), custom_call_target="tpu_custom_call" | custom-call | flops 25769803776 | bytes 100663296 | tf_op jit(solution)/shard_map/pallas_call | solution.py:434
  1177.2 40.8 %all-reduce.2 = (f32[]{:T(128)}, f32[]{:T(128)}) all-reduce(f32[]{:T(128)} %fusion.171, f32[]{:T(128)S(6)} %mul_shard_map.3), channel_id=1, replica_groups=mesh['seq'=2,'dp'=16] {'seq','dp'}, use_global_device_ids=true, to_apply=%region_16.17 | all-reduce | flops 2 | bytes 16 | tf_op jit(solution)/shard_map/psum | solution.py:811
  1250.2 8.7 multiply_subtract_fusion
  1260.6 46.1 %reduce-scatter.4.cloned.1.call-done = f32[64,64]{1,0:T(8,128)} async-done(((f32[1024,64]{1,0:T(8,128)}), f32[64,64]{1,0:T(8,128)}) %reduce-scatter.4.cloned.1.call-update) | async-done | bytes 16400
  1308.8 131.1 %all-reduce.9.cloned.1.call-done = (f32[16,1024]{1,0:T(8,128)}, f32[1024,32]{0,1:T(8,128)}, f32[35872]{0:T(1024)}) async-done(((f32[16,1024]{1,0:T(8,128)}, f32[1024,32]{0,1:T(8,128)}, f32[35872]{0:T(1024)}), (f32[16,1024]{1,0:T(8,128)}, f32[1024,32]{0,1:T(8,128)}, f32[35872]{0:T(1024)})) %all-reduce.9.cloned.1.call-update) | async-done | bytes 340112 | tf_op jit(solution)/shard_map/psum | solution.py:811
  (561 shorter events, 368.1 us)
Async XLA Ops:
  7.2 149.2 %all-reduce.7.cloned.1.call-start = ((), (), s32[]{:S(2)}) async-start(), calls=%async_computation.12 | async-start | bytes 3670016
  61.0 159.4 %all-gather.20.cloned.1.call-start = ((), (), s32[]{:S(2)}) async-start(), calls=%async_computation.2 | async-start | bytes 6684672 | tf_op jit(solution)/shard_map/all_gather | solution.py:567
  63.4 205.6 %all-gather.22.cloned.1.call-start = ((), (), s32[]{:S(2)}) async-start(), calls=%async_computation.3 | async-start | bytes 2228224 | tf_op jit(solution)/shard_map/all_gather | solution.py:567
  64.2 275.2 %all-gather.24.cloned.1.call-start = ((), (), s32[]{:S(2)}) async-start(), calls=%async_computation.4 | async-start | bytes 8912896 | tf_op jit(solution)/shard_map/all_gather | solution.py:567
  65.5 349.7 %all-gather.26.cloned.1.call-start = ((), (), s32[]{:S(2)}) async-start(), calls=%async_computation.5 | async-start | bytes 8912896 | tf_op jit(solution)/shard_map/all_gather | solution.py:567
  67.7 410.3 %all-gather.28.cloned.1.call-start = ((), (), s32[]{:S(2)}) async-start(), calls=%async_computation.6 | async-start | bytes 6684672 | tf_op jit(solution)/shard_map/all_gather | solution.py:567
  68.3 458.1 %all-gather.30.cloned.1.call-start = ((), (), s32[]{:S(2)}) async-start(), calls=%async_computation.7 | async-start | bytes 2228224 | tf_op jit(solution)/shard_map/all_gather | solution.py:567
  69.1 528.2 %all-gather.32.cloned.1.call-start = ((), (), s32[]{:S(2)}) async-start(), calls=%async_computation.8 | async-start | bytes 8912896 | tf_op jit(solution)/shard_map/all_gather | solution.py:567
  70.5 7.7 all-to-all-start
  74.0 599.2 %all-gather.34.cloned.1.call-start = ((), (), s32[]{:S(2)}) async-start(), calls=%async_computation.9 | async-start | bytes 8912896 | tf_op jit(solution)/shard_map/all_gather | solution.py:567
  74.7 1167.2 %all-gather.36.cloned.1.call-start = ((), (), s32[]{:S(2)}) async-start(), calls=%async_computation.10 | async-start | bytes 1892352 | tf_op jit(solution)/shard_map/all_gather | solution.py:773
  74.8 264.6 %copy-start.119 = (f32[4096]{0:T(1024)}, f32[4096]{0:T(1024)S(1)}, u32[]{:S(2)}) copy-start(f32[4096]{0:T(1024)S(1)} %get-tuple-element.145) | copy-start | bytes 49156
  78.3 613.4 %copy-start.63 = (f32[2,256,33]{1,0,2:T(2,128)}, f32[2,256,33]{1,0,2:T(2,128)S(1)}, u32[]{:S(2)}) copy-start(f32[2,256,33]{1,0,2:T(2,128)S(1)} %all_to_all.16) | copy-start | bytes 202756
  1156.1 150.6 %reduce-scatter.4.cloned.1.call-start = ((), (), s32[]{:S(2)}) async-start(), calls=%async_computation.11 | async-start | bytes 557056
  1250.1 189.8 %all-reduce.9.cloned.1.call-start = ((), (), s32[]{:S(2)}) async-start(), calls=%async_computation.13 | async-start | bytes 688128 | tf_op jit(solution)/shard_map/psum | solution.py:811
  1258.9 181.8 %copy-start.92 = (f32[64,32]{0,1:T(8,128)S(1)}, f32[64,32]{0,1:T(8,128)}, u32[]{:S(2)}) copy-start(f32[64,32]{0,1:T(8,128)} %param.58) | copy-start | bytes 24580
  1259.0 181.8 %copy-start.115 = (f32[64,32]{0,1:T(8,128)S(1)}, f32[64,32]{0,1:T(8,128)}, u32[]{:S(2)}) copy-start(f32[64,32]{0,1:T(8,128)} %param.59) | copy-start | bytes 24580
  1259.0 181.8 %copy-start.116 = (f32[64,32]{0,1:T(8,128)S(1)}, f32[64,32]{0,1:T(8,128)}, u32[]{:S(2)}) copy-start(f32[64,32]{0,1:T(8,128)} %param.60) | copy-start | bytes 24580
  1259.0 183.4 %copy-start.58 = (f32[35872]{0:T(1024)S(1)}, f32[35872]{0:T(1024)}, u32[]{:S(2)}) copy-start(f32[35872]{0:T(1024)} %param.61) | copy-start | bytes 430468
  1259.0 183.4 %copy-start.84 = (f32[35872]{0:T(1024)S(1)}, f32[35872]{0:T(1024)}, u32[]{:S(2)}) copy-start(f32[35872]{0:T(1024)} %param.62) | copy-start | bytes 430468
  1259.0 183.4 %copy-start.85 = (f32[35872]{0:T(1024)S(1)}, f32[35872]{0:T(1024)}, u32[]{:S(2)}) copy-start(f32[35872]{0:T(1024)} %param.63) | copy-start | bytes 430468
  1259.2 185.0 %copy-start.43 = (f32[1296,64]{0,1:T(8,128)S(1)}, f32[1296,64]{0,1:T(8,128)}, u32[]{:S(2)}) copy-start(f32[1296,64]{0,1:T(8,128)} %param.37) | copy-start | bytes 995332
  1259.2 185.0 %copy-start.61 = (f32[1296,64]{0,1:T(8,128)S(1)}, f32[1296,64]{0,1:T(8,128)}, u32[]{:S(2)}) copy-start(f32[1296,64]{0,1:T(8,128)} %param.38) | copy-start | bytes 995332
  1259.2 185.0 %copy-start.62 = (f32[1296,64]{0,1:T(8,128)S(1)}, f32[1296,64]{0,1:T(8,128)}, u32[]{:S(2)}) copy-start(f32[1296,64]{0,1:T(8,128)} %param.39) | copy-start | bytes 995332
  (131 other events, 1529.7 us)
Sparse Core Ops, SparseCore 0:
  61.1 95.2 all-reduce.6
  159.3 61.0 all-gather.19
  223.1 39.9 all-gather.21
  265.7 73.6 all-gather.23
  342.0 73.1 all-gather.25
  417.9 60.0 all-gather.27
  480.8 39.9 all-gather.29
  523.5 73.6 all-gather.31
  600.0 73.1 all-gather.33
  1156.2 56.2 all-gather.35
  1250.2 56.4 reduce-scatter.3
  1313.8 126.0 all-reduce.8

commit v3 on v2

--- a/solution.py
+++ b/solution.py
@@ -76,6 +76,8 @@
 MESH = pl.DeviceIdType.MESH
 TILE = 256
 PARTS = 4
+SHARED = 640
+GATHER_LAGS = (2, 2, 2, 1)
 
 
 def scatter_kernel(
@@ -448,6 +450,165 @@
     )(*operands)
 
 
+def gather_kernel(
+    lines,
+    qkv_own,
+    proj_own,
+    up_own,
+    down_own,
+    qkv_all,
+    proj_all,
+    up_all,
+    down_all,
+    own_sem,
+    zp_sem,
+    zq_sem,
+    yp_sem,
+    yq_sem,
+    x_sem,
+    core_sem,
+):
+    seq = lax.axis_index("seq")
+    dp = lax.axis_index("dp")
+    core = lax.rem(dp, 2)
+    why = lax.rem(dp // 2, 2)
+    zed = dp // 4
+    core_peer = {"seq": seq, "dp": dp + 1 - 2 * core}
+    x_peer = {"seq": 1 - seq, "dp": dp}
+    y_peer = {"seq": seq, "dp": dp + 2 - 4 * why}
+    z_peers = [
+        {"seq": seq, "dp": lax.rem(zed + step, lines) * 4 + 2 * why + core}
+        for step in range(1, lines)
+    ]
+    pairs = [(qkv_own, qkv_all), (proj_own, proj_all), (up_own, up_all), (down_own, down_all)]
+    firsts = [0, 3, 4, 8]
+    total = 12
+
+    keeps = [
+        pltpu.make_async_copy(own, every.at[zed, why, core], own_sem.at[at])
+        for at, (own, every) in enumerate(pairs)
+    ]
+    for keep in keeps:
+        keep.start()
+    for keep in keeps:
+        keep.wait()
+    barrier = pltpu.get_barrier_semaphore()
+    for peer in [core_peer, x_peer, y_peer] + z_peers:
+        pl.semaphore_signal(barrier, inc=1, device_id=peer, device_id_type=MESH)
+    pl.semaphore_wait(barrier, 2 + lines)
+
+    def places(kind, unit):
+        at = unit - firsts[kind]
+        if kind == 3:
+            return pl.multiple_of(at * 64, 64), 0
+        return 0, pl.multiple_of(at * D, D)
+
+    def span(first, begin, size):
+        return pl.ds(pl.multiple_of(first + begin, 128), size)
+
+    def copies(stage, kind, unit):
+        slot = unit
+        own, every = pairs[kind]
+        row, first = places(kind, unit)
+        rows = pl.ds(row, 64)
+        mine = pl.ds(pl.multiple_of(row + seq * 32, 32), 32)
+        halved = span(first, 0, SHARED)
+        rest = span(first, SHARED, D - SHARED)
+        whole = span(first, 0, D)
+
+        def remote(source, target, sems, peer):
+            return pltpu.make_async_remote_copy(
+                src_ref=source,
+                dst_ref=target,
+                send_sem=sems.at[0],
+                recv_sem=sems.at[1],
+                device_id=peer,
+                device_id_type=MESH,
+            )
+
+        def same(view, sems, peer):
+            return remote(view, view, sems, peer)
+
+        if stage == 0:
+            return [
+                remote(own.at[band, cols], every.at[zed, why, core, band, cols], sems, peer)
+                for band, cols, kinds in ((mine, halved, zp_sem), (rows, rest, zq_sem))
+                for sems, peer in [(kinds.at[slot, at], z_peers[at]) for at in range(lines - 1)]
+            ]
+        if stage == 1:
+            return [
+                same(every.at[:, why, core, mine, halved], yp_sem.at[slot], y_peer),
+                same(every.at[:, why, core, rows, rest], yq_sem.at[slot], y_peer),
+            ]
+        if stage == 2:
+            return [same(every.at[:, :, core, mine, halved], x_sem.at[slot], x_peer)]
+        return [same(every.at[:, :, core, rows, whole], core_sem.at[slot], core_peer)]
+
+    def each_kind(unit, run):
+        ends = firsts[1:] + [total]
+        for kind in range(4):
+
+            @pl.when(jnp.logical_and(unit >= firsts[kind], unit < ends[kind]))
+            def _():
+                run(kind)
+
+    def begin(stage, unit):
+        def run(kind):
+            for copy in copies(stage, kind, unit):
+                copy.start()
+
+        each_kind(unit, run)
+
+    def finish(stage, unit):
+        def run(kind):
+            for copy in copies(stage, kind, unit):
+                copy.wait()
+
+        each_kind(unit, run)
+
+    def turn(at, carry):
+        finish(3, at - sum(GATHER_LAGS))
+        for stage in (3, 2, 1):
+            behind = sum(GATHER_LAGS[:stage])
+            finish(stage - 1, at - behind)
+            begin(stage, at - behind)
+        begin(0, at)
+        return carry
+
+    lax.fori_loop(0, total + sum(GATHER_LAGS), turn, 0)
+
+
+def gather_blocks(qkv_own, proj_own, up_own, down_own, lines, collective_id):
+    owns = (qkv_own, proj_own, up_own, down_own)
+    dma = pltpu.SemaphoreType.DMA
+    outs = pl.pallas_call(
+        functools.partial(gather_kernel, lines),
+        out_shape=[
+            jax.ShapeDtypeStruct((lines, 2, 2) + own.shape, jnp.bfloat16) for own in owns
+        ],
+        in_specs=[pl.BlockSpec(memory_space=pltpu.VMEM)] * 4,
+        out_specs=[pl.BlockSpec(memory_space=pl.ANY)] * 4,
+        scratch_shapes=[
+            dma((4,)),
+            dma((12, lines - 1, 2)),
+            dma((12, lines - 1, 2)),
+            dma((12, 2)),
+            dma((12, 2)),
+            dma((12, 2)),
+            dma((12, 2)),
+        ],
+        compiler_params=pltpu.CompilerParams(
+            collective_id=collective_id,
+            has_side_effects=True,
+            vmem_limit_bytes=56 * 1024 * 1024,
+        ),
+        cost_estimate=pl.CostEstimate(
+            flops=0, bytes_accessed=12 * 4 * lines * 64 * D * 8, transcendentals=0
+        ),
+    )(*owns)
+    return tuple(every.reshape(-1, every.shape[-1]) for every in outs)
+
+
 def layer_forward(stream, modul, weight_set, bias_part, pad_mask):
     w_qkv, w_proj, w_up, w_down = weight_set
     images, tok_rows, _ = stream.shape
@@ -567,22 +728,32 @@
     return lax.all_gather(shard.astype(jnp.bfloat16), "dp", axis=0, tiled=True)
 
 
-def reduce_rows(partial):
-    owned = lax.psum_scatter(
-        partial.astype(jnp.bfloat16), "dp", scatter_dimension=0, tiled=True
-    )
-    return lax.psum(owned, "seq").astype(jnp.float32)
-
-
-def weight_sums(factors):
+def kernels_fit():
     dp_parts = lax.axis_size("dp")
-    by_kernel = (
+    return (
         lax.axis_size("seq") == 2
         and dp_parts % 4 == 0
         and D // dp_parts == 64
         and FF // dp_parts == PARTS * 64
     )
-    if not by_kernel:
+
+
+def gather_layer(shards, collective_id):
+    if kernels_fit():
+        return gather_blocks(*shards, lax.axis_size("dp") // 4, collective_id)
+    return tuple(gather_rows(shard) for shard in shards)
+
+
+def reduce_rows(partial):
+    owned = lax.psum_scatter(
+        partial.astype(jnp.bfloat16), "dp", scatter_dimension=0, tiled=True
+    )
+    return lax.psum(owned, "seq").astype(jnp.float32)
+
+
+def weight_sums(factors):
+    dp_parts = lax.axis_size("dp")
+    if not kernels_fit():
         return [
             (
                 reduce_rows(matdot(a_one.T, d_qkv)),
@@ -670,16 +841,27 @@
     )
     packed = lax.all_to_all(packed, "seq", split_axis=0, concat_axis=1, tiled=True)
     tok_rows = packed.shape[1]
-    latents, noise_target, keep_rows = (
-        packed[:, :, :PATCH_IN],
-        packed[:, :, PATCH_IN : 2 * PATCH_IN],
-        packed[:, :, 2 * PATCH_IN],
-    )
+    shards = [
+        tuple(
+            weight[at].astype(jnp.bfloat16)
+            for weight in (qkv_weight, proj_weight, up_weight, down_weight)
+        )
+        for at in range(LAYERS)
+    ]
+    weights_kept = [gather_layer(shards[0], 2)]
     ids = lax.all_gather(jnp.stack([labels, timesteps]), "dp", axis=1, tiled=True)
     small = jnp.concatenate(
         [embed_rows[: PATCH_IN + FREQ], head_weight.T], axis=0
     ).astype(jnp.bfloat16)
     small = lax.all_gather(small, "dp", axis=1, tiled=True)
+    ids, small, packed, weights_kept[0] = lax.optimization_barrier(
+        (ids, small, packed, weights_kept[0])
+    )
+    latents, noise_target, keep_rows = (
+        packed[:, :, :PATCH_IN],
+        packed[:, :, PATCH_IN : 2 * PATCH_IN],
+        packed[:, :, 2 * PATCH_IN],
+    )
     patch_part = small[:PATCH_IN]
     freq_part = small[PATCH_IN : PATCH_IN + FREQ]
     head_rows = small[PATCH_IN + FREQ :]
@@ -700,9 +882,10 @@
     plane_act = lax.dynamic_index_in_dim(
         cond_act.reshape(dp_parts, seq_parts, images, own_cols), seq_at, 1, keepdims=False
     ).reshape(dp_parts * images, own_cols)
-    modulation = lax.psum_scatter(
-        matdot(plane_act, cond_own), "dp", scatter_dimension=0, tiled=True
-    )
+    mod_partial = matdot(plane_act, cond_own)
+    mod_partial, shards[1] = lax.optimization_barrier((mod_partial, shards[1]))
+    weights_kept.append(gather_layer(shards[1], 3))
+    modulation = lax.psum_scatter(mod_partial, "dp", scatter_dimension=0, tiled=True)
     modulation = modulation + all_biases[3 * D : bias_base]
 
     position = position_table(jnp.arange(tok_rows, dtype=jnp.int32), D, GRID)
@@ -715,25 +898,20 @@
         for at in range(LAYERS)
     ]
     inputs_kept = []
-    weights_kept = []
     saved_kept = []
     for at in range(LAYERS):
-        weight_set = (
-            gather_rows(qkv_weight[at]),
-            gather_rows(proj_weight[at]),
-            gather_rows(up_weight[at]),
-            gather_rows(down_weight[at]),
-        )
-        weights_kept.append(weight_set)
         inputs_kept.append(stream)
         stream, saved = layer_forward(
             stream,
             modulation[:, 6 * at * D : 6 * (at + 1) * D],
-            weight_set,
+            weights_kept[at],
             layer_bias[at],
             keep_rows,
         )
         saved_kept.append(saved)
+        if at == 0:
+            stream, time_own = lax.optimization_barrier((stream, time_own))
+            time_full = lax.all_gather(time_own, "dp", axis=1, tiled=True)
     final_at = 6 * LAYERS * D
     final_shift = modulation[:, final_at : final_at + D]
     final_scale = modulation[:, final_at + D : final_at + 2 * D]
@@ -770,51 +948,49 @@
     d_mod_own = jnp.concatenate(modul_grads + [d_final_shift, d_final_scale], axis=1).astype(
         jnp.bfloat16
     )
+    d_patch = d_stream.astype(jnp.bfloat16).reshape(images * tok_rows, D)
+    flat = jnp.concatenate(
+        [column_sum(d_patch), jnp.zeros((2 * D,), jnp.float32), column_sum(d_mod_own)]
+        + layer_bias_grads
+        + [column_sum(d_head), loss_part[None], count_part[None]]
+        + [matdot(flat_in.T, d_patch).reshape(-1), g_head.reshape(-1)]
+    )
+    flat, d_mod_own, layer_factors = lax.optimization_barrier((flat, d_mod_own, layer_factors))
+    flat = lax.psum(flat, ("seq", "dp"))
     d_modulation = lax.all_gather(d_mod_own, ("dp", "seq"), axis=0, tiled=True)
+    layer_sums = weight_sums(layer_factors)
     d_cond_act = lax.dot_general(
         d_modulation, cond_own, (((1,), (1,)), ((), ())), preferred_element_type=jnp.float32
     )
     _, silu_back = jax.vjp(jax.nn.silu, condition)
     d_condition = silu_back(d_cond_act)[0]
-    d_time = d_condition.astype(jnp.bfloat16)
-    d_time_hidden = lax.psum_scatter(
-        lax.dot_general(
-            d_time, time_own, (((1,), (1,)), ((), ())), preferred_element_type=jnp.float32
-        ),
-        "dp",
-        scatter_dimension=1,
-        tiled=True,
-    )
-    time_pre_own = lax.dynamic_slice(time_pre, (0, dp_at * own_cols), (everyone, own_cols))
-    _, time_back = jax.vjp(jax.nn.silu, time_pre_own)
+    d_time_own = d_condition.astype(jnp.bfloat16)
+    d_time = lax.all_gather(d_time_own, "dp", axis=1, tiled=True)
+    d_time_hidden = lax.dot_general(
+        d_time, time_full, (((1,), (1,)), ((), ())), preferred_element_type=jnp.float32
+    )
+    _, time_back = jax.vjp(jax.nn.silu, time_pre)
     d_time_pre = time_back(d_time_hidden)[0].astype(jnp.bfloat16)
-    d_patch = d_stream.astype(jnp.bfloat16).reshape(images * tok_rows, D)
-    g_patch = matdot(flat_in.T, d_patch)
+    own_place = dp_at * own_cols
     s_cond = matdot(cond_act.T, d_modulation)
     s_table = jnp.dot(onehot.T, d_condition, precision=lax.Precision.HIGHEST)
-    g_time = matdot(time_hidden.T, d_time)
-    g_freq = matdot(features.T, d_time_pre)
-
-    lead_flag = (seq_at == 0).astype(jnp.float32)
-    own_place = dp_at * own_cols
-    first_time_bias = lax.dynamic_update_slice(
-        jnp.zeros((D,), jnp.float32), column_sum(d_time_pre) * lead_flag, (own_place,)
-    )
-    second_time_bias = lax.dynamic_update_slice(
-        jnp.zeros((D,), jnp.float32), column_sum(d_time) * lead_flag, (own_place,)
+    g_time = matdot(time_hidden.T, d_time_own)
+    g_freq = matdot(
+        features.T, lax.dynamic_slice(d_time_pre, (0, own_place), (everyone, own_cols))
     )
     bias_grad = jnp.concatenate(
-        [column_sum(d_patch), first_time_bias, second_time_bias, column_sum(d_mod_own)]
-        + layer_bias_grads
-        + [column_sum(d_head)]
-    )
-    bias_grad, g_patch, g_head, loss_sum, loss_count = lax.psum(
-        (bias_grad, g_patch, g_head, loss_part, count_part), ("seq", "dp")
-    )
-    s_patch = lax.dynamic_slice(g_patch, (0, own_place), (PATCH_IN, own_cols))
-    s_head = lax.dynamic_slice(g_head, (own_place, 0), (own_cols, OUT_CH))
+        [flat[:D], column_sum(d_time_pre), column_sum(d_time), flat[3 * D : NBIAS]]
+    )
+    loss_sum, loss_count = flat[NBIAS], flat[NBIAS + 1]
+    patch_at = NBIAS + 2
+    head_at = patch_at + PATCH_IN * D
+    s_patch = lax.dynamic_slice(
+        flat[patch_at:head_at].reshape(PATCH_IN, D), (0, own_place), (PATCH_IN, own_cols)
+    )
+    s_head = lax.dynamic_slice(
+        flat[head_at:].reshape(D, OUT_CH), (own_place, 0), (own_cols, OUT_CH)
+    )
     s_embed = jnp.concatenate([s_patch, g_freq, g_time], axis=0)
-    layer_sums = weight_sums(layer_factors)
     s_qkv = jnp.stack([layer_sums[at][0] for at in range(LAYERS)])
     s_proj = jnp.stack([layer_sums[at][1] for at in range(LAYERS)])
     s_up = jnp.stack([layer_sums[at][2] for at in range(LAYERS)])

time: 1460 us -> 1060 us (0.73)
  waiting for transfers between devices: 603 us -> 0.11 us
  Pallas kernels: 255 us -> 548 us
  matrix products: 210 us -> 161 us
  blocking collectives: 83.4 us -> 64.2 us
  other arithmetic: 95.5 us -> 80.6 us
    all_gather x8 -> x1, waiting for transfers between devices: 351 us -> 0.02 us  [body(): time_full = lax.all_gather(time_own, 'dp', axis=1, tiled=True)]
    pallas_call x0 -> x2, Pallas kernels: none -> 276 us  [gather_blocks(): pl.pallas_call(functools.partial(gather_kernel, lines), out_shape=[jax.Sh...]
    psum x1, waiting for transfers between devices: 131 us -> 0.01 us  [body(): flat = lax.psum(flat, ('seq', 'dp'))]
    unnamed x14 -> x5, waiting for transfers between devices: 121 us -> 0.09 us
    dot_general x27, matrix products: 168 us -> 124 us  [matdot(): return jnp.dot(left, right, preferred_element_type=jnp.float32)]
    psum x1 -> x0, blocking collectives: 40.8 us -> none  [body(): lax.psum((bias_grad, g_patch, g_head, loss_part, count_part), ('seq', 'dp'))]
    convert_element_type x6 -> x4, local copies, waits for them, and re-layouts: 37 us -> 12.1 us  [layer_backward(): jnp.stack([d_queries, d_keys, d_values], axis=2).astype(jnp.bfloat16)]
    all_gather x0 -> x1, blocking collectives: none -> 22 us  [body(): d_time = lax.all_gather(d_time_own, 'dp', axis=1, tiled=True)]
  transfers between devices with their start and end apart: 13 -> 5, of which waited for: 10 -> 0; matrix products, arithmetic and copies ran while one was open for 16% -> 9% of each run, Pallas kernels for 0% -> 52%
where the time goes in v3:
time: 1060 us; the launch traced here: 1050 us
  Pallas kernels  548 us (52%)
  local copies, waits for them, and re-layouts  176 us (17%)
  matrix products  161 us (15%)
  other arithmetic  80.6 us (8%)
  blocking collectives  64.2 us (6%)
  between operations  17.6 us (2%)
    pallas_call x2, Pallas kernels, gather_blocks(): pl.pallas_call(functools.partial(gather_kernel, lines), out_shape=[jax.Sh...  276 us
    pallas_call x1, Pallas kernels, scatter_sums(): pl.pallas_call(functools.partial(scatter_kernel, per_layer, total, lines)...  272 us
    dot_general x27, matrix products, matdot(): return jnp.dot(left, right, preferred_element_type=jnp.float32)  124 us
    unnamed x343, local copies, waits for them, and re-layouts  60.7 us
    all_gather x1, blocking collectives, body(): small = lax.all_gather(small, 'dp', axis=1, tiled=True)  24.6 us
    all_gather x1, blocking collectives, body(): d_time = lax.all_gather(d_time_own, 'dp', axis=1, tiled=True)  22 us
  transfers between devices with their start and end apart: 5, of which 0 were waited for; matrix products, arithmetic and copies ran while one was open for 9% of the time, Pallas kernels for 52%

profile of v3, /device:TPU:0, one launch (start us, length us, event | category | flops | bytes accessed | tf_op | source)
XLA Modules:
  0.0 1051.5 jit_solution(12639049462895076545)
XLA Ops:
  22.6 24.6 %all_gather.16 = bf16[304,1024]{0,1:T(8,128)(2,1)S(1)} all-gather(bf16[304,64]{0,1:T(8,128)(2,1)S(1)} %pad_maximum_fusion.3), channel_id=1, replica_groups=mesh['seq'=2,'dp'=16] {'dp'}, dimensions={1}, use_global_device_ids=true | all-gather | bytes 661504 | tf_op jit(solution)/shard_map/all_gather | solution.py:856
  49.9 17.6 %all-gather = s32[16,4,2]{1,2,0:T(2,128)S(1)} all-gather(s32[1,4,2]{1,2,0:T(2,128)S(1)} %add_bitcast_fusion), channel_id=1, replica_groups=mesh['seq'=2,'dp'=16] {'dp'}, dimensions={0}, use_global_device_ids=true | all-gather | bytes 544 | tf_op jit(solution)/shard_map/all_gather | solution.py:852
  68.9 123.4 %shard_map.527 = (bf16[4,2,2,64,3072]{4,3,2,1,0:T(8,128)(2,1)}, bf16[4,2,2,64,1024]{4,3,2,1,0:T(8,128)(2,1)}, bf16[4,2,2,64,4096]{4,3,2,1,0:T(8,128)(2,1)}, bf16[4,2,2,256,1024]{4,3,2,1,0:T(8,128)(2,1)}) custom-call(bf16[64,3072]{1,0:T(8,128)(2,1)} %get-tuple-element.267.qkv_own, bf16[64,1024]{1,0:T(8,128)(2,1)} %get-tuple-element.271.proj_own, ...), custom_call_target="tpu_custom_call" | custom-call | bytes 100663296 | tf_op jit(solution)/shard_map/pallas_call | solution.py:584
  205.6 152.4 %shard_map.528 = (bf16[4,2,2,64,3072]{4,3,2,1,0:T(8,128)(2,1)}, bf16[4,2,2,64,1024]{4,3,2,1,0:T(8,128)(2,1)}, bf16[4,2,2,64,4096]{4,3,2,1,0:T(8,128)(2,1)}, bf16[4,2,2,256,1024]{4,3,2,1,0:T(8,128)(2,1)}) custom-call(bf16[64,3072]{1,0:T(8,128)(2,1)} %get-tuple-element.82.qkv_own, bf16[64,1024]{1,0:T(8,128)(2,1)} %get-tuple-element.83.proj_own, ...), custom_call_target="tpu_custom_call" | custom-call | bytes 100663296 | tf_op jit(solution)/shard_map/pallas_call | solution.py:584
  360.9 7.5 add_convert_fusion.1
  368.4 8.6 reshape.571
  377.0 6.0 fusion.151
  410.6 8.5 multiply_convert_fusion.3
  428.0 7.7 add_convert_fusion
  435.7 8.6 reshape.572
  444.3 6.0 fusion.150
  459.1 5.5 fusion.158
  480.1 9.0 multiply_convert_fusion.2
  505.3 16.6 %convert_reduce_fusion = (f32[4096]{0:T(1024)}, bf16[512,4096]{1,0:T(8,128)(2,1)}) fusion(f32[512,4096]{1,0:T(8,128)} %get-tuple-element.329, f32[4096]{0:T(1024)S(1)} %get-tuple-element.278, bf16[512,1024]{1,0:T(8,128)(2,1)S(1)} %bitcast.358, bf16[4096,1024]{1,0:T(8,128)(2,1)} %bitcast.397), kind=kOutput, calls=%fused_computation.20 | convolution fusion | flops 4343197696 | bytes 22052864 | tf_op jit(solution)/shard_map/dot_general | solution.py:35
  521.9 6.8 multiply_reduce_fusion.13
  542.7 5.6 multiply_reduce_fusion.1
  567.7 14.5 %convert_reduce_fusion.1 = (f32[4096]{0:T(1024)}, bf16[512,4096]{1,0:T(8,128)(2,1)S(1)}) fusion(f32[512,4096]{1,0:T(8,128)} %get-tuple-element.325, f32[4096]{0:T(1024)S(1)} %copy-done.124, bf16[512,1024]{1,0:T(8,128)(2,1)S(1)} %bitcast.368, bf16[4096,1024]{1,0:T(8,128)(2,1)} %bitcast.387), kind=kOutput, calls=%fused_computation.21 | convolution fusion | flops 4343197696 | bytes 22052864 | tf_op jit(solution)/shard_map/dot_general | solution.py:35
  582.2 6.0 multiply_reduce_fusion.11
  631.9 7.5 multiply_reduce_fusion.9
  657.3 11.7 %concatenate.36 = f32[85026]{0:T(1024)} concatenate(f32[1024]{0:T(1024)S(1)} %copy-done.115, f32[2048]{0:T(1024)S(1)} %broadcast_in_dim.60, f32[14336]{0:T(1024)S(1)} %convert_reduce_fusion.11, f32[3072]{0:T(1024)S(1)} %copy-done.101, f32[1024]{0:T(1024)S(1)} %get-tuple-element.255, f32[4096]{0:T(1024)S(1)} %copy-done.122, f32[1024]{0:T(1024)S(1)} %get-tuple-element.219, ...), dimensions={0} | concatenate | bytes 680208 | tf_op jit(solution)/shard_map/concatenate | solution.py:952
  679.5 271.9 %shard_map.529 = f32[24,4,64,256]{3,2,1,0:T(8,128)} custom-call(bf16[512,1024]{1,0:T(8,128)(2,1)} %copy.250.refs_0_, bf16[512,1024]{1,0:T(8,128)(2,1)} %copy-done.56, bf16[512,1024]{1,0:T(8,128)(2,1)} %copy-done.63, bf16[512,4096]{1,0:T(8,128)(2,1)} %copy-done.134, bf16[512,1024]{1,0:T(8,128)(2,1)} %bitcast.361, bf16[512,3072]{1,0:T(8,128)(2,1)} %copy.251.refs_5_, ...), custom_call_target="tpu_custom_call" | custom-call | flops 25769803776 | bytes 100663296 | tf_op jit(solution)/shard_map/pallas_call | solution.py:436
  979.1 6.2 multiply_subtract_fusion.1
  1007.6 22.0 %all_gather.18 = bf16[64,1024]{0,1:T(8,128)(2,1)S(1)} all-gather(bf16[64,64]{0,1:T(8,128)(2,1)S(1)} %copy.249), channel_id=1, replica_groups=mesh['seq'=2,'dp'=16] {'dp'}, dimensions={1}, use_global_device_ids=true | all-gather | bytes 139264 | tf_op jit(solution)/shard_map/all_gather | solution.py:968
  1031.4 8.5 multiply_subtract_fusion
  (568 shorter events, 271.3 us)
Async XLA Ops:
  9.3 183.0 %all-to-all-start = ((f32[4,128,33]{1,2,0:T(8,128)}), f32[4,128,33]{1,2,0:T(8,128)S(1)}, u32[]{:S(2)}, u32[]{:S(2)}) async-start(f32[4,128,33]{1,2,0:T(8,128)} %pad_maximum_fusion.2), calls=%async_computation | async-start | bytes 163840 | tf_op jit(solution)/shard_map/all_to_all | solution.py:842
  13.5 344.5 %all-reduce.7.cloned.1.call-start = ((), (), s32[]{:S(2)}) async-start(), calls=%async_computation.4 | async-start | bytes 3670016
  15.8 392.8 %copy-start.123 = (f32[4096]{0:T(1024)}, f32[4096]{0:T(1024)S(1)}, u32[]{:S(2)}) copy-start(f32[4096]{0:T(1024)S(1)} %get-tuple-element.279) | copy-start | bytes 49156
  20.6 26.6 %copy-start.128 = (s32[4]{0:T(128)S(1)}, s32[4]{0:T(128)}, u32[]{:S(2)}) copy-start(s32[4]{0:T(128)} %param.36) | copy-start | bytes 52
  20.6 26.6 %copy-start.129 = (s32[4]{0:T(128)S(1)}, s32[4]{0:T(128)}, u32[]{:S(2)}) copy-start(s32[4]{0:T(128)} %param.35) | copy-start | bytes 52
  21.6 46.0 %copy-start.68 = (f32[35872]{0:T(1024)S(1)}, f32[35872]{0:T(1024)}, u32[]{:S(2)}) copy-start(f32[35872]{0:T(1024)} %param.61) | copy-start | bytes 430468
  21.6 46.1 %copy-start.133 = (u32[32]{0:T(128)S(1)}, u32[32]{0:T(128)}, u32[]{:S(2)}) copy-start(u32[32]{0:T(128)} %constant.133) | copy-start | bytes 388
  47.2 152.1 %copy-start.38 = (bf16[304,1024]{0,1:T(8,128)(2,1)}, bf16[304,1024]{0,1:T(8,128)(2,1)S(1)}, u32[]{:S(2)}) copy-start(bf16[304,1024]{0,1:T(8,128)(2,1)S(1)} %all_gather.16) | copy-start | bytes 1867780
  49.9 144.5 %copy-start.79 = (f32[1001,64]{0,1:T(8,128)S(1)}, f32[1001,64]{0,1:T(8,128)}, u32[]{:S(2)}) copy-start(f32[1001,64]{0,1:T(8,128)} %param.40) | copy-start | bytes 768772
  192.4 306.3 %copy-start.76 = (f32[2,256,33]{1,0,2:T(2,128)}, f32[2,256,33]{1,0,2:T(2,128)S(1)}, u32[]{:S(2)}) copy-start(f32[2,256,33]{1,0,2:T(2,128)S(1)} %all_to_all.16) | copy-start | bytes 202756
  198.9 797.4 %all-reduce.5.cloned.1.call-start = ((), (), s32[]{:S(2)}) async-start(), calls=%async_computation.1 | async-start | bytes 688128 | tf_op jit(solution)/shard_map/psum | solution.py:959
  199.3 224.4 %copy-start.5 = (f32[256,1024]{1,0:T(8,128)}, f32[256,1024]{1,0:T(8,128)S(1)}, u32[]{:S(2)}) copy-start(f32[256,1024]{1,0:T(8,128)S(1)} %pad_maximum_fusion) | copy-start | bytes 3145732
  202.1 203.1 %copy-start = (f32[512,1024]{1,0:T(8,128)}, f32[512,1024]{1,0:T(8,128)S(1)}, u32[]{:S(2)}) copy-start(f32[512,1024]{1,0:T(8,128)S(1)} %get-tuple-element.320) | copy-start | bytes 6291460
  202.7 155.3 %slice-start.8 = ((f32[35872]{0:T(1024)}), f32[14336]{0:T(1024)S(1)}, s32[]{:S(2)}) async-start(f32[35872]{0:T(1024)} %param.61), calls=%async_computation.13 | async-start | bytes 114688 | tf_op jit(solution)/shard_map/slice | solution.py:889
  203.2 154.8 %copy-start.110 = (f32[2,256]{1,0:T(2,128)}, f32[2,256]{1,0:T(2,128)S(1)}, u32[]{:S(2)}) copy-start(f32[2,256]{1,0:T(2,128)S(1)} %add.564) | copy-start | bytes 6148
  359.2 48.8 %copy-start.82 = (f32[2,1024]{1,0:T(2,128)}, f32[2,1024]{1,0:T(2,128)S(1)}, u32[]{:S(2)}) copy-start(f32[2,1024]{1,0:T(2,128)S(1)} %get-tuple-element.291) | copy-start | bytes 24580
  359.2 64.6 %copy-start.91 = (f32[2,1024]{1,0:T(2,128)}, f32[2,1024]{1,0:T(2,128)S(1)}, u32[]{:S(2)}) copy-start(f32[2,1024]{1,0:T(2,128)S(1)} %get-tuple-element.293) | copy-start | bytes 24580
  669.0 331.7 %all-gather.7.cloned.1.call-start = ((), (), s32[]{:S(2)}) async-start(), calls=%async_computation.3 | async-start | bytes 1892352 | tf_op jit(solution)/shard_map/all_gather | solution.py:960
  679.4 360.5 %all-gather.5.cloned.1.call-start = ((), (), s32[]{:S(2)}) async-start(), calls=%async_computation.2 | async-start | bytes 2228224 | tf_op jit(solution)/shard_map/all_gather | solution.py:914
  1004.6 25.1 %copy-start.73 = (bf16[64,1024]{1,0:T(8,128)(2,1)S(1)}, bf16[64,1024]{1,0:T(8,128)(2,1)}, u32[]{:S(2)}) copy-start(bf16[64,1024]{1,0:T(8,128)(2,1)} %copy-done.72) | copy-start | bytes 393220
  1004.6 25.3 %copy-start.80 = (f32[1001,64]{0,1:T(8,128)S(1)}, f32[1001,64]{0,1:T(8,128)}, u32[]{:S(2)}) copy-start(f32[1001,64]{0,1:T(8,128)} %param.40) | copy-start | bytes 768772
  1004.7 25.3 %copy-start.127 = (s32[64]{0:T(128)S(1)}, s32[64]{0:T(128)}, u32[]{:S(2)}) copy-start(s32[64]{0:T(128)} %copy-done.126) | copy-start | bytes 772
  1004.7 25.3 %copy-start.130 = (f32[1001,64]{0,1:T(8,128)S(1)}, f32[1001,64]{0,1:T(8,128)}, u32[]{:S(2)}) copy-start(f32[1001,64]{0,1:T(8,128)} %param.41) | copy-start | bytes 768772
  1004.7 25.3 %copy-start.131 = (f32[1001,64]{0,1:T(8,128)S(1)}, f32[1001,64]{0,1:T(8,128)}, u32[]{:S(2)}) copy-start(f32[1001,64]{0,1:T(8,128)} %param.42) | copy-start | bytes 768772
  (139 other events, 707.1 us)
Sparse Core Ops, SparseCore 0:
  199.1 133.4 all-reduce.6
  669.1 135.1 all-reduce.4
  808.2 64.6 all-gather.6
  974.9 42.5 all-gather.4

commit v4 on v3

--- a/solution.py
+++ b/solution.py
@@ -69,15 +69,16 @@
     return jnp.sum(grad_bf.astype(jnp.float32), axis=0)
 
 
-def split_six(modul):
-    return [modul[:, piece * D : (piece + 1) * D] for piece in range(6)]
-
-
 MESH = pl.DeviceIdType.MESH
 TILE = 256
 PARTS = 4
 SHARED = 640
 GATHER_LAGS = (2, 2, 2, 1)
+HALF = 512
+GELU_IN = math.sqrt(2.0 / math.pi)
+GELU_CUBE = 0.044715
+FORWARD_STEPS = 26
+BACKWARD_STEPS = 27
 
 
 def scatter_kernel(
@@ -450,24 +451,661 @@
     )(*operands)
 
 
-def gather_kernel(
-    lines,
-    qkv_own,
-    proj_own,
-    up_own,
-    down_own,
-    qkv_all,
-    proj_all,
-    up_all,
-    down_all,
-    own_sem,
-    zp_sem,
-    zq_sem,
-    yp_sem,
-    yq_sem,
-    x_sem,
-    core_sem,
-):
+def dot_nn(left, right):
+    return jnp.dot(left, right, preferred_element_type=jnp.float32)
+
+
+def dot_nt(left, right):
+    return lax.dot_general(
+        left, right, (((1,), (1,)), ((), ())), preferred_element_type=jnp.float32
+    )
+
+
+def dot_tn(left, right):
+    return lax.dot_general(
+        left, right, (((0,), (0,)), ((), ())), preferred_element_type=jnp.float32
+    )
+
+
+def column_tile(at, size=HALF):
+    return pl.ds(pl.multiple_of(at * size, size), size)
+
+
+def normalized(rows):
+    centered = rows - jnp.mean(rows, axis=-1, keepdims=True)
+    variance = jnp.mean(centered * centered, axis=-1, keepdims=True)
+    inverse = lax.rsqrt(variance + 1e-06)
+    return centered * inverse, inverse
+
+
+def head_probs(queries, keys, keep):
+    scores = jnp.where(keep > 0, dot_nt(queries, keys), -1000000000.0)
+    raised = jnp.exp(scores - jnp.max(scores, axis=-1, keepdims=True))
+    return raised * (1.0 / jnp.sum(raised, axis=-1, keepdims=True))
+
+
+def within(at, first, size):
+    return jnp.logical_and(at >= first, at < first + size)
+
+
+def forward_pieces(refs, mod_at):
+    (
+        x_ref,
+        mod_ref,
+        bias_ref,
+        keep_ref,
+        w_qkv,
+        w_proj,
+        w_up,
+        w_down,
+        a_one_out,
+        qkv_out,
+        merged_out,
+        attn_out,
+        x_one_out,
+        a_two_out,
+        pre_out,
+        act_out,
+        down_out,
+        x_two_out,
+        a_buf,
+        qkv_buf,
+        merged_buf,
+        attn_buf,
+        x_one_buf,
+        a_two_buf,
+        pre_buf,
+        act_buf,
+        down_buf,
+        x_two_buf,
+        wide_buf,
+        tall_buf,
+        load_sem,
+        tile_sem,
+        save_sem,
+    ) = refs
+    images, toks = keep_ref.shape
+    bf = jnp.bfloat16
+
+    def save(at, source, target):
+        return pltpu.make_async_copy(source, target, save_sem.at[at])
+
+    saves = [
+        save(at, *pair)
+        for at, pair in enumerate(
+            [
+                (a_buf, a_one_out),
+                (qkv_buf, qkv_out),
+                (merged_buf, merged_out),
+                (attn_buf, attn_out),
+                (x_one_buf, x_one_out),
+                (a_two_buf, a_two_out),
+                (down_buf, down_out),
+                (x_two_buf, x_two_out),
+            ]
+        )
+    ]
+
+    def wide_load(source, tile, slot):
+        return pltpu.make_async_copy(
+            source.at[:, :, :, :, column_tile(tile)], wide_buf.at[slot], load_sem.at[0, slot]
+        )
+
+    def tall_load(tile, slot):
+        return pltpu.make_async_copy(
+            w_down.at[tile // 2, lax.rem(tile, 2)], tall_buf.at[slot], load_sem.at[1, slot]
+        )
+
+    def tile_saves(tile, slot):
+        return [
+            pltpu.make_async_copy(
+                pre_buf.at[slot], pre_out.at[:, column_tile(tile)], tile_sem.at[0, slot]
+            ),
+            pltpu.make_async_copy(
+                act_buf.at[slot], act_out.at[:, column_tile(tile)], tile_sem.at[1, slot]
+            ),
+        ]
+
+    def wide_tile(slot):
+        return wide_buf[slot].reshape(D, HALF)
+
+    def tall_tile(slot):
+        return tall_buf[slot].reshape(HALF, D)
+
+    def loads(at, run):
+        slot = lax.rem(at, 2)
+
+        @pl.when(within(at, 1, 6))
+        def _():
+            run(wide_load(w_qkv, at - 1, slot))
+
+        @pl.when(within(at, 15, 2))
+        def _():
+            run(wide_load(w_proj, at - 15, slot))
+
+        @pl.when(within(at, 18, 8))
+        def _():
+            run(wide_load(w_up, at - 18, slot))
+            run(tall_load(at - 18, slot))
+
+    def modulated(source, target, piece):
+        def rows_of(block, carry):
+            image = block // 4
+            rows = pl.ds(pl.multiple_of(block * 64, 64), 64)
+            shift = mod_ref[pl.ds(mod_at + 2 * piece + image, 1), :]
+            scale = mod_ref[pl.ds(mod_at + 2 * piece + 2 + image, 1), :]
+            unit, _ = normalized(source[rows, :])
+            target[rows, :] = (unit * (1.0 + scale) + shift).astype(bf)
+            return carry
+
+        lax.fori_loop(0, images * toks // 64, rows_of, 0)
+
+    def attend(image, pair):
+        rows = pl.ds(pl.multiple_of(image * toks, toks), toks)
+        low = lax.broadcasted_iota(jnp.int32, (toks, 128), 1) < 64
+        queries = qkv_buf[rows, column_tile(pair, 128)] * jnp.asarray(0.125, bf)
+        keys = qkv_buf[rows, column_tile(8 + pair, 128)]
+        values = qkv_buf[rows, column_tile(16 + pair, 128)]
+        keep = keep_ref[pl.ds(image, 1), :]
+        zero = jnp.zeros_like(queries)
+        total = jnp.zeros((toks, 128), jnp.float32)
+        for own in (low, jnp.logical_not(low)):
+            probs = head_probs(jnp.where(own, queries, zero), keys, keep)
+            total = total + dot_nn(probs.astype(bf), jnp.where(own, values, zero))
+        merged_buf[rows, column_tile(pair, 128)] = total.astype(bf)
+
+    def step(at):
+        slot = lax.rem(at, 2)
+        loads(at + 1, lambda copy: copy.start())
+        loads(at, lambda copy: copy.wait())
+
+        @pl.when(at == 0)
+        def _():
+            modulated(x_ref, a_buf, 0)
+            saves[0].start()
+
+        @pl.when(within(at, 1, 6))
+        def _():
+            cols = column_tile(at - 1)
+            for image in range(images):
+                rows = pl.ds(image * toks, toks)
+                qkv_buf[rows, cols] = (
+                    dot_nn(a_buf[rows, :], wide_tile(slot)) + bias_ref[:, cols]
+                ).astype(bf)
+
+        @pl.when(at == 7)
+        def _():
+            saves[1].start()
+
+        @pl.when(within(at, 7, 8))
+        def _():
+            for turn in range(2):
+                item = (at - 7) * 2 + turn
+                attend(item // 8, lax.rem(item, 8))
+
+        @pl.when(within(at, 15, 2))
+        def _():
+            cols = column_tile(at - 15)
+            for image in range(images):
+                rows = pl.ds(image * toks, toks)
+                attn = dot_nn(merged_buf[rows, :], wide_tile(slot)) + bias_ref[
+                    :, column_tile(at - 15 + 6)
+                ]
+                attn_buf[rows, cols] = attn
+                gate = mod_ref[mod_at + 4 + image : mod_at + 5 + image, cols]
+                x_one_buf[rows, cols] = x_ref[rows, cols] + gate * attn
+
+        @pl.when(at == 17)
+        def _():
+            for which in (2, 3, 4):
+                saves[which].start()
+            modulated(x_one_buf, a_two_buf, 3)
+            saves[5].start()
+
+        @pl.when(within(at, 18, 8))
+        def _():
+            tile = at - 18
+
+            @pl.when(tile >= 2)
+            def _():
+                for copy in tile_saves(tile - 2, slot):
+                    copy.wait()
+
+            for image in range(images):
+                rows = pl.ds(image * toks, toks)
+                pre = dot_nn(a_two_buf[rows, :], wide_tile(slot)) + bias_ref[:, column_tile(tile + 8)]
+                pre_buf[slot, rows, :] = pre
+                inner = jnp.tanh(GELU_IN * (pre + GELU_CUBE * pre * pre * pre))
+                active = (0.5 * pre * (1.0 + inner)).astype(bf)
+                act_buf[slot, rows, :] = active
+                part = dot_nn(active, tall_tile(slot))
+
+                @pl.when(tile == 0)
+                def _():
+                    down_buf[rows, :] = part + bias_ref[:, 8 * D : 9 * D]
+
+                @pl.when(tile > 0)
+                def _():
+                    down_buf[rows, :] += part
+
+            for copy in tile_saves(tile, slot):
+                copy.start()
+
+        @pl.when(at == FORWARD_STEPS - 1)
+        def _():
+            for image in range(images):
+                rows = pl.ds(image * toks, toks)
+                gate = mod_ref[mod_at + 10 + image : mod_at + 11 + image, :]
+                x_two_buf[rows, :] = x_one_buf[rows, :] + gate * down_buf[rows, :]
+            saves[6].start()
+            saves[7].start()
+
+    def finish():
+        for tile in (6, 7):
+            for copy in tile_saves(tile, tile % 2):
+                copy.wait()
+        for copy in saves:
+            copy.wait()
+
+    return step, finish
+
+
+FORWARD_OUTS = [
+    (D, jnp.bfloat16),
+    (3 * D, jnp.bfloat16),
+    (D, jnp.bfloat16),
+    (D, jnp.float32),
+    (D, jnp.float32),
+    (D, jnp.bfloat16),
+    (FF, jnp.float32),
+    (FF, jnp.bfloat16),
+    (D, jnp.float32),
+    (D, jnp.float32),
+]
+
+
+def forward_scratch(toks):
+    bf, f32 = jnp.bfloat16, jnp.float32
+    return [
+        pltpu.VMEM((toks, D), bf),
+        pltpu.VMEM((toks, 3 * D), bf),
+        pltpu.VMEM((toks, D), bf),
+        pltpu.VMEM((toks, D), f32),
+        pltpu.VMEM((toks, D), f32),
+        pltpu.VMEM((toks, D), bf),
+        pltpu.VMEM((2, toks, HALF), f32),
+        pltpu.VMEM((2, toks, HALF), bf),
+        pltpu.VMEM((toks, D), f32),
+        pltpu.VMEM((toks, D), f32),
+        pltpu.VMEM((2, 4, 2, 2, 64, HALF), bf),
+        pltpu.VMEM((2, 2, 256, D), bf),
+        pltpu.SemaphoreType.DMA((2, 2)),
+        pltpu.SemaphoreType.DMA((2, 2)),
+        pltpu.SemaphoreType.DMA((8,)),
+    ]
+
+
+def forward_kernel(mod_at, *refs):
+    step, finish = forward_pieces(refs, mod_at)
+
+    def turn(at, carry):
+        step(at)
+        return carry
+
+    lax.fori_loop(0, FORWARD_STEPS, turn, 0)
+    finish()
+
+
+def grouped(weights):
+    return [each.reshape(4, 2, 2, -1, each.shape[-1]) for each in weights]
+
+
+def forward_layer(x, mods, mod_at, biases, keep, weights):
+    toks = x.shape[0]
+    return pl.pallas_call(
+        functools.partial(forward_kernel, mod_at),
+        out_shape=[jax.ShapeDtypeStruct((toks, width), kind) for width, kind in FORWARD_OUTS],
+        in_specs=[pl.BlockSpec(memory_space=pltpu.VMEM)] * 4
+        + [pl.BlockSpec(memory_space=pl.ANY)] * 4,
+        out_specs=[pl.BlockSpec(memory_space=pl.ANY)] * len(FORWARD_OUTS),
+        scratch_shapes=forward_scratch(toks),
+        compiler_params=pltpu.CompilerParams(vmem_limit_bytes=56 * 1024 * 1024),
+        cost_estimate=pl.CostEstimate(
+            flops=24 * toks * D * D, bytes_accessed=60 * 1024 * 1024, transcendentals=4 * toks * D
+        ),
+    )(x, mods, biases, keep, *grouped(weights))
+
+
+def backward_pieces(refs, mod_at):
+    (
+        grad_ref,
+        x_ref,
+        x_one_ref,
+        attn_ref,
+        down_ref,
+        qkv_ref,
+        mod_ref,
+        keep_ref,
+        pre_hbm,
+        w_qkv,
+        w_proj,
+        w_up,
+        w_down,
+        d_x_out,
+        d_down_out,
+        d_up_out,
+        d_attn_out,
+        d_qkv_out,
+        d_mod_ref,
+        d_bias_ref,
+        total_buf,
+        d_x_one_buf,
+        d_down_buf,
+        d_up_buf,
+        d_attn_buf,
+        d_heads_buf,
+        d_qkv_buf,
+        pre_buf,
+        wide_buf,
+        tall_buf,
+        load_sem,
+        tile_sem,
+        save_sem,
+    ) = refs
+    images, toks = keep_ref.shape
+    bf = jnp.bfloat16
+    blocks = toks // 64
+    saves = [
+        pltpu.make_async_copy(source, target, save_sem.at[at])
+        for at, (source, target) in enumerate(
+            [
+                (d_down_buf, d_down_out),
+                (d_attn_buf, d_attn_out),
+                (d_qkv_buf, d_qkv_out),
+                (total_buf, d_x_out),
+            ]
+        )
+    ]
+
+    def wide_load(source, tile, slot):
+        return pltpu.make_async_copy(
+            source.at[:, :, :, :, column_tile(tile)], wide_buf.at[slot], load_sem.at[0, slot]
+        )
+
+    def tall_load(tile, slot):
+        return pltpu.make_async_copy(
+            w_down.at[tile // 2, lax.rem(tile, 2)], tall_buf.at[slot], load_sem.at[1, slot]
+        )
+
+    def pre_load(tile, slot):
+        return pltpu.make_async_copy(
+            pre_hbm.at[:, column_tile(tile)], pre_buf.at[slot], load_sem.at[2, slot]
+        )
+
+    def up_save(tile, slot):
+        return pltpu.make_async_copy(
+            d_up_buf.at[slot], d_up_out.at[:, column_tile(tile)], tile_sem.at[slot]
+        )
+
+    def wide_tile(slot):
+        return wide_buf[slot].reshape(D, HALF)
+
+    def tall_tile(slot):
+        return tall_buf[slot].reshape(HALF, D)
+
+    def loads(at, run):
+        slot = lax.rem(at, 2)
+
+        @pl.when(within(at, 1, 8))
+        def _():
+            run(tall_load(at - 1, slot))
+            run(wide_load(w_up, at - 1, slot))
+            run(pre_load(at - 1, slot))
+
+        @pl.when(within(at, 10, 2))
+        def _():
+            run(wide_load(w_proj, at - 10, slot))
+
+        @pl.when(within(at, 20, 6))
+        def _():
+            run(wide_load(w_qkv, at - 20, slot))
+
+    def column_sums(rows):
+        return jnp.sum(rows.astype(jnp.float32), axis=0, keepdims=True)
+
+    def gated(image, gate_row, gradient, branch, target, bias_cols):
+        def rows_of(block, sums):
+            rows = pl.ds(pl.multiple_of(image * toks + block * 64, 64), 64)
+            upper = gradient[rows, :]
+            gate = mod_ref[mod_at + gate_row + image : mod_at + gate_row + image + 1, :]
+            lower = (upper * gate).astype(bf)
+            target[rows, :] = lower
+            return sums[0] + column_sums(upper * branch[rows, :]), sums[1] + column_sums(lower)
+
+        zero = jnp.zeros((1, D), jnp.float32)
+        gate, bias = lax.fori_loop(0, blocks, rows_of, (zero, zero))
+        d_mod_ref[gate_row + image : gate_row + image + 1, :] = gate
+        if image == 0:
+            d_bias_ref[:, bias_cols] = bias
+        else:
+            d_bias_ref[:, bias_cols] += bias
+
+    def modulate_back(image, first_row, source, passed, target):
+        def rows_of(block, sums):
+            rows = pl.ds(pl.multiple_of(image * toks + block * 64, 64), 64)
+            scale_row = mod_at + first_row + 2 + image
+            scale = mod_ref[scale_row : scale_row + 1, :]
+            unit, inverse = normalized(source[rows, :])
+            upper = total_buf[rows, :]
+            inner = upper * (1.0 + scale)
+            back = inverse * (
+                inner
+                - jnp.mean(inner, axis=-1, keepdims=True)
+                - unit * jnp.mean(inner * unit, axis=-1, keepdims=True)
+            )
+            target[rows, :] = back + passed[rows, :]
+            return sums[0] + column_sums(upper), sums[1] + column_sums(upper * unit)
+
+        zero = jnp.zeros((1, D), jnp.float32)
+        shift, scale = lax.fori_loop(0, blocks, rows_of, (zero, zero))
+        d_mod_ref[first_row + image : first_row + image + 1, :] = shift
+        d_mod_ref[first_row + 2 + image : first_row + 3 + image, :] = scale
+
+    def attend_back(image, pair):
+        rows = pl.ds(pl.multiple_of(image * toks, toks), toks)
+        low = lax.broadcasted_iota(jnp.int32, (toks, 128), 1) < 64
+        eighth = jnp.asarray(0.125, bf)
+        queries = qkv_ref[rows, column_tile(pair, 128)] * eighth
+        keys = qkv_ref[rows, column_tile(8 + pair, 128)]
+        values = qkv_ref[rows, column_tile(16 + pair, 128)]
+        upper = d_heads_buf[rows, column_tile(pair, 128)]
+        keep = keep_ref[pl.ds(image, 1), :]
+        zero = jnp.zeros_like(queries)
+        total = jnp.zeros((toks, 128), jnp.float32)
+        d_q, d_k, d_v = total, total, total
+        for own in (low, jnp.logical_not(low)):
+            own_q = jnp.where(own, queries, zero)
+            own_up = jnp.where(own, upper, zero)
+            probs = head_probs(own_q, keys, keep)
+            d_probs = dot_nt(own_up, values)
+            mean = jnp.sum(probs * d_probs, axis=-1, keepdims=True)
+            d_scores = (probs * (d_probs - mean)).astype(bf)
+            d_v = d_v + dot_tn(probs.astype(bf), own_up)
+            d_q = d_q + dot_nn(d_scores, jnp.where(own, keys * eighth, zero))
+            d_k = d_k + dot_tn(d_scores, own_q)
+        d_qkv_buf[rows, column_tile(pair, 128)] = d_q.astype(bf)
+        d_qkv_buf[rows, column_tile(8 + pair, 128)] = d_k.astype(bf)
+        d_qkv_buf[rows, column_tile(16 + pair, 128)] = d_v.astype(bf)
+
+    def add_product(first, image_rows, part):
+        @pl.when(first)
+        def _():
+            total_buf[image_rows, :] = part
+
+        @pl.when(jnp.logical_not(first))
+        def _():
+            total_buf[image_rows, :] += part
+
+    def step(at):
+        slot = lax.rem(at, 2)
+        loads(at + 1, lambda copy: copy.start())
+        loads(at, lambda copy: copy.wait())
+
+        @pl.when(at == 0)
+        def _():
+            for image in range(images):
+                gated(image, 10, grad_ref, down_ref, d_down_buf, slice(8 * D, 9 * D))
+            saves[0].start()
+
+        @pl.when(within(at, 1, 8))
+        def _():
+            tile = at - 1
+
+            @pl.when(tile >= 2)
+            def _():
+                up_save(tile - 2, slot).wait()
+
+            bias = jnp.zeros((1, HALF), jnp.float32)
+            for image in range(images):
+                rows = pl.ds(image * toks, toks)
+                upper = dot_nt(d_down_buf[rows, :], tall_tile(slot))
+                pre = pre_buf[slot, rows, :]
+                square = pre * pre
+                inner = jnp.tanh(GELU_IN * (pre + GELU_CUBE * square * pre))
+                slope = 0.5 * (1.0 + inner) + 0.5 * pre * (1.0 - inner * inner) * (
+                    GELU_IN * (1.0 + 3.0 * GELU_CUBE * square)
+                )
+                lower = (upper * slope).astype(bf)
+                d_up_buf[slot, rows, :] = lower
+                bias = bias + column_sums(lower)
+                add_product(tile == 0, rows, dot_nt(lower, wide_tile(slot)))
+            d_bias_ref[:, column_tile(tile + 8)] = bias
+            up_save(tile, slot).start()
+
+        @pl.when(at == 9)
+        def _():
+            for image in range(images):
+                modulate_back(image, 6, x_one_ref, grad_ref, d_x_one_buf)
+                gated(image, 4, d_x_one_buf, attn_ref, d_attn_buf, slice(3 * D, 4 * D))
+            saves[1].start()
+
+        @pl.when(within(at, 10, 2))
+        def _():
+            for image in range(images):
+                rows = pl.ds(image * toks, toks)
+                part = dot_nt(d_attn_buf[rows, column_tile(at - 10)], wide_tile(slot))
+                add_product(at == 10, rows, part)
+
+            @pl.when(at == 11)
+            def _():
+                d_heads_buf[...] = total_buf[...].astype(bf)
+
+        @pl.when(within(at, 12, 8))
+        def _():
+            for turn in range(2):
+                item = (at - 12) * 2 + turn
+                attend_back(item // 8, lax.rem(item, 8))
+
+        @pl.when(at == 20)
+        def _():
+            saves[2].start()
+
+        @pl.when(within(at, 20, 6))
+        def _():
+            cols = column_tile(at - 20)
+            bias = jnp.zeros((1, HALF), jnp.float32)
+            for image in range(images):
+                rows = pl.ds(image * toks, toks)
+                lower = d_qkv_buf[rows, cols]
+                bias = bias + column_sums(lower)
+                add_product(at == 20, rows, dot_nt(lower, wide_tile(slot)))
+            d_bias_ref[:, cols] = bias
+
+        @pl.when(at == BACKWARD_STEPS - 1)
+        def _():
+            for image in range(images):
+                modulate_back(image, 0, x_ref, d_x_one_buf, total_buf)
+            saves[3].start()
+
+    def finish():
+        for tile in (6, 7):
+            up_save(tile, tile % 2).wait()
+        for copy in saves:
+            copy.wait()
+
+    return step, finish
+
+
+BACKWARD_OUTS = [
+    (D, jnp.float32),
+    (D, jnp.bfloat16),
+    (FF, jnp.bfloat16),
+    (D, jnp.bfloat16),
+    (3 * D, jnp.bfloat16),
+]
+
+
+def backward_scratch(toks):
+    bf, f32 = jnp.bfloat16, jnp.float32
+    return [
+        pltpu.VMEM((toks, D), f32),
+        pltpu.VMEM((toks, D), f32),
+        pltpu.VMEM((toks, D), bf),
+        pltpu.VMEM((2, toks, HALF), bf),
+        pltpu.VMEM((toks, D), bf),
+        pltpu.VMEM((toks, D), bf),
+        pltpu.VMEM((toks, 3 * D), bf),
+        pltpu.VMEM((2, toks, HALF), f32),
+        pltpu.VMEM((2, 4, 2, 2, 64, HALF), bf),
+        pltpu.VMEM((2, 2, 256, D), bf),
+        pltpu.SemaphoreType.DMA((3, 2)),
+        pltpu.SemaphoreType.DMA((2,)),
+        pltpu.SemaphoreType.DMA((4,)),
+    ]
+
+
+def backward_kernel(mod_at, *refs):
+    step, finish = backward_pieces(refs, mod_at)
+
+    def turn(at, carry):
+        step(at)
+        return carry
+
+    lax.fori_loop(0, BACKWARD_STEPS, turn, 0)
+    finish()
+
+
+def backward_layer(grad, x, saved, mods, mod_at, keep, weights):
+    a_one, qkv, merged, attn, x_one, a_two, pre, act, down, _ = saved
+    toks = x.shape[0]
+    vmem = pl.BlockSpec(memory_space=pltpu.VMEM)
+    hbm = pl.BlockSpec(memory_space=pl.ANY)
+    outs = pl.pallas_call(
+        functools.partial(backward_kernel, mod_at),
+        out_shape=[jax.ShapeDtypeStruct((toks, width), kind) for width, kind in BACKWARD_OUTS]
+        + [
+            jax.ShapeDtypeStruct((12, D), jnp.float32),
+            jax.ShapeDtypeStruct((1, 9 * D), jnp.float32),
+        ],
+        in_specs=[vmem] * 8 + [hbm] * 5,
+        out_specs=[hbm] * len(BACKWARD_OUTS) + [vmem] * 2,
+        scratch_shapes=backward_scratch(toks),
+        compiler_params=pltpu.CompilerParams(vmem_limit_bytes=56 * 1024 * 1024),
+        cost_estimate=pl.CostEstimate(
+            flops=28 * toks * D * D, bytes_accessed=80 * 1024 * 1024, transcendentals=4 * toks * D
+        ),
+    )(grad, x, x_one, attn, down, qkv, mods, keep, pre, *grouped(weights))
+    d_x, d_down, d_up, d_attn, d_qkv, d_mod, d_bias = outs
+    factors = (merged, a_one, a_two, act, d_attn, d_qkv, d_up, d_down)
+    return d_x, d_mod, factors, d_bias
+
+
+def gather_pieces(lines, refs):
+    layers = (len(refs) - 7) // 8
+    pairs = list(zip(refs[: 4 * layers], refs[4 * layers : 8 * layers]))
+    own_sem, zp_sem, zq_sem, yp_sem, yq_sem, x_sem, core_sem = refs[8 * layers :]
+    firsts = [12 * layer + first for layer in range(layers) for first in (0, 3, 4, 8)]
+    total = 12 * layers
     seq = lax.axis_index("seq")
     dp = lax.axis_index("dp")
     core = lax.rem(dp, 2)
@@ -480,10 +1118,6 @@
         {"seq": seq, "dp": lax.rem(zed + step, lines) * 4 + 2 * why + core}
         for step in range(1, lines)
     ]
-    pairs = [(qkv_own, qkv_all), (proj_own, proj_all), (up_own, up_all), (down_own, down_all)]
-    firsts = [0, 3, 4, 8]
-    total = 12
-
     keeps = [
         pltpu.make_async_copy(own, every.at[zed, why, core], own_sem.at[at])
         for at, (own, every) in enumerate(pairs)
@@ -499,7 +1133,7 @@
 
     def places(kind, unit):
         at = unit - firsts[kind]
-        if kind == 3:
+        if kind % 4 == 3:
             return pl.multiple_of(at * 64, 64), 0
         return 0, pl.multiple_of(at * D, D)
 
@@ -546,7 +1180,7 @@
 
     def each_kind(unit, run):
         ends = firsts[1:] + [total]
-        for kind in range(4):
+        for kind in range(len(firsts)):
 
             @pl.when(jnp.logical_and(unit >= firsts[kind], unit < ends[kind]))
             def _():
@@ -566,162 +1200,265 @@
 
         each_kind(unit, run)
 
-    def turn(at, carry):
+    def step(at):
         finish(3, at - sum(GATHER_LAGS))
         for stage in (3, 2, 1):
             behind = sum(GATHER_LAGS[:stage])
             finish(stage - 1, at - behind)
             begin(stage, at - behind)
         begin(0, at)
+
+    return step, total + sum(GATHER_LAGS)
+
+
+def gather_scratch(lines, layers):
+    dma = pltpu.SemaphoreType.DMA
+    units = 12 * layers
+    return [
+        dma((4 * layers,)),
+        dma((units, lines - 1, 2)),
+        dma((units, lines - 1, 2)),
+        dma((units, 2)),
+        dma((units, 2)),
+        dma((units, 2)),
+        dma((units, 2)),
+    ]
+
+
+def modulation_pieces(lines, refs):
+    (
+        partial_ref,
+        bias_ref,
+        mods_ref,
+        core_in,
+        core_total,
+        y_in,
+        y_total,
+        z_in,
+        core_sem,
+        y_sem,
+        z_sem,
+    ) = refs
+    seq = lax.axis_index("seq")
+    dp = lax.axis_index("dp")
+    core = lax.rem(dp, 2)
+    why = lax.rem(dp // 2, 2)
+    zed = dp // 4
+
+    def remote(source, target, sems, peer):
+        return pltpu.make_async_remote_copy(
+            src_ref=source,
+            dst_ref=target,
+            send_sem=sems.at[0],
+            recv_sem=sems.at[1],
+            device_id={"seq": seq, "dp": peer},
+            device_id_type=MESH,
+        )
+
+    to_core = remote(partial_ref.at[:, :, 1 - core], core_in, core_sem, dp + 1 - 2 * core)
+    to_y = remote(core_total.at[:, 1 - why], y_in, y_sem, dp + 2 - 4 * why)
+    to_z = []
+    for ahead in range(1, lines):
+        there = lax.rem(zed + ahead, lines)
+        to_z.append(
+            remote(
+                y_total.at[there],
+                z_in.at[ahead - 1],
+                z_sem.at[ahead - 1],
+                there * 4 + 2 * why + core,
+            )
+        )
+
+    def step(at):
+        @pl.when(at == 0)
+        def _():
+            to_core.start()
+
+        @pl.when(at == 1)
+        def _():
+            to_core.wait()
+            core_total[...] = partial_ref[:, :, core] + core_in[...]
+            to_y.start()
+
+        @pl.when(at == 4)
+        def _():
+            to_y.wait()
+            y_total[...] = core_total[:, why] + y_in[...]
+            for copy in to_z:
+                copy.start()
+
+        @pl.when(at == 8)
+        def _():
+            total = y_total[zed] + bias_ref[...]
+            for ahead, copy in enumerate(to_z):
+                copy.wait()
+                total = total + z_in[ahead]
+            mods_ref[...] = total
+
+    return step
+
+
+def modulation_scratch(lines, rows):
+    dma = pltpu.SemaphoreType.DMA
+    f32 = jnp.float32
+    return [
+        pltpu.VMEM((lines, 2, rows, D), f32),
+        pltpu.VMEM((lines, 2, rows, D), f32),
+        pltpu.VMEM((lines, rows, D), f32),
+        pltpu.VMEM((lines, rows, D), f32),
+        pltpu.VMEM((lines - 1, rows, D), f32),
+        dma((2,)),
+        dma((2,)),
+        dma((lines - 1, 2)),
+    ]
+
+
+def whole_forward_kernel(lines, *refs):
+    refs = list(refs)
+
+    def take(count):
+        taken, refs[:] = tuple(refs[:count]), refs[count:]
+        return taken
+
+    own = take(8)
+    partial_ref, mod_bias, x_ref, first_bias, second_bias, keep = take(6)
+    every = take(8)
+    first_outs, second_outs = take(len(FORWARD_OUTS)), take(len(FORWARD_OUTS))
+    (mods,) = take(1)
+    gather_sems = take(7)
+    mod_scratch = take(8)
+    scratch = tuple(refs)
+    gather, steps = gather_pieces(lines, own + every + gather_sems)
+    modulate_step = modulation_pieces(lines, (partial_ref, mod_bias, mods) + mod_scratch)
+    first, first_finish = forward_pieces(
+        (x_ref, mods, first_bias, keep) + every[:4] + first_outs + scratch, 0
+    )
+    second, second_finish = forward_pieces(
+        (scratch[9], mods, second_bias, keep) + every[4:] + second_outs + scratch, 12
+    )
+
+    def run(step, begin, end):
+        def one(at, carry):
+            step(at)
+            return carry
+
+        lax.fori_loop(begin, end, one, 0)
+
+    def turn(at, carry):
+        gather(at)
+        modulate_step(at)
+
+        @pl.when(within(at, 10, 13))
+        def _():
+            run(first, 2 * (at - 10), 2 * (at - 9))
+
+        @pl.when(at == 23)
+        def _():
+            first_finish()
+
+        @pl.when(at >= 24)
+        def _():
+            run(second, 18 * (at - 24) // 7, 18 * (at - 23) // 7)
+
         return carry
 
-    lax.fori_loop(0, total + sum(GATHER_LAGS), turn, 0)
-
-
-def gather_blocks(qkv_own, proj_own, up_own, down_own, lines, collective_id):
-    owns = (qkv_own, proj_own, up_own, down_own)
-    dma = pltpu.SemaphoreType.DMA
+    lax.fori_loop(0, steps + 4, turn, 0)
+    second_finish()
+
+
+def whole_forward(own, partial, mod_bias, x, biases, keep, lines):
+    toks = x.shape[0]
+    rows = mod_bias.shape[0]
+    vmem = pl.BlockSpec(memory_space=pltpu.VMEM)
+    hbm = pl.BlockSpec(memory_space=pl.ANY)
+    layer_outs = [jax.ShapeDtypeStruct((toks, width), kind) for width, kind in FORWARD_OUTS]
     outs = pl.pallas_call(
-        functools.partial(gather_kernel, lines),
+        functools.partial(whole_forward_kernel, lines),
         out_shape=[
-            jax.ShapeDtypeStruct((lines, 2, 2) + own.shape, jnp.bfloat16) for own in owns
-        ],
-        in_specs=[pl.BlockSpec(memory_space=pltpu.VMEM)] * 4,
-        out_specs=[pl.BlockSpec(memory_space=pl.ANY)] * 4,
-        scratch_shapes=[
-            dma((4,)),
-            dma((12, lines - 1, 2)),
-            dma((12, lines - 1, 2)),
-            dma((12, 2)),
-            dma((12, 2)),
-            dma((12, 2)),
-            dma((12, 2)),
-        ],
+            jax.ShapeDtypeStruct((lines, 2, 2) + each.shape, jnp.bfloat16) for each in own
+        ]
+        + layer_outs
+        + layer_outs
+        + [jax.ShapeDtypeStruct((rows, D), jnp.float32)],
+        in_specs=[vmem] * 14,
+        out_specs=[hbm] * (8 + 2 * len(FORWARD_OUTS)) + [vmem],
+        scratch_shapes=gather_scratch(lines, 2)
+        + modulation_scratch(lines, rows)
+        + forward_scratch(toks),
         compiler_params=pltpu.CompilerParams(
-            collective_id=collective_id,
-            has_side_effects=True,
-            vmem_limit_bytes=56 * 1024 * 1024,
+            collective_id=2, has_side_effects=True, vmem_limit_bytes=58 * 1024 * 1024
         ),
         cost_estimate=pl.CostEstimate(
-            flops=0, bytes_accessed=12 * 4 * lines * 64 * D * 8, transcendentals=0
+            flops=48 * toks * D * D,
+            bytes_accessed=24 * 4 * lines * 64 * D * 8,
+            transcendentals=8 * toks * D,
         ),
-    )(*owns)
-    return tuple(every.reshape(-1, every.shape[-1]) for every in outs)
-
-
-def layer_forward(stream, modul, weight_set, bias_part, pad_mask):
-    w_qkv, w_proj, w_up, w_down = weight_set
-    images, tok_rows, _ = stream.shape
-    shift_one, scale_one, gate_one, shift_two, scale_two, gate_two = split_six(modul)
-    a_one = (
-        modulate(stream, shift_one, scale_one).astype(jnp.bfloat16).reshape(images * tok_rows, D)
-    )
-    qkv_all = (matdot(a_one, w_qkv) + bias_part[: 3 * D]).astype(jnp.bfloat16)
-    heads_in = qkv_all.reshape(images, tok_rows, 3, HEADS, HEAD_DIM)
-    queries, key_rows, value_rows = (heads_in[:, :, 0], heads_in[:, :, 1], heads_in[:, :, 2])
-    scores = jnp.einsum(
-        "bqhd,bkhd->bhqk", queries, key_rows, preferred_element_type=jnp.float32
-    ) * HEAD_DIM ** (-0.5)
-    attn_probs = jax.nn.softmax(
-        jnp.where(pad_mask[:, None, None, :] > 0, scores, -1000000000.0), axis=-1
-    )
-    heads_out = jnp.einsum(
-        "bhqk,bkhd->bqhd",
-        attn_probs.astype(jnp.bfloat16),
-        value_rows,
-        preferred_element_type=jnp.float32,
-    )
-    merged = heads_out.astype(jnp.bfloat16).reshape(images * tok_rows, D)
-    attn_out = (matdot(merged, w_proj) + bias_part[3 * D : 4 * D]).reshape(images, tok_rows, D)
-    stream_one = stream + gate_one[:, None, :] * attn_out
-    a_two = (
-        modulate(stream_one, shift_two, scale_two)
-        .astype(jnp.bfloat16)
-        .reshape(images * tok_rows, D)
-    )
-    up_pre = matdot(a_two, w_up) + bias_part[4 * D : 4 * D + FF]
-    activated = jax.nn.gelu(up_pre, approximate=True).astype(jnp.bfloat16)
-    down_out = (matdot(activated, w_down) + bias_part[4 * D + FF :]).reshape(images, tok_rows, D)
-    stream_two = stream_one + gate_two[:, None, :] * down_out
-    saved = (
-        a_one,
-        queries,
-        key_rows,
-        value_rows,
-        attn_probs,
-        merged,
-        attn_out,
-        stream_one,
-        a_two,
-        up_pre,
-        activated,
-        down_out,
-    )
-    return (stream_two, saved)
-
-
-def layer_backward(grad_in, stream, modul, weight_set, saved):
-    w_qkv, w_proj, w_up, w_down = weight_set
-    (
-        a_one,
-        queries,
-        key_rows,
-        value_rows,
-        attn_probs,
-        merged,
-        attn_out,
-        stream_one,
-        a_two,
-        up_pre,
-        activated,
-        down_out,
-    ) = saved
-    images, tok_rows, _ = stream.shape
-    shift_one, scale_one, gate_one, shift_two, scale_two, gate_two = split_six(modul)
-    d_gate_two = jnp.sum(grad_in * down_out, axis=1)
-    d_down = (grad_in * gate_two[:, None, :]).astype(jnp.bfloat16).reshape(images * tok_rows, D)
-    d_activated = matdot(d_down, w_down.T)
-    _, gelu_back = jax.vjp(lambda inner: jax.nn.gelu(inner, approximate=True), up_pre)
-    d_up = gelu_back(d_activated)[0].astype(jnp.bfloat16)
-    d_a_two = matdot(d_up, w_up.T).reshape(images, tok_rows, D)
-    _, mod_back_two = jax.vjp(modulate, stream_one, shift_two, scale_two)
-    d_stream_one, d_shift_two, d_scale_two = mod_back_two(d_a_two)
-    d_stream_one = d_stream_one + grad_in
-    d_gate_one = jnp.sum(d_stream_one * attn_out, axis=1)
-    d_attn = (
-        (d_stream_one * gate_one[:, None, :]).astype(jnp.bfloat16).reshape(images * tok_rows, D)
-    )
-    d_heads = matdot(d_attn, w_proj.T).astype(jnp.bfloat16)
-    d_heads = d_heads.reshape(images, tok_rows, HEADS, HEAD_DIM)
-    d_values = jnp.einsum(
-        "bhqk,bqhd->bkhd",
-        attn_probs.astype(jnp.bfloat16),
-        d_heads,
-        preferred_element_type=jnp.float32,
-    )
-    d_probs = jnp.einsum("bqhd,bkhd->bhqk", d_heads, value_rows, preferred_element_type=jnp.float32)
-    d_scores = attn_probs * (d_probs - jnp.sum(attn_probs * d_probs, axis=-1, keepdims=True))
-    d_scores = d_scores.astype(jnp.bfloat16)
-    d_queries = jnp.einsum(
-        "bhqk,bkhd->bqhd", d_scores, key_rows, preferred_element_type=jnp.float32
-    ) * HEAD_DIM ** (-0.5)
-    d_keys = jnp.einsum(
-        "bhqk,bqhd->bkhd", d_scores, queries, preferred_element_type=jnp.float32
-    ) * HEAD_DIM ** (-0.5)
-    d_qkv = jnp.stack([d_queries, d_keys, d_values], axis=2).astype(jnp.bfloat16)
-    d_qkv = d_qkv.reshape(images * tok_rows, 3 * D)
-    d_a_one = matdot(d_qkv, w_qkv.T).reshape(images, tok_rows, D)
-    _, mod_back_one = jax.vjp(modulate, stream, shift_one, scale_one)
-    d_stream, d_shift_one, d_scale_one = mod_back_one(d_a_one)
-    d_stream = d_stream + d_stream_one
-    d_modul = jnp.concatenate(
-        [d_shift_one, d_scale_one, d_gate_one, d_shift_two, d_scale_two, d_gate_two], axis=1
-    )
-    d_bias = jnp.concatenate(
-        [column_sum(d_qkv), column_sum(d_attn), column_sum(d_up), column_sum(d_down)]
-    )
-    factors = (merged, a_one, a_two, activated, d_attn, d_qkv, d_up, d_down)
-    return (d_stream, d_modul, factors, d_bias)
+    )(*own, partial, mod_bias, x, *biases, keep)
+    weights = outs[:8]
+    count = len(FORWARD_OUTS)
+    saved = [outs[8 : 8 + count], outs[8 + count : 8 + 2 * count]]
+    return [weights[:4], weights[4:]], saved, outs[-1]
+
+
+def gather_small_kernel(lines, own_ref, every_ref, z_sem, y_sem, core_sem):
+    seq = lax.axis_index("seq")
+    dp = lax.axis_index("dp")
+    core = lax.rem(dp, 2)
+    why = lax.rem(dp // 2, 2)
+    zed = dp // 4
+    core_peer = {"seq": seq, "dp": dp + 1 - 2 * core}
+    y_peer = {"seq": seq, "dp": dp + 2 - 4 * why}
+    z_peers = [
+        {"seq": seq, "dp": lax.rem(zed + step, lines) * 4 + 2 * why + core}
+        for step in range(1, lines)
+    ]
+    barrier = pltpu.get_barrier_semaphore()
+    for peer in [core_peer, y_peer] + z_peers:
+        pl.semaphore_signal(barrier, inc=1, device_id=peer, device_id_type=MESH)
+    every_ref[zed, why, core] = own_ref[...]
+    pl.semaphore_wait(barrier, 1 + lines)
+
+    def remote(source, target, sems, peer):
+        return pltpu.make_async_remote_copy(
+            src_ref=source,
+            dst_ref=target,
+            send_sem=sems.at[0],
+            recv_sem=sems.at[1],
+            device_id=peer,
+            device_id_type=MESH,
+        )
+
+    copies = [
+        remote(own_ref, every_ref.at[zed, why, core], z_sem.at[at], peer)
+        for at, peer in enumerate(z_peers)
+    ]
+    for copy in copies:
+        copy.start()
+    for copy in copies:
+        copy.wait()
+    for view, sems, peer in (
+        (every_ref.at[:, why, core], y_sem, y_peer),
+        (every_ref.at[:, :, core], core_sem, core_peer),
+    ):
+        copy = remote(view, view, sems, peer)
+        copy.start()
+        copy.wait()
+
+
+def gather_small(own, lines, collective_id):
+    dma = pltpu.SemaphoreType.DMA
+    every = pl.pallas_call(
+        functools.partial(gather_small_kernel, lines),
+        out_shape=jax.ShapeDtypeStruct((lines, 2, 2) + own.shape, own.dtype),
+        in_specs=[pl.BlockSpec(memory_space=pltpu.VMEM)],
+        out_specs=pl.BlockSpec(memory_space=pltpu.VMEM),
+        scratch_shapes=[dma((lines - 1, 2)), dma((2,)), dma((2,))],
+        compiler_params=pltpu.CompilerParams(collective_id=collective_id, has_side_effects=True),
+        cost_estimate=pl.CostEstimate(
+            flops=0, bytes_accessed=own.size * 32 * lines, transcendentals=0
+        ),
+    )(own)
+    return every.reshape(-1, own.shape[-1])
 
 
 def gather_rows(shard):
@@ -736,12 +1473,6 @@
         and D // dp_parts == 64
         and FF // dp_parts == PARTS * 64
     )
-
-
-def gather_layer(shards, collective_id):
-    if kernels_fit():
-        return gather_blocks(*shards, lax.axis_size("dp") // 4, collective_id)
-    return tuple(gather_rows(shard) for shard in shards)
 
 
 def reduce_rows(partial):
@@ -830,48 +1561,69 @@
     dp_parts = lax.axis_size("dp")
     seq_at = lax.axis_index("seq")
     dp_at = lax.axis_index("dp")
-    group, _, _ = latents.shape
+    lines = dp_parts // 4
+    group, half_rows, _ = latents.shape
     images = group // seq_parts
     everyone = group * dp_parts
     own_cols = embed_rows.shape[1]
+    own_place = dp_at * own_cols
     cond_cols = cond_weight.shape[1]
+    pieces = cond_cols // D
     bias_base = 3 * D + cond_cols
+    by_kernel = kernels_fit()
     packed = jnp.concatenate(
         [latents, noise_target, pad_mask.astype(jnp.float32)[:, :, None]], axis=2
     )
-    packed = lax.all_to_all(packed, "seq", split_axis=0, concat_axis=1, tiled=True)
+    shards = [
+        weight[at].astype(jnp.bfloat16)
+        for at in range(LAYERS)
+        for weight in (qkv_weight, proj_weight, up_weight, down_weight)
+    ]
+    narrow = jnp.concatenate(
+        [embed_rows[: PATCH_IN + FREQ].T, head_weight], axis=1
+    ).astype(jnp.bfloat16)
+    if by_kernel:
+        ids = jnp.stack([labels, timesteps])
+        parts = jnp.stack([ids // 32, ids % 32]).astype(jnp.bfloat16).reshape(-1, 1)
+        parts = jnp.pad(parts, ((0, own_cols - parts.shape[0]), (0, 0)))
+        width = narrow.shape[1]
+        block = jnp.concatenate(
+            [narrow, parts, jnp.zeros((own_cols, 383 - width), jnp.bfloat16)], axis=1
+        )
+        small = gather_small(block, lines, 4)
+        parts = small[:, width].astype(jnp.float32).reshape(dp_parts, own_cols)[:, : 4 * group]
+        parts = parts.reshape(dp_parts, 2, 2, group)
+        ids = (parts[:, 0] * 32.0 + parts[:, 1]).astype(jnp.int32)
+        ids = ids.transpose(1, 0, 2).reshape(2, everyone)
+        theirs = lax.dynamic_slice(
+            packed, ((1 - seq_at) * images, 0, 0), (images,) + packed.shape[1:]
+        )
+        mine = lax.dynamic_slice(packed, (seq_at * images, 0, 0), (images,) + packed.shape[1:])
+        came = lax.ppermute(theirs, "seq", [(0, 1), (1, 0)])
+        packed = jnp.concatenate(
+            [jnp.where(seq_at == 0, mine, came), jnp.where(seq_at == 0, came, mine)], axis=1
+        )
+    else:
+        small = lax.all_gather(narrow, "dp", axis=0, tiled=True)
+        ids = lax.all_gather(jnp.stack([labels, timesteps]), "dp", axis=1, tiled=True)
+        packed = lax.all_to_all(packed, "seq", split_axis=0, concat_axis=1, tiled=True)
     tok_rows = packed.shape[1]
-    shards = [
-        tuple(
-            weight[at].astype(jnp.bfloat16)
-            for weight in (qkv_weight, proj_weight, up_weight, down_weight)
-        )
-        for at in range(LAYERS)
-    ]
-    weights_kept = [gather_layer(shards[0], 2)]
-    ids = lax.all_gather(jnp.stack([labels, timesteps]), "dp", axis=1, tiled=True)
-    small = jnp.concatenate(
-        [embed_rows[: PATCH_IN + FREQ], head_weight.T], axis=0
-    ).astype(jnp.bfloat16)
-    small = lax.all_gather(small, "dp", axis=1, tiled=True)
-    ids, small, packed, weights_kept[0] = lax.optimization_barrier(
-        (ids, small, packed, weights_kept[0])
-    )
+    toks = images * tok_rows
     latents, noise_target, keep_rows = (
         packed[:, :, :PATCH_IN],
         packed[:, :, PATCH_IN : 2 * PATCH_IN],
         packed[:, :, 2 * PATCH_IN],
     )
-    patch_part = small[:PATCH_IN]
-    freq_part = small[PATCH_IN : PATCH_IN + FREQ]
-    head_rows = small[PATCH_IN + FREQ :]
+    patch_part = small[:, :PATCH_IN]
+    freq_part = small[:, PATCH_IN : PATCH_IN + FREQ]
+    head_full = small[:, PATCH_IN + FREQ : PATCH_IN + FREQ + OUT_CH]
     time_own = embed_rows[PATCH_IN + FREQ :].astype(jnp.bfloat16)
     cond_own = cond_weight.astype(jnp.bfloat16)
 
     features = time_features(ids[1], FREQ).astype(jnp.bfloat16)
-    time_pre = matdot(features, freq_part) + all_biases[D : 2 * D]
+    time_pre = dot_nt(features, freq_part) + all_biases[D : 2 * D]
     time_hidden = jax.nn.silu(time_pre).astype(jnp.bfloat16)
-    second_bias_own = lax.dynamic_slice(all_biases, (2 * D + dp_at * own_cols,), (own_cols,))
+    second_bias_own = lax.dynamic_slice(all_biases, (2 * D + own_place,), (own_cols,))
     onehot = (ids[0][:, None] == jnp.arange(NCLASS, dtype=jnp.int32)[None, :]).astype(jnp.float32)
     condition = (
         matdot(time_hidden, time_own)
@@ -882,44 +1634,57 @@
     plane_act = lax.dynamic_index_in_dim(
         cond_act.reshape(dp_parts, seq_parts, images, own_cols), seq_at, 1, keepdims=False
     ).reshape(dp_parts * images, own_cols)
-    mod_partial = matdot(plane_act, cond_own)
-    mod_partial, shards[1] = lax.optimization_barrier((mod_partial, shards[1]))
-    weights_kept.append(gather_layer(shards[1], 3))
-    modulation = lax.psum_scatter(mod_partial, "dp", scatter_dimension=0, tiled=True)
-    modulation = modulation + all_biases[3 * D : bias_base]
+    partial = matdot(plane_act, cond_own).reshape(dp_parts, images, pieces, D)
+    partial = partial.transpose(0, 2, 1, 3).reshape(dp_parts, pieces * images, D)
+    mod_bias = jnp.repeat(all_biases[3 * D : bias_base].reshape(pieces, D), images, axis=0)
 
     position = position_table(jnp.arange(tok_rows, dtype=jnp.int32), D, GRID)
-    flat_in = latents.astype(jnp.bfloat16).reshape(images * tok_rows, PATCH_IN)
-    stream = (matdot(flat_in, patch_part) + all_biases[:D]).reshape(images, tok_rows, D) + position[
-        None
-    ]
+    flat_in = latents.astype(jnp.bfloat16).reshape(toks, PATCH_IN)
+    stream = (dot_nt(flat_in, patch_part) + all_biases[:D]).reshape(
+        images, tok_rows, D
+    ) + position[None]
+    stream = stream.reshape(toks, D)
     layer_bias = [
-        all_biases[bias_base + at * (5 * D + FF) : bias_base + (at + 1) * (5 * D + FF)]
+        all_biases[bias_base + at * 9 * D : bias_base + (at + 1) * 9 * D].reshape(1, 9 * D)
         for at in range(LAYERS)
     ]
-    inputs_kept = []
-    saved_kept = []
-    for at in range(LAYERS):
-        inputs_kept.append(stream)
-        stream, saved = layer_forward(
+    if by_kernel:
+        weights_kept, saved_kept, mods = whole_forward(
+            shards,
+            partial.reshape(lines, 2, 2, pieces * images, D),
+            mod_bias,
             stream,
-            modulation[:, 6 * at * D : 6 * (at + 1) * D],
-            weights_kept[at],
-            layer_bias[at],
+            layer_bias,
             keep_rows,
-        )
-        saved_kept.append(saved)
-        if at == 0:
-            stream, time_own = lax.optimization_barrier((stream, time_own))
-            time_full = lax.all_gather(time_own, "dp", axis=1, tiled=True)
-    final_at = 6 * LAYERS * D
-    final_shift = modulation[:, final_at : final_at + D]
-    final_scale = modulation[:, final_at + D : final_at + 2 * D]
-    moved, final_back = jax.vjp(modulate, stream, final_shift, final_scale)
-    a_final = moved.astype(jnp.bfloat16).reshape(images * tok_rows, D)
-    head_out = lax.dot_general(
-        a_final, head_rows, (((1,), (1,)), ((), ())), preferred_element_type=jnp.float32
-    ) + all_biases[NBIAS - OUT_CH :]
+            lines,
+        )
+    else:
+        mods = mod_bias + lax.psum_scatter(
+            partial, "dp", scatter_dimension=0, tiled=True
+        ).reshape(pieces * images, D)
+        weights_kept = [
+            [gather_rows(shard) for shard in shards[4 * at : 4 * at + 4]] for at in range(LAYERS)
+        ]
+        saved_kept = []
+        upper = stream
+        for at in range(LAYERS):
+            saved_kept.append(
+                forward_layer(
+                    upper, mods, 6 * images * at, layer_bias[at], keep_rows, weights_kept[at]
+                )
+            )
+            upper = saved_kept[at][-1]
+    inputs_kept = [stream] + [saved[-1] for saved in saved_kept]
+    final, time_own = lax.optimization_barrier((inputs_kept[-1], time_own))
+    time_full = lax.all_gather(time_own, "dp", axis=1, tiled=True)
+    final_at = 6 * LAYERS * images
+    final_shift = mods[final_at : final_at + images]
+    final_scale = mods[final_at + images :]
+    moved, final_back = jax.vjp(
+        modulate, final.reshape(images, tok_rows, D), final_shift, final_scale
+    )
+    a_final = moved.astype(jnp.bfloat16).reshape(toks, D)
+    head_out = matdot(a_final, head_full) + all_biases[NBIAS - OUT_CH :]
     split_out = head_out.reshape(images, tok_rows, 4, 2, OUT_CH // 8)
     predicted = split_out[:, :, :, 0, :].reshape(images, tok_rows, PATCH_IN)
     errors = predicted - noise_target
@@ -928,27 +1693,32 @@
     d_pred = (2.0 * keep_rows[:, :, None] * errors).reshape(images, tok_rows, 4, 1, OUT_CH // 8)
     d_head = (
         jnp.concatenate([d_pred, jnp.zeros_like(d_pred)], axis=3)
-        .reshape(images * tok_rows, OUT_CH)
+        .reshape(toks, OUT_CH)
         .astype(jnp.bfloat16)
     )
     g_head = matdot(a_final.T, d_head)
-    d_a_final = matdot(d_head, head_rows).reshape(images, tok_rows, D)
+    d_a_final = dot_nt(d_head, head_full).reshape(images, tok_rows, D)
     d_stream, d_final_shift, d_final_scale = final_back(d_a_final)
+    d_stream = d_stream.reshape(toks, D)
     layer_factors = [None] * LAYERS
     layer_bias_grads = [None] * LAYERS
     modul_grads = [None] * LAYERS
     for at in reversed(range(LAYERS)):
-        d_stream, modul_grads[at], layer_factors[at], layer_bias_grads[at] = layer_backward(
+        d_stream, d_mod, layer_factors[at], d_bias = backward_layer(
             d_stream,
             inputs_kept[at],
-            modulation[:, 6 * at * D : 6 * (at + 1) * D],
+            saved_kept[at],
+            mods,
+            6 * images * at,
+            keep_rows,
             weights_kept[at],
-            saved_kept[at],
-        )
+        )
+        modul_grads[at] = d_mod.reshape(6, images, D).transpose(1, 0, 2).reshape(images, 6 * D)
+        layer_bias_grads[at] = d_bias.reshape(-1)
     d_mod_own = jnp.concatenate(modul_grads + [d_final_shift, d_final_scale], axis=1).astype(
         jnp.bfloat16
     )
-    d_patch = d_stream.astype(jnp.bfloat16).reshape(images * tok_rows, D)
+    d_patch = d_stream.astype(jnp.bfloat16)
     flat = jnp.concatenate(
         [column_sum(d_patch), jnp.zeros((2 * D,), jnp.float32), column_sum(d_mod_own)]
         + layer_bias_grads
@@ -971,7 +1741,6 @@
     )
     _, time_back = jax.vjp(jax.nn.silu, time_pre)
     d_time_pre = time_back(d_time_hidden)[0].astype(jnp.bfloat16)
-    own_place = dp_at * own_cols
     s_cond = matdot(cond_act.T, d_modulation)
     s_table = jnp.dot(onehot.T, d_condition, precision=lax.Precision.HIGHEST)
     g_time = matdot(time_hidden.T, d_time_own)

time: 1060 us -> 848 us (0.80)
  matrix products: 161 us -> 26 us
  Pallas kernels: 548 us -> 669 us
  local copies, waits for them, and re-layouts: 176 us -> 67.2 us
  blocking collectives: 64.2 us -> 20.9 us
  other arithmetic: 80.6 us -> 38.2 us
    pallas_call x2 -> x4, Pallas kernels: 276 us -> 398 us  [the longest x1 263 us: whole_forward(): pl.pallas_call(functools.partial(whole_forward_kernel, lines), out_shape=...]
    dot_general x27 -> x9, matrix products: 124 us -> 15.6 us  [matdot(): return jnp.dot(left, right, preferred_element_type=jnp.float32)]
    unnamed x343 -> x139, local copies, waits for them, and re-layouts: 60.7 us -> 16.1 us
    all_gather x2 -> x0, blocking collectives: 42.2 us -> none  [the longest x1 24.6 us: body(): small = lax.all_gather(small, 'dp', axis=1, tiled=True)]
    reshape x6 -> x5, local copies, waits for them, and re-layouts: 28.5 us -> 0.87 us  [the longest x1 0.74 us: body(): jnp.repeat(all_biases[3 * D:bias_base].reshape(pieces, D), images, axis=0)]
    dot_general x13 -> x3, matrix products: 30.2 us -> 4.59 us  [dot_nt(): lax.dot_general(left, right, (((1,), (1,)), ((), ())), preferred_element_...]
    convert_element_type x6 -> x4, local copies, waits for them, and re-layouts: 14.3 us -> 0.34 us  [the longest x2 0.18 us: time_features(): angles = timesteps.astype(jnp.float32)[:, None] * frequencies[None, :]]
    optimization_barrier x5 -> x0, local copies, waits for them, and re-layouts: 11.6 us -> none  [the longest x4 10.4 us: body(): lax.optimization_barrier((flat, d_mod_own, layer_factors))]
  transfers between devices with their start and end apart: 5 -> 4, of which waited for: 0 -> 0; matrix products, arithmetic and copies ran while one was open for 9% -> 11% of each run, Pallas kernels for 52% -> 34%
where the time goes in v4:
time: 848 us; the launch traced here: 841 us
  Pallas kernels  669 us (79%)
  local copies, waits for them, and re-layouts  67.2 us (8%)
  other arithmetic  38.2 us (5%)
  matrix products  26 us (3%)
  blocking collectives  20.9 us (2%)
  between operations  16 us (2%)
    pallas_call x1, Pallas kernels, scatter_sums(): pl.pallas_call(functools.partial(scatter_kernel, per_layer, total, lines)...  271 us
    pallas_call x1, Pallas kernels, whole_forward(): pl.pallas_call(functools.partial(whole_forward_kernel, lines), out_shape=...  263 us
    pallas_call x2, Pallas kernels, backward_layer(): pl.pallas_call(functools.partial(backward_kernel, mod_at), out_shape=[jax...  119 us
    all_gather x1, blocking collectives, body(): d_time = lax.all_gather(d_time_own, 'dp', axis=1, tiled=True)  20.9 us
    sub x7, other arithmetic, adamw(): weight - rate * (first_hat / (jnp.sqrt(second_hat) + EPSILON) + DECAY * w...  17.5 us
  transfers between devices with their start and end apart: 4, of which 0 were waited for; matrix products, arithmetic and copies ran while one was open for 11% of the time, Pallas kernels for 34%

profile of v4, /device:TPU:0, one launch (start us, length us, event | category | flops | bytes accessed | tf_op | source)
XLA Modules:
  0.0 841.4 jit_solution(15141666695447013727)
XLA Ops:
  9.6 3.0 collective-permute-start
  19.9 16.3 %shard_map.527 = bf16[4,2,2,64,384]{4,3,2,1,0:T(8,128)(2,1)} custom-call(bf16[64,384]{1,0:T(8,128)(2,1)} %fusion.30.own_ref), custom_call_target="tpu_custom_call" | custom-call | bytes 3145728 | tf_op jit(solution)/shard_map/pallas_call | solution.py:1450
  38.0 2.4 convert_element_type.162
  51.1 1.9 multiply_sine_fusion.1
  54.8 2.6 copy.205
  57.5 3.8 reshape.536.refs_8_
  65.3 263.5 %shard_map.528 = (bf16[4,2,2,64,3072]{4,3,2,1,0:T(8,128)(2,1)}, bf16[4,2,2,64,1024]{4,3,2,1,0:T(8,128)(2,1)}, bf16[4,2,2,64,4096]{4,3,2,1,0:T(8,128)(2,1)}, bf16...) custom-call(bf16[64,3072]{1,0:T(8,128)(2,1)} %get-tuple-element.294., ...), custom_call_target="tpu_custom_call" | custom-call | flops 25769803776 | bytes 201326592 | tf_op jit(solution)/shard_map/pallas_call | solution.py:1375
  328.8 1.9 reduce_sum.118
  337.8 1.9 broadcast_add_fusion
  339.7 59.3 %shard_map.529 = (f32[512,1024]{1,0:T(8,128)}, bf16[512,1024]{1,0:T(8,128)(2,1)}, bf16[512,4096]{1,0:T(8,128)(2,1)}, bf16[512,1024]{1,0:T(8,128)(2,1)}, bf16[512...) custom-call(f32[512,1024]{1,0:T(8,128)} %bitcast.155, f32[512,1024]{1,0:T(8,128)} %get-tuple-element.95.refs_1_, ...), custom_call_target="tpu_custom_call" | custom-call | flops 15032385536 | bytes 83886080 | tf_op jit(solution)/shard_map/pallas_call | solution.py:1083
  399.0 59.5 %shard_map.530 = (f32[512,1024]{1,0:T(8,128)}, bf16[512,1024]{1,0:T(8,128)(2,1)}, bf16[512,4096]{1,0:T(8,128)(2,1)}, bf16[512,1024]{1,0:T(8,128)(2,1)}, bf16[512...) custom-call(f32[512,1024]{1,0:T(8,128)} %get-tuple-element.105.refs_0_, ...), custom_call_target="tpu_custom_call" | custom-call | flops 15032385536 | bytes 83886080 | tf_op jit(solution)/shard_map/pallas_call | solution.py:1083
  458.5 2.0 convolution_bitcast_fusion
  463.3 8.2 concatenate.80
  472.2 270.7 %shard_map.531 = f32[24,4,64,256]{3,2,1,0:T(8,128)} custom-call(bf16[512,1024]{1,0:T(8,128)(2,1)} %get-tuple-element.139.refs_0_, bf16[512,1024]{1,0:T(8,128)(2,1)} %get-tuple-element.140.refs_1_, bf16[512,1024]{1,0:T(8,128)(2,1)} %get-tuple-element.141.refs_2_, bf16[512,4096]{1,0:T(8,128)(2,1)} %get-tuple-element.142.refs_3_, ...), custom_call_target="tpu_custom_call" | custom-call | flops 25769803776 | bytes 100663296 | tf_op jit(solution)/shard_map/pallas_call | solution.py:437
  743.0 3.5 slice_bitcast_fusion
  749.9 1.9 copy.198
  770.7 6.3 multiply_subtract_fusion.1
  777.0 3.3 multiply_subtract_fusion.3
  782.7 3.9 multiply_subtract_fusion.2
  791.1 4.9 reshape.532
  796.0 2.2 fusion.59
  798.3 20.9 %all_gather.10 = bf16[64,1024]{0,1:T(8,128)(2,1)S(1)} all-gather(bf16[64,64]{0,1:T(8,128)(2,1)S(1)} %copy.193), channel_id=1, replica_groups=mesh['seq'=2,'dp'=16] {'dp'}, dimensions={1}, use_global_device_ids=true | all-gather | bytes 139264 | tf_op jit(solution)/shard_map/all_gather | solution.py:1738
  821.1 8.5 %multiply_subtract_fusion = (f32[64,14336]{1,0:T(8,128)}, f32[64,14336]{1,0:T(8,128)}, f32[64,14336]{1,0:T(8,128)}) fusion(f32[64,14336]{1,0:T(8,128)} %param.55, f32[64,14336]{1,0:T(8,128)} %param.56, f32[64,14336]{1,0:T(8,128)} %param.57, bf16[64,64]{1,0:T(8,128)(2,1)S(1)} %copy-done.49, bf16[64,14336]{1,0:T(8,128)(2,1)S(1)} %copy-done.8), kind=kOutput, calls=%fused_computation.2 | convolution fusion | flops 131203072 | bytes 23863296 | tf_op jit(solution)/shard_map/dot_general | solution.py:35
  829.6 2.2 convert_reduce_fusion.2
  (275 shorter events, 71.0 us)
Async XLA Ops:
  7.2 30.5 %copy-start.26 = (f32[35872]{0:T(1024)S(1)}, f32[35872]{0:T(1024)}, u32[]{:S(2)}) copy-start(f32[35872]{0:T(1024)} %param.61) | copy-start | bytes 430468
  7.2 779.4 %all-reduce.4.cloned.1.call-start = ((), (), s32[]{:S(2)}) async-start(), calls=%async_computation | async-start | bytes 688128 | tf_op jit(solution)/shard_map/psum | solution.py:1729
  9.6 52.5 %collective-permute-start = (f32[2,128,33]{1,0,2:T(2,128)S(1)}, f32[2,128,33]{1,0,2:T(2,128)}, u32[]{:S(2)}, u32[]{:S(2)}) collective-permute-start(f32[2,128,33]{1,0,2:T(2,128)S(1)} %constant_dynamic-slice_fusion.3), channel_id=1, source_target_pairs={{0,16},{16,0},{1,17},{17,1},{2,18},{18,2},{3,19},{19,3},{4,20},{20... | collective-permute-start | bytes 101384 | tf_op jit(solution)/shard_map/ppermute | solution.py:1602
  38.0 10.5 %copy-start.57 = (s32[64]{0:T(128)}, s32[64]{0:T(128)S(1)}, u32[]{:S(2)}) copy-start(s32[64]{0:T(128)S(1)} %eq.24) | copy-start | bytes 772
  40.7 8.7 %copy-start.1 = (bf16[64,14336]{1,0:T(8,128)(2,1)}, bf16[64,14336]{1,0:T(8,128)(2,1)S(1)}, u32[]{:S(2)}) copy-start(bf16[64,14336]{1,0:T(8,128)(2,1)S(1)} %convert_element_type.162) | copy-start | bytes 5505028
  57.5 6.0 copy-start.52
  471.4 319.6 %all-gather.6.cloned.1.call-start = ((), (), s32[]{:S(2)}) async-start(), calls=%async_computation.2 | async-start | bytes 1892352 | tf_op jit(solution)/shard_map/all_gather | solution.py:1730
  472.2 357.4 %all-gather.4.cloned.1.call-start = ((), (), s32[]{:S(2)}) async-start(), calls=%async_computation.1 | async-start | bytes 2228224 | tf_op jit(solution)/shard_map/all_gather | solution.py:1679
  770.7 6.3 copy-start.11
  770.7 6.3 copy-start.22
  770.7 6.3 copy-start.23
  782.7 7.8 copy-start.39
  782.7 7.8 copy-start.53
  782.7 7.8 copy-start.54
  788.9 7.0 copy-start.2
  789.0 7.0 copy-start.38
  796.0 23.4 %copy-start.31 = (bf16[64,1024]{1,0:T(8,128)(2,1)S(1)}, bf16[64,1024]{1,0:T(8,128)(2,1)}, u32[]{:S(2)}) copy-start(bf16[64,1024]{1,0:T(8,128)(2,1)} %copy-done.30) | copy-start | bytes 393220
  796.0 23.7 %copy-start.35 = (f32[1001,64]{0,1:T(8,128)S(1)}, f32[1001,64]{0,1:T(8,128)}, u32[]{:S(2)}) copy-start(f32[1001,64]{0,1:T(8,128)} %param.40) | copy-start | bytes 768772
  796.0 23.7 %copy-start.58 = (s32[64]{0:T(128)S(1)}, s32[64]{0:T(128)}, u32[]{:S(2)}) copy-start(s32[64]{0:T(128)} %copy-done.57) | copy-start | bytes 772
  796.0 23.7 %copy-start.60 = (f32[1001,64]{0,1:T(8,128)S(1)}, f32[1001,64]{0,1:T(8,128)}, u32[]{:S(2)}) copy-start(f32[1001,64]{0,1:T(8,128)} %param.41) | copy-start | bytes 768772
  796.0 23.7 %copy-start.61 = (f32[1001,64]{0,1:T(8,128)S(1)}, f32[1001,64]{0,1:T(8,128)}, u32[]{:S(2)}) copy-start(f32[1001,64]{0,1:T(8,128)} %param.42) | copy-start | bytes 768772
  798.2 22.8 %copy-start.8 = (bf16[64,14336]{1,0:T(8,128)(2,1)S(1)}, bf16[64,14336]{1,0:T(8,128)(2,1)}, u32[]{:S(2)}) copy-start(bf16[64,14336]{1,0:T(8,128)(2,1)} %reshape.532) | copy-start | bytes 5505028
  798.2 22.8 %copy-start.49 = (bf16[64,64]{1,0:T(8,128)(2,1)S(1)}, bf16[64,64]{1,0:T(8,128)(2,1)}, u32[]{:S(2)}) copy-start(bf16[64,64]{1,0:T(8,128)(2,1)} %copy-done.48) | copy-start | bytes 24580
  821.1 8.5 %copy-start.62 = (f32[64,1024]{1,0:T(8,128)S(1)}, f32[64,1024]{1,0:T(8,128)}, u32[]{:S(2)}) copy-start(f32[64,1024]{1,0:T(8,128)} %get-tuple-element.324) | copy-start | bytes 786436
  (47 other events, 121.3 us)
Sparse Core Ops, SparseCore 0:
  471.6 140.2 all-reduce.3
  615.8 62.4 all-gather.5
  766.5 41.3 all-gather.3

commit v5 on v4

--- a/solution.py
+++ b/solution.py
@@ -30,45 +30,6 @@
 RATE_TABLE = 0.4
 RATE_BIAS = 0.2
 
-
-def matdot(left, right):
-    return jnp.dot(left, right, preferred_element_type=jnp.float32)
-
-
-def layer_norm(stream):
-    row_mean = jnp.mean(stream, axis=-1, keepdims=True)
-    centered = stream - row_mean
-    variance = jnp.mean(centered * centered, axis=-1, keepdims=True)
-    return centered * lax.rsqrt(variance + 1e-06)
-
-
-def modulate(stream, shift_by, scale_by):
-    return layer_norm(stream) * (1.0 + scale_by[:, None, :]) + shift_by[:, None, :]
-
-
-def position_table(position_ids, feature_width, grid_side):
-    quarter_width = feature_width // 4
-    omegas = 1.0 / 10000.0 ** (jnp.arange(quarter_width, dtype=jnp.float32) / quarter_width)
-    col_angle = (position_ids % grid_side).astype(jnp.float32)[:, None] * omegas[None, :]
-    row_angle = (position_ids // grid_side).astype(jnp.float32)[:, None] * omegas[None, :]
-    return jnp.concatenate(
-        [jnp.sin(col_angle), jnp.cos(col_angle), jnp.sin(row_angle), jnp.cos(row_angle)], axis=1
-    )
-
-
-def time_features(timesteps, feature_width):
-    half_width = feature_width // 2
-    frequencies = jnp.exp(
-        -math.log(10000.0) * jnp.arange(half_width, dtype=jnp.float32) / half_width
-    )
-    angles = timesteps.astype(jnp.float32)[:, None] * frequencies[None, :]
-    return jnp.concatenate([jnp.cos(angles), jnp.sin(angles)], axis=1)
-
-
-def column_sum(grad_bf):
-    return jnp.sum(grad_bf.astype(jnp.float32), axis=0)
-
-
 MESH = pl.DeviceIdType.MESH
 TILE = 256
 PARTS = 4
@@ -81,374 +42,42 @@
 BACKWARD_STEPS = 27
 
 
-def scatter_kernel(
-    per_layer,
-    total,
-    lines,
-    *refs,
-):
-    count = 8 * LAYERS
-    sources = [refs[8 * layer : 8 * layer + 8] for layer in range(LAYERS)]
-    (
-    out_ref,
-    lhs_buf,
-    act_buf,
-    wide_buf,
-    down_buf,
-    load_sem,
-    made,
-    core_in,
-    x_out,
-    x_in,
-    p_keep,
-    yq_out,
-    yq_in,
-    q_keep,
-    yp_out,
-    yp_in,
-    p_line,
-    zq_out,
-    zq_in,
-    zp_out,
-    zp_in,
-    xq_out,
-    xq_in,
-    xp_out,
-    xp_in,
-    core_sem,
-    x_sem,
-    yq_sem,
-    yp_sem,
-    zq_sem,
-    zp_sem,
-    xq_sem,
-    xp_sem,
-    ) = refs[count:]
-    seq = lax.axis_index("seq")
-    dp = lax.axis_index("dp")
-    core = lax.rem(dp, 2)
-    why = lax.rem(dp // 2, 2)
-    zed = dp // 4
-    core_peer = {"seq": seq, "dp": dp + 1 - 2 * core}
-    x_peer = {"seq": 1 - seq, "dp": dp}
-    y_peer = {"seq": seq, "dp": dp + 2 - 4 * why}
-
-    def z_place(step):
-        return lax.rem(zed + step, lines)
-
-    def z_peer(step):
-        return {"seq": seq, "dp": z_place(step) * 4 + 2 * why + core}
-
-    barrier = pltpu.get_barrier_semaphore()
-    for peer in [core_peer, x_peer, y_peer] + [z_peer(step) for step in range(1, lines)]:
-        pl.semaphore_signal(barrier, inc=1, device_id=peer, device_id_type=MESH)
-    pl.semaphore_wait(barrier, 2 + lines)
-
-    def remote(source, target, sems, peer):
-        return pltpu.make_async_remote_copy(
-            src_ref=source,
-            dst_ref=target,
-            send_sem=sems.at[0],
-            recv_sem=sems.at[1],
-            device_id=peer,
-            device_id_type=MESH,
-        )
-
-    def core_copy(slot):
-        return remote(made.at[slot, 1 - core], core_in.at[slot], core_sem.at[slot], core_peer)
-
-    def x_copy(slot):
-        return remote(x_out.at[slot], x_in.at[slot], x_sem.at[slot], x_peer)
-
-    def yq_copy(slot):
-        return remote(yq_out.at[slot], yq_in.at[slot], yq_sem.at[slot], y_peer)
-
-    def yp_copy(slot):
-        return remote(yp_out.at[slot], yp_in.at[slot], yp_sem.at[slot], y_peer)
-
-    def zq_copy(slot, step):
-        return remote(
-            zq_out.at[slot, z_place(step)],
-            zq_in.at[slot, step - 1],
-            zq_sem.at[slot, step - 1],
-            z_peer(step),
-        )
-
-    def zp_copy(slot, step):
-        return remote(
-            zp_out.at[slot, z_place(step)],
-            zp_in.at[slot, step - 1],
-            zp_sem.at[slot, step - 1],
-            z_peer(step),
-        )
-
-    def xq_copy(slot):
-        return remote(xq_out.at[slot], xq_in.at[slot], xq_sem.at[slot], x_peer)
-
-    def xp_copy(slot):
-        return remote(xp_out.at[slot], xp_in.at[slot], xp_sem.at[slot], x_peer)
-
-    def loads(unit, slot):
-        found = []
-        for layer in range(LAYERS):
-            merged, a_one, a_two, act, d_attn, d_qkv, d_up, d_down = sources[layer]
-            at = unit - layer * per_layer
-
-            def slab(ref, index, size):
-                return ref.at[:, pl.ds(pl.multiple_of(index * size, size), size)]
-
-            wide_to = wide_buf.at[slot], load_sem.at[1, slot]
-            lhs_to = lhs_buf.at[slot], load_sem.at[0, slot]
-            found += [
-                (at == 0, (merged, *lhs_to), (d_attn, *wide_to)),
-                (
-                    jnp.logical_and(at >= 1, at < 4),
-                    (a_one, *lhs_to),
-                    (slab(d_qkv, at - 1, D), *wide_to),
-                ),
-                (
-                    jnp.logical_and(at >= 4, at < 8),
-                    (a_two, *lhs_to),
-                    (slab(d_up, at - 4, D), *wide_to),
-                ),
-                (
-                    jnp.logical_and(at >= 8, at < per_layer),
-                    (slab(d_down, at - 8, TILE), down_buf.at[slot], load_sem.at[2, slot]),
-                ),
-                (at == 8, (act, act_buf, load_sem.at[3, 0])),
-            ]
-        return found
-
-    def prefetch(unit):
-        for due, *moves in loads(unit, lax.rem(unit, 2)):
-
-            @pl.when(due)
-            def _():
-                for move in moves:
-                    pltpu.make_async_copy(*move).start()
-
-    def fetched(unit):
-        for due, *moves in loads(unit, lax.rem(unit, 2)):
-
-            @pl.when(due)
-            def _():
-                for move in moves:
-                    pltpu.make_async_copy(*move).wait()
-
-    def dot_rows(left, right):
-        return lax.dot_general(
-            left, right, (((0,), (0,)), ((), ())), preferred_element_type=jnp.float32
-        )
-
-    def compute(unit):
-        at = lax.rem(unit, per_layer)
-        slot = lax.rem(unit, 2)
-        fetched(unit)
-
-        @pl.when(at < 8)
-        def _():
-            def rows(pair, carry):
-                left = lhs_buf[slot, :, pl.ds(pl.multiple_of(pair * 128, 128), 128)]
-                block = dot_rows(left, wide_buf[slot]).astype(jnp.bfloat16)
-                for own in range(2):
-                    for part in range(PARTS):
-                        made[slot, own, part, pair // 2, lax.rem(pair, 2)] = block[
-                            own * 64 : own * 64 + 64, part * TILE : part * TILE + TILE
-                        ]
-                return carry
-
-            lax.fori_loop(0, 2 * lines, rows, 0)
-
-        @pl.when(at >= 8)
-        def _():
-            def rows(pair, carry):
-                left = act_buf[:, pl.ds(pl.multiple_of(pair * 512, 512), 512)]
-                block = dot_rows(left, down_buf[slot]).astype(jnp.bfloat16)
-                for own in range(2):
-                    for part in range(PARTS):
-                        first = own * 256 + part * 64
-                        made[slot, own, part, pair // 2, lax.rem(pair, 2)] = block[
-                            first : first + 64
-                        ]
-                return carry
-
-            lax.fori_loop(0, 2 * lines, rows, 0)
-
-    def wide_sum(one, other):
-        return one.astype(jnp.float32) + other.astype(jnp.float32)
-
-    def stage_two(slot):
-        core_copy(slot).wait()
-
-        def rows(line, carry):
-            for side in range(2):
-                x_out[slot, line, side] = wide_sum(
-                    made[slot, core, 1 - seq, line, side], core_in[slot, 1 - seq, line, side]
-                ).astype(jnp.bfloat16)
-                p_keep[slot, line, side] = wide_sum(
-                    made[slot, core, seq, line, side], core_in[slot, seq, line, side]
-                ).astype(jnp.bfloat16)
-            for part in range(2):
-                yq_out[slot, line, part] = wide_sum(
-                    made[slot, core, 2 + part, line, 1 - why],
-                    core_in[slot, 2 + part, line, 1 - why],
-                ).astype(jnp.bfloat16)
-                q_keep[slot, line, part] = wide_sum(
-                    made[slot, core, 2 + part, line, why], core_in[slot, 2 + part, line, why]
-                ).astype(jnp.bfloat16)
-            return carry
-
-        lax.fori_loop(0, lines, rows, 0)
-        x_copy(slot).start()
-        yq_copy(slot).start()
-
-    def stage_three(slot):
-        x_copy(slot).wait()
-        yq_copy(slot).wait()
-
-        def rows(line, carry):
-            yp_out[slot, line] = wide_sum(
-                p_keep[slot, line, 1 - why], x_in[slot, line, 1 - why]
-            ).astype(jnp.bfloat16)
-            p_line[slot, line] = wide_sum(p_keep[slot, line, why], x_in[slot, line, why]).astype(
-                jnp.bfloat16
-            )
-            for part in range(2):
-                zq_out[slot, line, part] = wide_sum(
-                    q_keep[slot, line, part], yq_in[slot, line, part]
-                ).astype(jnp.bfloat16)
-            return carry
-
-        lax.fori_loop(0, lines, rows, 0)
-        yp_copy(slot).start()
-        for step in range(1, lines):
-            zq_copy(slot, step).start()
-
-    def stage_four(slot):
-        yp_copy(slot).wait()
-        for step in range(1, lines):
-            zq_copy(slot, step).wait()
-
-        def rows(line, carry):
-            zp_out[slot, line] = wide_sum(p_line[slot, line], yp_in[slot, line]).astype(
-                jnp.bfloat16
-            )
-            return carry
-
-        lax.fori_loop(0, lines, rows, 0)
-        total_q = zq_out[slot, zed].astype(jnp.float32)
-        for step in range(1, lines):
-            total_q = total_q + zq_in[slot, step - 1].astype(jnp.float32)
-        xq_out[slot] = total_q.astype(jnp.bfloat16)
-        for step in range(1, lines):
-            zp_copy(slot, step).start()
-        xq_copy(slot).start()
-
-    def stage_five(unit, slot):
-        for step in range(1, lines):
-            zp_copy(slot, step).wait()
-        xq_copy(slot).wait()
-        total_p = zp_out[slot, zed].astype(jnp.float32)
-        for step in range(1, lines):
-            total_p = total_p + zp_in[slot, step - 1].astype(jnp.float32)
-        rounded = total_p.astype(jnp.bfloat16)
-        xp_out[slot] = rounded
-        xp_copy(slot).start()
-        out_ref[unit, seq] = rounded.astype(jnp.float32)
-        for part in range(2):
-            out_ref[unit, 2 + part] = wide_sum(xq_out[slot, part], xq_in[slot, part])
-
-    def stage_six(unit, slot):
-        xp_copy(slot).wait()
-        out_ref[unit, 1 - seq] = xp_in[slot].astype(jnp.float32)
-
-    prefetch(jnp.int32(0))
-
-    def turn(at, carry):
-        def when_due(behind, run):
-            unit = at - behind
-
-            @pl.when(jnp.logical_and(unit >= 0, unit < total))
-            def _():
-                run(unit, lax.rem(unit, 2))
-
-        prefetch(at + 1)
-        when_due(5, stage_six)
-        when_due(4, stage_five)
-        when_due(3, lambda unit, slot: stage_four(slot))
-        when_due(2, lambda unit, slot: stage_three(slot))
-        when_due(1, lambda unit, slot: stage_two(slot))
-
-        @pl.when(at < total)
-        def _():
-            compute(at)
-            core_copy(lax.rem(at, 2)).start()
-
-        return carry
-
-    lax.fori_loop(0, total + 5, turn, 0)
-
-
-def scatter_sums(operands, lines):
-    toks, hidden = operands[3].shape
-    width = D
-    per_layer = 12
-    total = LAYERS * per_layer
-    bf = jnp.bfloat16
-    dma = pltpu.SemaphoreType.DMA
-
-    def buf(*shape):
-        return pltpu.VMEM((2,) + shape, bf)
-
-    scratch = [
-        buf(toks, width),
-        pltpu.VMEM((toks, hidden), bf),
-        buf(toks, width),
-        buf(toks, TILE),
-        dma((4, 2)),
-        buf(2, PARTS, lines, 2, 64, TILE),
-        buf(PARTS, lines, 2, 64, TILE),
-        buf(lines, 2, 64, TILE),
-        buf(lines, 2, 64, TILE),
-        buf(lines, 2, 64, TILE),
-        buf(lines, 2, 64, TILE),
-        buf(lines, 2, 64, TILE),
-        buf(lines, 2, 64, TILE),
-        buf(lines, 64, TILE),
-        buf(lines, 64, TILE),
-        buf(lines, 64, TILE),
-        buf(lines, 2, 64, TILE),
-        buf(lines - 1, 2, 64, TILE),
-        buf(lines, 64, TILE),
-        buf(lines - 1, 64, TILE),
-        buf(2, 64, TILE),
-        buf(2, 64, TILE),
-        buf(64, TILE),
-        buf(64, TILE),
-        dma((2, 2)),
-        dma((2, 2)),
-        dma((2, 2)),
-        dma((2, 2)),
-        dma((2, lines - 1, 2)),
-        dma((2, lines - 1, 2)),
-        dma((2, 2)),
-        dma((2, 2)),
-    ]
-    return pl.pallas_call(
-        functools.partial(scatter_kernel, per_layer, total, lines),
-        out_shape=jax.ShapeDtypeStruct((total, PARTS, 64, TILE), jnp.float32),
-        in_specs=[pl.BlockSpec(memory_space=pl.ANY)] * len(operands),
-        out_specs=pl.BlockSpec(memory_space=pltpu.VMEM),
-        scratch_shapes=scratch,
-        compiler_params=pltpu.CompilerParams(
-            collective_id=1, has_side_effects=True, vmem_limit_bytes=56 * 1024 * 1024
-        ),
-        cost_estimate=pl.CostEstimate(
-            flops=2 * total * toks * width * width,
-            bytes_accessed=total * 4 * 1024 * 1024,
-            transcendentals=0,
-        ),
-    )(*operands)
+def matdot(left, right):
+    return jnp.dot(left, right, preferred_element_type=jnp.float32)
+
+
+def layer_norm(stream):
+    row_mean = jnp.mean(stream, axis=-1, keepdims=True)
+    centered = stream - row_mean
+    variance = jnp.mean(centered * centered, axis=-1, keepdims=True)
+    return centered * lax.rsqrt(variance + 1e-06)
+
+
+def modulate(stream, shift_by, scale_by):
+    return layer_norm(stream) * (1.0 + scale_by[:, None, :]) + shift_by[:, None, :]
+
+
+def position_table(position_ids, feature_width, grid_side):
+    quarter_width = feature_width // 4
+    omegas = 1.0 / 10000.0 ** (jnp.arange(quarter_width, dtype=jnp.float32) / quarter_width)
+    col_angle = (position_ids % grid_side).astype(jnp.float32)[:, None] * omegas[None, :]
+    row_angle = (position_ids // grid_side).astype(jnp.float32)[:, None] * omegas[None, :]
+    return jnp.concatenate(
+        [jnp.sin(col_angle), jnp.cos(col_angle), jnp.sin(row_angle), jnp.cos(row_angle)], axis=1
+    )
+
+
+def time_features(timesteps, feature_width):
+    half_width = feature_width // 2
+    frequencies = jnp.exp(
+        -math.log(10000.0) * jnp.arange(half_width, dtype=jnp.float32) / half_width
+    )
+    angles = timesteps.astype(jnp.float32)[:, None] * frequencies[None, :]
+    return jnp.concatenate([jnp.cos(angles), jnp.sin(angles)], axis=1)
+
+
+def column_sum(grad_bf):
+    return jnp.sum(grad_bf.astype(jnp.float32), axis=0)
 
 
 def dot_nn(left, right):
@@ -776,28 +405,30 @@
     )(x, mods, biases, keep, *grouped(weights))
 
 
-def backward_pieces(refs, mod_at):
+def backward_pieces(ins, outs, scratch, mod_at):
     (
-        grad_ref,
-        x_ref,
-        x_one_ref,
-        attn_ref,
-        down_ref,
-        qkv_ref,
-        mod_ref,
-        keep_ref,
+        x_hbm,
+        x_one_hbm,
+        attn_hbm,
+        down_hbm,
+        qkv_hbm,
         pre_hbm,
         w_qkv,
         w_proj,
         w_up,
         w_down,
-        d_x_out,
-        d_down_out,
-        d_up_out,
-        d_attn_out,
-        d_qkv_out,
+        mod_ref,
+        keep_ref,
+    ) = ins
+    d_down_out, d_up_out, d_attn_out, d_qkv_out = outs
+    (
         d_mod_ref,
         d_bias_ref,
+        grad_ref,
+        side_ref,
+        x_one_ref,
+        attn_ref,
+        qkv_ref,
         total_buf,
         d_x_one_buf,
         d_down_buf,
@@ -811,7 +442,8 @@
         load_sem,
         tile_sem,
         save_sem,
-    ) = refs
+        in_sem,
+    ) = scratch
     images, toks = keep_ref.shape
     bf = jnp.bfloat16
     blocks = toks // 64
@@ -822,10 +454,26 @@
                 (d_down_buf, d_down_out),
                 (d_attn_buf, d_attn_out),
                 (d_qkv_buf, d_qkv_out),
-                (total_buf, d_x_out),
             ]
         )
     ]
+
+    in_down, in_x_one, in_attn, in_qkv, in_x = [
+        pltpu.make_async_copy(source, target, in_sem.at[at])
+        for at, (source, target) in enumerate(
+            [
+                (down_hbm, side_ref),
+                (x_one_hbm, x_one_ref),
+                (attn_hbm, attn_ref),
+                (qkv_hbm, qkv_ref),
+                (x_hbm, side_ref),
+            ]
+        )
+    ]
+
+    def begin():
+        for copy in (in_down, in_x_one, in_attn, in_qkv):
+            copy.start()
 
     def wide_load(source, tile, slot):
         return pltpu.make_async_copy(
@@ -884,7 +532,8 @@
 
         zero = jnp.zeros((1, D), jnp.float32)
         gate, bias = lax.fori_loop(0, blocks, rows_of, (zero, zero))
-        d_mod_ref[gate_row + image : gate_row + image + 1, :] = gate
+        gate_at = mod_at + gate_row + image
+        d_mod_ref[gate_at : gate_at + 1, :] = gate
         if image == 0:
             d_bias_ref[:, bias_cols] = bias
         else:
@@ -908,8 +557,9 @@
 
         zero = jnp.zeros((1, D), jnp.float32)
         shift, scale = lax.fori_loop(0, blocks, rows_of, (zero, zero))
-        d_mod_ref[first_row + image : first_row + image + 1, :] = shift
-        d_mod_ref[first_row + 2 + image : first_row + 3 + image, :] = scale
+        shift_at = mod_at + first_row + image
+        d_mod_ref[shift_at : shift_at + 1, :] = shift
+        d_mod_ref[shift_at + 2 : shift_at + 3, :] = scale
 
     def attend_back(image, pair):
         rows = pl.ds(pl.multiple_of(image * toks, toks), toks)
@@ -953,18 +603,14 @@
 
         @pl.when(at == 0)
         def _():
+            in_down.wait()
             for image in range(images):
-                gated(image, 10, grad_ref, down_ref, d_down_buf, slice(8 * D, 9 * D))
+                gated(image, 10, grad_ref, side_ref, d_down_buf, slice(8 * D, 9 * D))
             saves[0].start()
 
         @pl.when(within(at, 1, 8))
         def _():
             tile = at - 1
-
-            @pl.when(tile >= 2)
-            def _():
-                up_save(tile - 2, slot).wait()
-
             bias = jnp.zeros((1, HALF), jnp.float32)
             for image in range(images):
                 rows = pl.ds(image * toks, toks)
@@ -982,8 +628,19 @@
             d_bias_ref[:, column_tile(tile + 8)] = bias
             up_save(tile, slot).start()
 
+            @pl.when(tile == 0)
+            def _():
+                saves[0].wait()
+
+            @pl.when(tile >= 1)
+            def _():
+                up_save(tile - 1, 1 - slot).wait()
+
         @pl.when(at == 9)
         def _():
+            up_save(7, 0).wait()
+            in_x_one.wait()
+            in_attn.wait()
             for image in range(images):
                 modulate_back(image, 6, x_one_ref, grad_ref, d_x_one_buf)
                 gated(image, 4, d_x_one_buf, attn_ref, d_attn_buf, slice(3 * D, 4 * D))
@@ -996,8 +653,14 @@
                 part = dot_nt(d_attn_buf[rows, column_tile(at - 10)], wide_tile(slot))
                 add_product(at == 10, rows, part)
 
+            @pl.when(at == 10)
+            def _():
+                in_x.start()
+                saves[1].wait()
+
             @pl.when(at == 11)
             def _():
+                in_qkv.wait()
                 d_heads_buf[...] = total_buf[...].astype(bf)
 
         @pl.when(within(at, 12, 8))
@@ -1021,33 +684,30 @@
                 add_product(at == 20, rows, dot_nt(lower, wide_tile(slot)))
             d_bias_ref[:, cols] = bias
 
+            @pl.when(at == 21)
+            def _():
+                saves[2].wait()
+
         @pl.when(at == BACKWARD_STEPS - 1)
         def _():
+            in_x.wait()
             for image in range(images):
-                modulate_back(image, 0, x_ref, d_x_one_buf, total_buf)
-            saves[3].start()
-
-    def finish():
-        for tile in (6, 7):
-            up_save(tile, tile % 2).wait()
-        for copy in saves:
-            copy.wait()
-
-    return step, finish
-
-
-BACKWARD_OUTS = [
-    (D, jnp.float32),
-    (D, jnp.bfloat16),
-    (FF, jnp.bfloat16),
-    (D, jnp.bfloat16),
-    (3 * D, jnp.bfloat16),
-]
+                modulate_back(image, 0, side_ref, d_x_one_buf, grad_ref)
+
+    return begin, step
+
+
+BACKWARD_OUTS = [(D, jnp.bfloat16), (FF, jnp.bfloat16), (D, jnp.bfloat16), (3 * D, jnp.bfloat16)]
 
 
 def backward_scratch(toks):
     bf, f32 = jnp.bfloat16, jnp.float32
     return [
+        pltpu.VMEM((toks, D), f32),
+        pltpu.VMEM((toks, D), f32),
+        pltpu.VMEM((toks, D), f32),
+        pltpu.VMEM((toks, D), f32),
+        pltpu.VMEM((toks, 3 * D), bf),
         pltpu.VMEM((toks, D), f32),
         pltpu.VMEM((toks, D), f32),
         pltpu.VMEM((toks, D), bf),
@@ -1060,23 +720,38 @@
         pltpu.VMEM((2, 2, 256, D), bf),
         pltpu.SemaphoreType.DMA((3, 2)),
         pltpu.SemaphoreType.DMA((2,)),
-        pltpu.SemaphoreType.DMA((4,)),
+        pltpu.SemaphoreType.DMA((3,)),
+        pltpu.SemaphoreType.DMA((5,)),
     ]
 
 
 def backward_kernel(mod_at, *refs):
-    step, finish = backward_pieces(refs, mod_at)
+    grad_in, ins, outs = refs[0], refs[1:13], refs[13:17]
+    d_x_out, d_mod_ref, d_bias_ref = refs[17:20]
+    scratch, sem = refs[20:-1], refs[-1]
+    begin, step = backward_pieces(ins, outs, (d_mod_ref, d_bias_ref) + scratch, mod_at)
+    begin()
+    copy = pltpu.make_async_copy(grad_in, scratch[0], sem.at[0])
+    copy.start()
+    copy.wait()
 
     def turn(at, carry):
         step(at)
         return carry
 
     lax.fori_loop(0, BACKWARD_STEPS, turn, 0)
-    finish()
+    copy = pltpu.make_async_copy(scratch[0], d_x_out, sem.at[1])
+    copy.start()
+    copy.wait()
+
+
+def backward_operands(x, saved, weights):
+    _, qkv, _, attn, x_one, _, pre, _, down, _ = saved
+    return (x, x_one, attn, down, qkv, pre, *weights)
 
 
 def backward_layer(grad, x, saved, mods, mod_at, keep, weights):
-    a_one, qkv, merged, attn, x_one, a_two, pre, act, down, _ = saved
+    a_one, _, merged, _, _, a_two, _, act, _, _ = saved
     toks = x.shape[0]
     vmem = pl.BlockSpec(memory_space=pltpu.VMEM)
     hbm = pl.BlockSpec(memory_space=pl.ANY)
@@ -1084,20 +759,21 @@
         functools.partial(backward_kernel, mod_at),
         out_shape=[jax.ShapeDtypeStruct((toks, width), kind) for width, kind in BACKWARD_OUTS]
         + [
-            jax.ShapeDtypeStruct((12, D), jnp.float32),
+            jax.ShapeDtypeStruct((toks, D), jnp.float32),
+            jax.ShapeDtypeStruct((mod_at + 12, D), jnp.float32),
             jax.ShapeDtypeStruct((1, 9 * D), jnp.float32),
         ],
-        in_specs=[vmem] * 8 + [hbm] * 5,
-        out_specs=[hbm] * len(BACKWARD_OUTS) + [vmem] * 2,
-        scratch_shapes=backward_scratch(toks),
+        in_specs=[hbm] * 11 + [vmem] * 2,
+        out_specs=[hbm] * 5 + [vmem] * 2,
+        scratch_shapes=backward_scratch(toks) + [pltpu.SemaphoreType.DMA((2,))],
         compiler_params=pltpu.CompilerParams(vmem_limit_bytes=56 * 1024 * 1024),
         cost_estimate=pl.CostEstimate(
             flops=28 * toks * D * D, bytes_accessed=80 * 1024 * 1024, transcendentals=4 * toks * D
         ),
-    )(grad, x, x_one, attn, down, qkv, mods, keep, pre, *grouped(weights))
-    d_x, d_down, d_up, d_attn, d_qkv, d_mod, d_bias = outs
+    )(grad, *backward_operands(x, saved, grouped(weights)), mods, keep)
+    d_down, d_up, d_attn, d_qkv, d_x, d_mod, d_bias = outs
     factors = (merged, a_one, a_two, act, d_attn, d_qkv, d_up, d_down)
-    return d_x, d_mod, factors, d_bias
+    return d_x, d_mod[mod_at:], factors, d_bias
 
 
 def gather_pieces(lines, refs):
@@ -1461,6 +1137,654 @@
     return every.reshape(-1, own.shape[-1])
 
 
+def scatter_pieces(lines, sources, scratch):
+    per_layer = 12
+    total = len(sources) * per_layer
+    (
+    out_ref,
+    lhs_buf,
+    act_buf,
+    wide_buf,
+    down_buf,
+    load_sem,
+    made,
+    core_in,
+    x_out,
+    x_in,
+    p_keep,
+    yq_out,
+    yq_in,
+    q_keep,
+    yp_out,
+    yp_in,
+    p_line,
+    zq_out,
+    zq_in,
+    zp_out,
+    zp_in,
+    xq_out,
+    xq_in,
+    xp_out,
+    xp_in,
+    core_sem,
+    x_sem,
+    yq_sem,
+    yp_sem,
+    zq_sem,
+    zp_sem,
+    xq_sem,
+    xp_sem,
+    out_buf,
+    out_sem,
+    ) = scratch
+    seq = lax.axis_index("seq")
+    dp = lax.axis_index("dp")
+    core = lax.rem(dp, 2)
+    why = lax.rem(dp // 2, 2)
+    zed = dp // 4
+    core_peer = {"seq": seq, "dp": dp + 1 - 2 * core}
+    x_peer = {"seq": 1 - seq, "dp": dp}
+    y_peer = {"seq": seq, "dp": dp + 2 - 4 * why}
+
+    def z_place(step):
+        return lax.rem(zed + step, lines)
+
+    def z_peer(step):
+        return {"seq": seq, "dp": z_place(step) * 4 + 2 * why + core}
+
+    def remote(source, target, sems, peer):
+        return pltpu.make_async_remote_copy(
+            src_ref=source,
+            dst_ref=target,
+            send_sem=sems.at[0],
+            recv_sem=sems.at[1],
+            device_id=peer,
+            device_id_type=MESH,
+        )
+
+    def core_copy(slot):
+        return remote(made.at[slot, 1 - core], core_in.at[slot], core_sem.at[slot], core_peer)
+
+    def x_copy(slot):
+        return remote(x_out.at[slot], x_in.at[slot], x_sem.at[slot], x_peer)
+
+    def yq_copy(slot):
+        return remote(yq_out.at[slot], yq_in.at[slot], yq_sem.at[slot], y_peer)
+
+    def yp_copy(slot):
+        return remote(yp_out.at[slot], yp_in.at[slot], yp_sem.at[slot], y_peer)
+
+    def zq_copy(slot, step):
+        return remote(
+            zq_out.at[slot, z_place(step)],
+            zq_in.at[slot, step - 1],
+            zq_sem.at[slot, step - 1],
+            z_peer(step),
+        )
+
+    def zp_copy(slot, step):
+        return remote(
+            zp_out.at[slot, z_place(step)],
+            zp_in.at[slot, step - 1],
+            zp_sem.at[slot, step - 1],
+            z_peer(step),
+        )
+
+    def xq_copy(slot):
+        return remote(xq_out.at[slot], xq_in.at[slot], xq_sem.at[slot], x_peer)
+
+    def xp_copy(slot):
+        return remote(xp_out.at[slot], xp_in.at[slot], xp_sem.at[slot], x_peer)
+
+    def loads(unit, slot):
+        found = []
+        for layer in range(len(sources)):
+            merged, a_one, a_two, act, d_attn, d_qkv, d_up, d_down = sources[layer]
+            at = unit - layer * per_layer
+
+            def slab(ref, index, size):
+                return ref.at[:, pl.ds(pl.multiple_of(index * size, size), size)]
+
+            wide_to = wide_buf.at[slot], load_sem.at[1, slot]
+            lhs_to = lhs_buf.at[slot], load_sem.at[0, slot]
+            found += [
+                (
+                    jnp.logical_and(at >= 0, at < 4),
+                    (slab(d_down, at, TILE), down_buf.at[slot], load_sem.at[2, slot]),
+                ),
+                (at == 0, (act, act_buf, load_sem.at[3, 0])),
+                (
+                    jnp.logical_and(at >= 4, at < 8),
+                    (a_two, *lhs_to),
+                    (slab(d_up, at - 4, D), *wide_to),
+                ),
+                (at == 8, (merged, *lhs_to), (d_attn, *wide_to)),
+                (
+                    jnp.logical_and(at >= 9, at < per_layer),
+                    (a_one, *lhs_to),
+                    (slab(d_qkv, at - 9, D), *wide_to),
+                ),
+            ]
+        return found
+
+    def prefetch(unit):
+        for due, *moves in loads(unit, lax.rem(unit, 2)):
+
+            @pl.when(due)
+            def _():
+                for move in moves:
+                    pltpu.make_async_copy(*move).start()
+
+    def fetched(unit):
+        for due, *moves in loads(unit, lax.rem(unit, 2)):
+
+            @pl.when(due)
+            def _():
+                for move in moves:
+                    pltpu.make_async_copy(*move).wait()
+
+    def dot_rows(left, right):
+        return lax.dot_general(
+            left, right, (((0,), (0,)), ((), ())), preferred_element_type=jnp.float32
+        )
+
+    def compute(unit):
+        at = lax.rem(unit, per_layer)
+        slot = lax.rem(unit, 2)
+        fetched(unit)
+
+        @pl.when(at >= 4)
+        def _():
+            def rows(pair, carry):
+                left = lhs_buf[slot, :, pl.ds(pl.multiple_of(pair * 128, 128), 128)]
+                block = dot_rows(left, wide_buf[slot]).astype(jnp.bfloat16)
+                for own in range(2):
+                    for part in range(PARTS):
+                        made[slot, own, part, pair // 2, lax.rem(pair, 2)] = block[
+                            own * 64 : own * 64 + 64, part * TILE : part * TILE + TILE
+                        ]
+                return carry
+
+            lax.fori_loop(0, 2 * lines, rows, 0)
+
+        @pl.when(at < 4)
+        def _():
+            def rows(pair, carry):
+                left = act_buf[:, pl.ds(pl.multiple_of(pair * 512, 512), 512)]
+                block = dot_rows(left, down_buf[slot]).astype(jnp.bfloat16)
+                for own in range(2):
+                    for part in range(PARTS):
+                        first = own * 256 + part * 64
+                        made[slot, own, part, pair // 2, lax.rem(pair, 2)] = block[
+                            first : first + 64
+                        ]
+                return carry
+
+            lax.fori_loop(0, 2 * lines, rows, 0)
+
+    def wide_sum(one, other):
+        return one.astype(jnp.float32) + other.astype(jnp.float32)
+
+    def out_copy(unit, slot):
+        return pltpu.make_async_copy(out_buf.at[slot], out_ref.at[unit], out_sem.at[slot])
+
+    def stage_two(slot):
+        core_copy(slot).wait()
+
+        def rows(line, carry):
+            for side in range(2):
+                x_out[slot, line, side] = wide_sum(
+                    made[slot, core, 1 - seq, line, side], core_in[slot, 1 - seq, line, side]
+                ).astype(jnp.bfloat16)
+                p_keep[slot, line, side] = wide_sum(
+                    made[slot, core, seq, line, side], core_in[slot, seq, line, side]
+                ).astype(jnp.bfloat16)
+            for part in range(2):
+                yq_out[slot, line, part] = wide_sum(
+                    made[slot, core, 2 + part, line, 1 - why],
+                    core_in[slot, 2 + part, line, 1 - why],
+                ).astype(jnp.bfloat16)
+                q_keep[slot, line, part] = wide_sum(
+                    made[slot, core, 2 + part, line, why], core_in[slot, 2 + part, line, why]
+                ).astype(jnp.bfloat16)
+            return carry
+
+        lax.fori_loop(0, lines, rows, 0)
+        x_copy(slot).start()
+        yq_copy(slot).start()
+
+    def stage_three(slot):
+        x_copy(slot).wait()
+        yq_copy(slot).wait()
+
+        def rows(line, carry):
+            yp_out[slot, line] = wide_sum(
+                p_keep[slot, line, 1 - why], x_in[slot, line, 1 - why]
+            ).astype(jnp.bfloat16)
+            p_line[slot, line] = wide_sum(p_keep[slot, line, why], x_in[slot, line, why]).astype(
+                jnp.bfloat16
+            )
+            for part in range(2):
+                zq_out[slot, line, part] = wide_sum(
+                    q_keep[slot, line, part], yq_in[slot, line, part]
+                ).astype(jnp.bfloat16)
+            return carry
+
+        lax.fori_loop(0, lines, rows, 0)
+        yp_copy(slot).start()
+        for step in range(1, lines):
+            zq_copy(slot, step).start()
+
+    def stage_four(slot):
+        yp_copy(slot).wait()
+        for step in range(1, lines):
+            zq_copy(slot, step).wait()
+
+        def rows(line, carry):
+            zp_out[slot, line] = wide_sum(p_line[slot, line], yp_in[slot, line]).astype(
+                jnp.bfloat16
+            )
+            return carry
+
+        lax.fori_loop(0, lines, rows, 0)
+        total_q = zq_out[slot, zed].astype(jnp.float32)
+        for step in range(1, lines):
+            total_q = total_q + zq_in[slot, step - 1].astype(jnp.float32)
+        xq_out[slot] = total_q.astype(jnp.bfloat16)
+        for step in range(1, lines):
+            zp_copy(slot, step).start()
+        xq_copy(slot).start()
+
+    def stage_five(unit, slot):
+        for step in range(1, lines):
+            zp_copy(slot, step).wait()
+        xq_copy(slot).wait()
+        total_p = zp_out[slot, zed].astype(jnp.float32)
+        for step in range(1, lines):
+            total_p = total_p + zp_in[slot, step - 1].astype(jnp.float32)
+        rounded = total_p.astype(jnp.bfloat16)
+        xp_out[slot] = rounded
+        xp_copy(slot).start()
+        @pl.when(unit >= 2)
+        def _():
+            out_copy(unit - 2, slot).wait()
+
+        out_buf[slot, seq] = rounded.astype(jnp.float32)
+        for part in range(2):
+            out_buf[slot, 2 + part] = wide_sum(xq_out[slot, part], xq_in[slot, part])
+
+    def stage_six(unit, slot):
+        xp_copy(slot).wait()
+        out_buf[slot, 1 - seq] = xp_in[slot].astype(jnp.float32)
+        out_copy(unit, slot).start()
+
+    def turn(at):
+        def when_due(behind, run):
+            unit = at - behind
+
+            @pl.when(jnp.logical_and(unit >= 0, unit < total))
+            def _():
+                run(unit, lax.rem(unit, 2))
+
+        when_due(5, stage_six)
+        when_due(4, stage_five)
+        when_due(3, lambda unit, slot: stage_four(slot))
+        when_due(2, lambda unit, slot: stage_three(slot))
+        when_due(1, lambda unit, slot: stage_two(slot))
+
+        @pl.when(at < total)
+        def _():
+            compute(at)
+            core_copy(lax.rem(at, 2)).start()
+
+    def finish():
+        for unit in (total - 2, total - 1):
+            out_copy(unit, unit % 2).wait()
+
+    return prefetch, turn, finish, total + 5
+
+
+def scatter_scratch(toks, lines):
+    bf = jnp.bfloat16
+    dma = pltpu.SemaphoreType.DMA
+
+    buf_f32 = pltpu.VMEM((2, PARTS, 64, TILE), jnp.float32)
+
+    def buf(*shape):
+        return pltpu.VMEM((2,) + shape, bf)
+
+    return [
+        buf(toks, D),
+        pltpu.VMEM((toks, FF), bf),
+        buf(toks, D),
+        buf(toks, TILE),
+        dma((4, 2)),
+        buf(2, PARTS, lines, 2, 64, TILE),
+        buf(PARTS, lines, 2, 64, TILE),
+        buf(lines, 2, 64, TILE),
+        buf(lines, 2, 64, TILE),
+        buf(lines, 2, 64, TILE),
+        buf(lines, 2, 64, TILE),
+        buf(lines, 2, 64, TILE),
+        buf(lines, 2, 64, TILE),
+        buf(lines, 64, TILE),
+        buf(lines, 64, TILE),
+        buf(lines, 64, TILE),
+        buf(lines, 2, 64, TILE),
+        buf(lines - 1, 2, 64, TILE),
+        buf(lines, 64, TILE),
+        buf(lines - 1, 64, TILE),
+        buf(2, 64, TILE),
+        buf(2, 64, TILE),
+        buf(64, TILE),
+        buf(64, TILE),
+        dma((2, 2)),
+        dma((2, 2)),
+        dma((2, 2)),
+        dma((2, 2)),
+        dma((2, lines - 1, 2)),
+        dma((2, lines - 1, 2)),
+        dma((2, 2)),
+        dma((2, 2)),
+        buf_f32,
+        dma((2,)),
+    ]
+
+
+def summary_pieces(lines, refs):
+    (
+        flat_own,
+        mod_own,
+        flat_all,
+        mod_all,
+        core_in,
+        core_total,
+        x_in,
+        x_total,
+        y_in,
+        y_total,
+        z_in,
+        pair_sem,
+        line_sem,
+    ) = refs
+    seq = lax.axis_index("seq")
+    dp = lax.axis_index("dp")
+    core = lax.rem(dp, 2)
+    why = lax.rem(dp // 2, 2)
+    zed = dp // 4
+    core_peer = {"seq": seq, "dp": dp + 1 - 2 * core}
+    x_peer = {"seq": 1 - seq, "dp": dp}
+    y_peer = {"seq": seq, "dp": dp + 2 - 4 * why}
+    places = [lax.rem(zed + ahead, lines) for ahead in range(1, lines)]
+    z_peers = [{"seq": seq, "dp": there * 4 + 2 * why + core} for there in places]
+
+    def remote(source, target, sems, peer):
+        return pltpu.make_async_remote_copy(
+            src_ref=source,
+            dst_ref=target,
+            send_sem=sems.at[0],
+            recv_sem=sems.at[1],
+            device_id=peer,
+            device_id_type=MESH,
+        )
+
+    def same(view, sems, peer):
+        return remote(view, view, sems, peer)
+
+    flat_core = remote(flat_own.at[1 - core], core_in, pair_sem.at[0], core_peer)
+    flat_x = remote(core_total, x_in, pair_sem.at[1], x_peer)
+    flat_y = remote(x_total, y_in, pair_sem.at[2], y_peer)
+    flat_z = [
+        remote(y_total.at[there], z_in.at[at], line_sem.at[0, at], peer)
+        for at, (there, peer) in enumerate(zip(places, z_peers))
+    ]
+    back_z = [
+        same(flat_all.at[core, zed], line_sem.at[1, at], peer) for at, peer in enumerate(z_peers)
+    ]
+    back_core = same(flat_all.at[core], pair_sem.at[3], core_peer)
+    mod_x = remote(mod_own, mod_all.at[zed, why, core, seq], pair_sem.at[4], x_peer)
+    mod_z = [
+        same(mod_all.at[zed, why, core], line_sem.at[2, at], peer)
+        for at, peer in enumerate(z_peers)
+    ]
+    mod_y = same(mod_all.at[:, why, core], pair_sem.at[5], y_peer)
+    mod_core = same(mod_all.at[:, :, core], pair_sem.at[6], core_peer)
+
+    def first():
+        mod_all[zed, why, core, seq] = mod_own[...]
+        flat_core.start()
+        mod_x.start()
+
+    def second():
+        flat_core.wait()
+        core_total[...] = flat_own[core] + core_in[...]
+        flat_x.start()
+        mod_x.wait()
+        for copy in mod_z:
+            copy.start()
+
+    def third():
+        flat_x.wait()
+        x_total[...] = core_total[...] + x_in[...]
+        flat_y.start()
+        for copy in mod_z:
+            copy.wait()
+        mod_y.start()
+
+    def fourth():
+        flat_y.wait()
+        y_total[...] = x_total[...] + y_in[...]
+        for copy in flat_z:
+            copy.start()
+
+    def fifth():
+        total = y_total[zed]
+        for at, copy in enumerate(flat_z):
+            copy.wait()
+            total = total + z_in[at]
+        flat_all[core, zed] = total
+        for copy in back_z:
+            copy.start()
+        mod_y.wait()
+        mod_core.start()
+
+    def sixth():
+        for copy in back_z:
+            copy.wait()
+        back_core.start()
+        mod_core.wait()
+
+    def seventh():
+        back_core.wait()
+
+    return [first, second, third, fourth, fifth, sixth, seventh]
+
+
+def summary_scratch(lines):
+    f32 = jnp.float32
+    part = pltpu.VMEM((lines, 8, D), f32)
+    return [
+        pltpu.VMEM((2, lines, 8, D), f32),
+        pltpu.VMEM((32, D), jnp.bfloat16),
+        part,
+        part,
+        part,
+        part,
+        part,
+        part,
+        pltpu.VMEM((lines - 1, 8, D), f32),
+        pltpu.SemaphoreType.DMA((7, 2)),
+        pltpu.SemaphoreType.DMA((3, lines - 1, 2)),
+    ]
+
+
+def whole_backward_kernel(lines, *refs):
+    refs = list(refs)
+
+    def take(count):
+        taken, refs[:] = tuple(refs[:count]), refs[count:]
+        return taken
+
+    (grad_in,) = take(1)
+    operands = [take(10), take(10)]
+    kept = [take(4), take(4)]
+    mod_ref, keep_ref, final_rows, head_rows, misc_row, flat_in = take(6)
+    units_out = take(1)
+    outs = [take(4), take(4)]
+    flat_all, mod_all = take(2)
+    back_scratch = take(19)
+    d_mod_ref, *d_bias_refs = take(3)
+    (grad_sem,) = take(1)
+    summary = take(11)
+    scatter_refs = tuple(refs)
+
+    dp = lax.axis_index("dp")
+    seq = lax.axis_index("seq")
+    core = lax.rem(dp, 2)
+    why = lax.rem(dp // 2, 2)
+    zed = dp // 4
+    barrier = pltpu.get_barrier_semaphore()
+    peers = [dp + 1 - 2 * core, dp + 2 - 4 * why]
+    peers += [lax.rem(zed + ahead, lines) * 4 + 2 * why + core for ahead in range(1, lines)]
+    for peer in [{"seq": seq, "dp": peer} for peer in peers] + [{"seq": 1 - seq, "dp": dp}]:
+        pl.semaphore_signal(barrier, inc=1, device_id=peer, device_id_type=MESH)
+
+    load = pltpu.make_async_copy(grad_in, back_scratch[0], grad_sem.at[0])
+    load.start()
+    begins, steps = [], []
+    for at, mod_at in ((0, 12), (1, 0)):
+        begin, step = backward_pieces(
+            operands[at] + (mod_ref, keep_ref),
+            outs[at],
+            (d_mod_ref, d_bias_refs[at]) + back_scratch,
+            mod_at,
+        )
+        begins.append(begin)
+        steps.append(step)
+    begins[0]()
+    load.wait()
+
+    sources = []
+    for at in range(2):
+        merged, a_one, a_two, act = kept[at]
+        d_down, d_up, d_attn, d_qkv = outs[at]
+        sources.append((merged, a_one, a_two, act, d_attn, d_qkv, d_up, d_down))
+    prefetch, scatter, scatter_finish, turns = scatter_pieces(
+        lines, sources, units_out + scatter_refs
+    )
+    flat_own, mod_own = summary[:2]
+    summary_steps = summary_pieces(
+        lines, (flat_own, mod_own, flat_all, mod_all) + summary[2:]
+    )
+
+    def put(row, value):
+        flat_own[row // (8 * lines), row // 8 % lines, row % 8 : row % 8 + 1, :] = value
+
+    def collect():
+        d_patch = back_scratch[0][...].astype(jnp.bfloat16)
+        for layer in range(2):
+            for row in range(9):
+                put(9 * layer + row, d_bias_refs[1 - layer][:, row * D : (row + 1) * D])
+        put(18, jnp.sum(d_patch.astype(jnp.float32), axis=0, keepdims=True))
+        g_patch = dot_nn(flat_in[...], d_patch)
+        for row in range(16):
+            put(19 + row, g_patch[row : row + 1, :])
+            put(35 + row, head_rows[row : row + 1, :])
+        put(51, misc_row[...])
+        for row in range(52, 16 * lines):
+            put(row, jnp.zeros((1, D), jnp.float32))
+        d_mod_ref[24:28, :] = final_rows[...]
+        d_mod_ref[28:32, :] = jnp.zeros((4, D), jnp.float32)
+        mod_own[...] = d_mod_ref[...].astype(jnp.bfloat16)
+
+    def back(at, carry):
+        @pl.when(at < BACKWARD_STEPS)
+        def _():
+            steps[0](at)
+
+        @pl.when(at == BACKWARD_STEPS)
+        def _():
+            begins[1]()
+
+        @pl.when(jnp.logical_and(at >= BACKWARD_STEPS, at < 2 * BACKWARD_STEPS))
+        def _():
+            steps[1](at - BACKWARD_STEPS)
+
+        return carry
+
+    lax.fori_loop(0, 2, back, 0)
+    prefetch(jnp.int32(0))
+    pl.semaphore_wait(barrier, 2 + lines)
+
+    def turn(at, carry):
+        @pl.when(at <= 20)
+        def _():
+            lax.fori_loop(2 + at * 5 // 2, 2 + (at + 1) * 5 // 2, back, 0)
+
+        prefetch(at + 1)
+        scatter(at)
+
+        @pl.when(at == 21)
+        def _():
+            collect()
+
+        for offset, run in enumerate(summary_steps):
+
+            @pl.when(at == 21 + offset)
+            def _():
+                run()
+
+        return carry
+
+    lax.fori_loop(0, turns, turn, 0)
+    scatter_finish()
+
+
+def whole_backward(
+    grad, inputs, saved, weights, mods, keep, final_rows, head_rows, misc_row, flat_in, lines
+):
+    toks = grad.shape[0]
+    vmem = pl.BlockSpec(memory_space=pltpu.VMEM)
+    hbm = pl.BlockSpec(memory_space=pl.ANY)
+    operands = [grad]
+    for at in (1, 0):
+        operands += backward_operands(inputs[at], saved[at], weights[at])
+    for at in (1, 0):
+        a_one, _, merged, _, _, a_two, _, act, _, _ = saved[at]
+        operands += [merged, a_one, a_two, act]
+    layer_outs = [jax.ShapeDtypeStruct((toks, width), kind) for width, kind in BACKWARD_OUTS]
+    outs = pl.pallas_call(
+        functools.partial(whole_backward_kernel, lines),
+        out_shape=[jax.ShapeDtypeStruct((24, PARTS, 64, TILE), jnp.float32)]
+        + layer_outs
+        + layer_outs
+        + [
+            jax.ShapeDtypeStruct((2, lines, 8, D), jnp.float32),
+            jax.ShapeDtypeStruct((lines, 2, 2, 2, 32, D), jnp.bfloat16),
+        ],
+        in_specs=[hbm] * len(operands) + [vmem] * 6,
+        out_specs=[hbm] * 9 + [vmem] * 2,
+        scratch_shapes=backward_scratch(toks)
+        + [
+            pltpu.VMEM((32, D), jnp.float32),
+            pltpu.VMEM((1, 9 * D), jnp.float32),
+            pltpu.VMEM((1, 9 * D), jnp.float32),
+            pltpu.SemaphoreType.DMA((1,)),
+        ]
+        + summary_scratch(lines)
+        + scatter_scratch(toks, lines),
+        compiler_params=pltpu.CompilerParams(
+            collective_id=1, has_side_effects=True, vmem_limit_bytes=61 * 1024 * 1024
+        ),
+        cost_estimate=pl.CostEstimate(
+            flops=104 * toks * D * D,
+            bytes_accessed=300 * 1024 * 1024,
+            transcendentals=8 * toks * D,
+        ),
+    )(*operands, mods, keep, final_rows, head_rows, misc_row, flat_in)
+    return outs[0], outs[9], outs[10]
+
+
 def gather_rows(shard):
     return lax.all_gather(shard.astype(jnp.bfloat16), "dp", axis=0, tiled=True)
 
@@ -1482,33 +1806,16 @@
     return lax.psum(owned, "seq").astype(jnp.float32)
 
 
-def weight_sums(factors):
-    dp_parts = lax.axis_size("dp")
-    if not kernels_fit():
-        return [
-            (
-                reduce_rows(matdot(a_one.T, d_qkv)),
-                reduce_rows(matdot(merged.T, d_attn)),
-                reduce_rows(matdot(a_two.T, d_up)),
-                reduce_rows(matdot(activated.T, d_down)),
-            )
-            for merged, a_one, a_two, activated, d_attn, d_qkv, d_up, d_down in factors
-        ]
-    units = scatter_sums([each for layer in factors for each in layer], dp_parts // 4)
-    units = units.reshape(LAYERS, 12, PARTS, 64, TILE)
-
+def unit_sums(units):
     def by_columns(some):
         return some.transpose(2, 0, 1, 3).reshape(64, some.shape[0] * D)
 
-    return [
-        (
-            by_columns(layer[1:4]),
-            by_columns(layer[:1]),
-            by_columns(layer[4:8]),
-            layer[8:].transpose(1, 2, 0, 3).reshape(PARTS * 64, D),
-        )
-        for layer in units
-    ]
+    return (
+        by_columns(units[9:]),
+        by_columns(units[8:9]),
+        by_columns(units[4:8]),
+        units[:4].transpose(1, 2, 0, 3).reshape(PARTS * 64, D),
+    )
 
 
 def adamw(weight, gradient, first, second, rate):
@@ -1696,49 +2003,112 @@
         .reshape(toks, OUT_CH)
         .astype(jnp.bfloat16)
     )
-    g_head = matdot(a_final.T, d_head)
     d_a_final = dot_nt(d_head, head_full).reshape(images, tok_rows, D)
     d_stream, d_final_shift, d_final_scale = final_back(d_a_final)
     d_stream = d_stream.reshape(toks, D)
-    layer_factors = [None] * LAYERS
-    layer_bias_grads = [None] * LAYERS
-    modul_grads = [None] * LAYERS
-    for at in reversed(range(LAYERS)):
-        d_stream, d_mod, layer_factors[at], d_bias = backward_layer(
+    d_bias_head = column_sum(d_head)
+    if by_kernel:
+        d_noise = d_pred.astype(jnp.bfloat16).reshape(toks, PATCH_IN)
+        misc_row = jnp.concatenate([d_bias_head, loss_part[None], count_part[None]])
+        misc_row = jnp.pad(misc_row, (0, D - misc_row.shape[0])).reshape(1, D)
+        units, flat, mod_all = whole_backward(
             d_stream,
-            inputs_kept[at],
-            saved_kept[at],
+            inputs_kept,
+            saved_kept,
+            weights_kept,
             mods,
-            6 * images * at,
             keep_rows,
-            weights_kept[at],
-        )
-        modul_grads[at] = d_mod.reshape(6, images, D).transpose(1, 0, 2).reshape(images, 6 * D)
-        layer_bias_grads[at] = d_bias.reshape(-1)
-    d_mod_own = jnp.concatenate(modul_grads + [d_final_shift, d_final_scale], axis=1).astype(
-        jnp.bfloat16
-    )
-    d_patch = d_stream.astype(jnp.bfloat16)
-    flat = jnp.concatenate(
-        [column_sum(d_patch), jnp.zeros((2 * D,), jnp.float32), column_sum(d_mod_own)]
-        + layer_bias_grads
-        + [column_sum(d_head), loss_part[None], count_part[None]]
-        + [matdot(flat_in.T, d_patch).reshape(-1), g_head.reshape(-1)]
-    )
-    flat, d_mod_own, layer_factors = lax.optimization_barrier((flat, d_mod_own, layer_factors))
-    flat = lax.psum(flat, ("seq", "dp"))
-    d_modulation = lax.all_gather(d_mod_own, ("dp", "seq"), axis=0, tiled=True)
-    layer_sums = weight_sums(layer_factors)
-    d_cond_act = lax.dot_general(
-        d_modulation, cond_own, (((1,), (1,)), ((), ())), preferred_element_type=jnp.float32
-    )
+            jnp.concatenate([d_final_shift, d_final_scale], axis=0),
+            matdot(d_noise.T, a_final),
+            misc_row,
+            flat_in.T,
+            lines,
+        )
+        layer_sums = [unit_sums(units[12:]), unit_sums(units[:12])]
+        d_modulation = (
+            mod_all[..., : pieces * images, :]
+            .reshape(dp_parts * seq_parts, pieces, images, D)
+            .transpose(0, 2, 1, 3)
+            .reshape(everyone, cond_cols)
+        )
+        flat = flat.reshape(64, D)
+        d_bias_mod = column_sum(d_modulation)
+        d_bias_patch = flat[18]
+        d_bias_layers = flat[:18].reshape(-1)
+        d_bias_head, loss_sum, loss_count = (
+            flat[51, :OUT_CH],
+            flat[51, OUT_CH],
+            flat[51, OUT_CH + 1],
+        )
+        own_flat = lax.dynamic_slice(flat, (0, own_place), (64, own_cols))
+        s_patch = own_flat[19:35]
+        s_head = own_flat[35:51].T.reshape(own_cols, 4, 1, OUT_CH // 8)
+        s_head = jnp.concatenate([s_head, jnp.zeros_like(s_head)], axis=2)
+        s_head = s_head.reshape(own_cols, OUT_CH)
+    else:
+        layer_sums = [None] * LAYERS
+        layer_bias_grads = [None] * LAYERS
+        modul_grads = [None] * LAYERS
+        for at in reversed(range(LAYERS)):
+            d_stream, d_mod, factors, d_bias = backward_layer(
+                d_stream,
+                inputs_kept[at],
+                saved_kept[at],
+                mods,
+                6 * images * at,
+                keep_rows,
+                weights_kept[at],
+            )
+            merged, a_one, a_two, active, d_attn, d_qkv, d_up, d_down = factors
+            layer_sums[at] = (
+                reduce_rows(matdot(a_one.T, d_qkv)),
+                reduce_rows(matdot(merged.T, d_attn)),
+                reduce_rows(matdot(a_two.T, d_up)),
+                reduce_rows(matdot(active.T, d_down)),
+            )
+            modul_grads[at] = d_mod.reshape(6, images, D).transpose(1, 0, 2).reshape(images, 6 * D)
+            layer_bias_grads[at] = d_bias.reshape(-1)
+        d_mod_own = jnp.concatenate(
+            modul_grads + [d_final_shift, d_final_scale], axis=1
+        ).astype(jnp.bfloat16)
+        d_patch = d_stream.astype(jnp.bfloat16)
+        d_modulation = lax.all_gather(d_mod_own, ("dp", "seq"), axis=0, tiled=True)
+        (
+            d_bias_patch,
+            d_bias_mod,
+            d_bias_layers,
+            d_bias_head,
+            loss_sum,
+            loss_count,
+            g_patch,
+            g_head,
+        ) = lax.psum(
+            (
+                column_sum(d_patch),
+                column_sum(d_mod_own),
+                jnp.concatenate(layer_bias_grads),
+                d_bias_head,
+                loss_part,
+                count_part,
+                matdot(flat_in.T, d_patch),
+                matdot(a_final.T, d_head),
+            ),
+            ("seq", "dp"),
+        )
+        s_patch = lax.dynamic_slice(g_patch, (0, own_place), (PATCH_IN, own_cols))
+        s_head = lax.dynamic_slice(g_head, (own_place, 0), (own_cols, OUT_CH))
+    d_cond_act = dot_nt(d_modulation, cond_own)
     _, silu_back = jax.vjp(jax.nn.silu, condition)
     d_condition = silu_back(d_cond_act)[0]
     d_time_own = d_condition.astype(jnp.bfloat16)
-    d_time = lax.all_gather(d_time_own, "dp", axis=1, tiled=True)
-    d_time_hidden = lax.dot_general(
-        d_time, time_full, (((1,), (1,)), ((), ())), preferred_element_type=jnp.float32
-    )
+    if by_kernel:
+        d_time = gather_small(
+            jnp.pad(d_time_own.T, ((0, 0), (0, everyone))), lines, 5
+        )
+        d_time = d_time[:, :everyone].T
+    else:
+        d_time = lax.all_gather(d_time_own, "dp", axis=1, tiled=True)
+    d_time_hidden = dot_nt(d_time, time_full)
     _, time_back = jax.vjp(jax.nn.silu, time_pre)
     d_time_pre = time_back(d_time_hidden)[0].astype(jnp.bfloat16)
     s_cond = matdot(cond_act.T, d_modulation)
@@ -1748,16 +2118,14 @@
         features.T, lax.dynamic_slice(d_time_pre, (0, own_place), (everyone, own_cols))
     )
     bias_grad = jnp.concatenate(
-        [flat[:D], column_sum(d_time_pre), column_sum(d_time), flat[3 * D : NBIAS]]
-    )
-    loss_sum, loss_count = flat[NBIAS], flat[NBIAS + 1]
-    patch_at = NBIAS + 2
-    head_at = patch_at + PATCH_IN * D
-    s_patch = lax.dynamic_slice(
-        flat[patch_at:head_at].reshape(PATCH_IN, D), (0, own_place), (PATCH_IN, own_cols)
-    )
-    s_head = lax.dynamic_slice(
-        flat[head_at:].reshape(D, OUT_CH), (own_place, 0), (own_cols, OUT_CH)
+        [
+            d_bias_patch,
+            column_sum(d_time_pre),
+            column_sum(d_time),
+            d_bias_mod,
+            d_bias_layers,
+            d_bias_head,
+        ]
     )
     s_embed = jnp.concatenate([s_patch, g_freq, g_time], axis=0)
     s_qkv = jnp.stack([layer_sums[at][0] for at in range(LAYERS)])

time: 848 us -> 766 us (0.903)
  Pallas kernels: 669 us -> 594 us
  blocking collectives: 20.9 us -> 0 us
  local copies, waits for them, and re-layouts: 67.2 us -> 86.6 us
    pallas_call x3 -> x1, Pallas kernels: 389 us -> 295 us  [whole_backward(): pl.pallas_call(functools.partial(whole_backward_kernel, lines), out_shape...]
    all_gather x1 -> x0, blocking collectives: 20.9 us -> none  [body(): d_time = lax.all_gather(d_time_own, 'dp', axis=1, tiled=True)]
    pallas_call x1, Pallas kernels: 263 us -> 273 us  [whole_forward(): pl.pallas_call(functools.partial(whole_forward_kernel, lines), out_shape=...]
    pallas_call x1 -> x2, Pallas kernels: 16.3 us -> 26.2 us  [gather_small(): pl.pallas_call(functools.partial(gather_small_kernel, lines), out_shape=j...]
    unnamed x139 -> x138, local copies, waits for them, and re-layouts: 16.1 us -> 17.5 us
  transfers between devices with their start and end apart: 4 -> 2, of which waited for: 0 -> 0; matrix products, arithmetic and copies ran while one was open for 11% -> 13% of each run, Pallas kernels for 34% -> 2%
where the time goes in v5:
time: 766 us; the launch traced here: 765 us
  Pallas kernels  594 us (78%)
  local copies, waits for them, and re-layouts  86.6 us (11%)
  other arithmetic  40.8 us (5%)
  matrix products  23.6 us (3%)
  between operations  15.9 us (2%)
    pallas_call x1, Pallas kernels, whole_backward(): pl.pallas_call(functools.partial(whole_backward_kernel, lines), out_shape...  295 us
    pallas_call x1, Pallas kernels, whole_forward(): pl.pallas_call(functools.partial(whole_forward_kernel, lines), out_shape=...  273 us
    pallas_call x2, Pallas kernels, gather_small(): pl.pallas_call(functools.partial(gather_small_kernel, lines), out_shape=j...  26.2 us
    sub x7, other arithmetic, adamw(): weight - rate * (first_hat / (jnp.sqrt(second_hat) + EPSILON) + DECAY * w...  18.7 us
    unnamed x138, local copies, waits for them, and re-layouts  17.5 us
  transfers between devices with their start and end apart: 2, of which 0 were waited for; matrix products, arithmetic and copies ran while one was open for 13% of the time, Pallas kernels for 2%

profile of v5, /device:TPU:0, one launch (start us, length us, event | category | flops | bytes accessed | tf_op | source)
XLA Modules:
  0.0 764.5 jit_solution(16647557854528133416)
XLA Ops:
  9.6 3.0 collective-permute-start
  18.2 16.3 %shard_map.527 = bf16[4,2,2,64,384]{4,3,2,1,0:T(8,128)(2,1)} custom-call(bf16[64,384]{1,0:T(8,128)(2,1)} %fusion.33.own_ref), custom_call_target="tpu_custom_call" | custom-call | bytes 3145728 | tf_op jit(solution)/shard_map/pallas_call | solution.py:1126
  36.3 2.4 convert_element_type.170
  52.7 2.6 copy.215
  55.4 3.8 reshape.521.refs_8_
  62.6 273.4 %shard_map.528 = (bf16[4,2,2,64,3072]{4,3,2,1,0:T(8,128)(2,1)}, bf16[4,2,2,64,1024]{4,3,2,1,0:T(8,128)(2,1)}, bf16[4,2,2,64,4096]{4,3,2,1,0:T(8,128)(2,1)}, bf16...) custom-call(bf16[64,3072]{1,0:T(8,128)(2,1)} %get-tuple-element.145., ...), custom_call_target="tpu_custom_call" | custom-call | flops 25769803776 | bytes 201326592 | tf_op jit(solution)/shard_map/pallas_call | solution.py:1051
  350.7 294.8 %shard_map.529 = (f32[24,4,64,256]{3,2,1,0:T(8,128)}, bf16[512,1024]{1,0:T(8,128)(2,1)}, bf16[512,4096]{1,0:T(8,128)(2,1)}, bf16[512,1024]{1,0:T(8,128)(2,1)}, b...) custom-call(f32[512,1024]{1,0:T(8,128)} %bitcast.180, ...), custom_call_target="tpu_custom_call" | custom-call | flops 55834574848 | bytes 314572800 | tf_op jit(solution)/shard_map/pallas_call | solution.py:1756
  645.5 4.0 reshape.522
  652.4 4.3 slice_bitcast_fusion
  658.5 2.7 slice_bitcast_fusion.4
  665.6 9.9 %shard_map.530 = bf16[4,2,2,64,128]{4,3,2,1,0:T(8,128)(2,1)} custom-call(bf16[64,128]{1,0:T(8,128)(2,1)} %pad.16.own_ref), custom_call_target="tpu_custom_call" | custom-call | bytes 1048576 | tf_op jit(solution)/shard_map/pallas_call | solution.py:1126
  681.3 2.4 constant_dynamic-update-slice_fusion.7
  687.1 2.9 copy.207
  690.0 2.7 stack_reshape.28
  696.7 2.7 stack_reshape.29
  705.1 2.5 copy.203
  707.6 2.4 stack_reshape.24
  713.5 2.4 stack_reshape.25
  724.4 2.7 multiply_subtract_fusion.6
  727.1 2.6 multiply_subtract_fusion.4
  731.1 5.9 multiply_subtract_fusion.1
  737.0 3.1 multiply_subtract_fusion.3
  741.9 5.9 multiply_subtract_fusion
  747.8 3.9 multiply_subtract_fusion.2
  (263 shorter events, 89.3 us)
Async XLA Ops:
  7.2 28.8 %copy-start.30 = (f32[35872]{0:T(1024)S(1)}, f32[35872]{0:T(1024)}, u32[]{:S(2)}) copy-start(f32[35872]{0:T(1024)} %param.61) | copy-start | bytes 430468
  7.2 744.6 %all-gather.2.cloned.1.call-start = ((), (), s32[]{:S(2)}) async-start(), calls=%async_computation | async-start | bytes 2228224 | tf_op jit(solution)/shard_map/all_gather | solution.py:1986
  9.6 50.5 %collective-permute-start = (f32[2,128,33]{1,0,2:T(2,128)S(1)}, f32[2,128,33]{1,0,2:T(2,128)S(1)}, u32[]{:S(2)}, u32[]{:S(2)}) collective-permute-start(f32[2,128,33]{1,0,2:T(2,128)S(1)} %constant_dynamic-slice_fusion.1), channel_id=1, source_target_pairs={{0,16},{16,0},{1,17},{17,1},{2,18},{18,2},{3,19},{19,3},{4,20},{20... | collective-permute-start | bytes 101384 | tf_op jit(solution)/shard_map/ppermute | solution.py:1909
  36.3 9.8 %copy-start.57 = (s32[64]{0:T(128)}, s32[64]{0:T(128)S(1)}, u32[]{:S(2)}) copy-start(s32[64]{0:T(128)S(1)} %eq.24) | copy-start | bytes 772
  39.0 8.3 %copy-start.1 = (bf16[64,14336]{1,0:T(8,128)(2,1)}, bf16[64,14336]{1,0:T(8,128)(2,1)S(1)}, u32[]{:S(2)}) copy-start(bf16[64,14336]{1,0:T(8,128)(2,1)S(1)} %convert_element_type.170) | copy-start | bytes 5505028
  47.3 12.7 %copy-start.46 = (f32[64,64]{1,0:T(8,128)}, f32[64,64]{1,0:T(8,128)S(1)}, u32[]{:S(2)}) copy-start(f32[64,64]{1,0:T(8,128)S(1)} %get-tuple-element.177) | copy-start | bytes 49156
  55.4 5.4 copy-start.13
  60.7 275.3 %copy-start.48 = (bf16[2,8,2,256]{3,1,2,0:T(8,128)(2,1)}, bf16[2,8,2,256]{3,1,2,0:T(8,128)(2,1)S(1)}, u32[]{:S(2)}) copy-start(bf16[2,8,2,256]{3,1,2,0:T(8,128)(2,1)S(1)} %copy.228) | copy-start | bytes 49156
  722.9 6.8 copy-start.49
  724.3 6.7 copy-start.20
  724.4 5.3 copy-start.56
  724.4 6.6 copy-start.11
  731.1 5.9 copy-start.10
  731.1 5.9 copy-start.25
  731.1 5.9 copy-start.26
  731.1 9.0 %copy-start.60 = (f32[64,14336]{1,0:T(8,128)S(1)}, f32[64,14336]{1,0:T(8,128)}, u32[]{:S(2)}) copy-start(f32[64,14336]{1,0:T(8,128)} %param.57) | copy-start | bytes 11010052
  737.0 4.9 copy-start.59
  741.9 5.9 copy-start.6
  741.9 5.9 copy-start.21
  741.9 5.9 copy-start.22
  751.7 4.3 copy-start.37
  751.8 4.5 copy-start.27
  751.8 4.5 copy-start.33
  751.8 4.5 copy-start.34
  (41 other events, 115.5 us)
Sparse Core Ops, SparseCore 0:
  675.7 41.1 all-gather.1

commit v6 on v5

--- a/solution.py
+++ b/solution.py
@@ -34,11 +34,12 @@
 TILE = 256
 PARTS = 4
 SHARED = 640
+SHARED_ROWS = 80
 GATHER_LAGS = (2, 2, 2, 1)
 HALF = 512
 GELU_IN = math.sqrt(2.0 / math.pi)
 GELU_CUBE = 0.044715
-FORWARD_STEPS = 26
+FORWARD_STEPS = 30
 BACKWARD_STEPS = 27
 
 
@@ -171,6 +172,7 @@
                 (a_two_buf, a_two_out),
                 (down_buf, down_out),
                 (x_two_buf, x_two_out),
+                (act_buf, act_out),
             ]
         )
     ]
@@ -182,7 +184,7 @@
 
     def tall_load(tile, slot):
         return pltpu.make_async_copy(
-            w_down.at[tile // 2, lax.rem(tile, 2)], tall_buf.at[slot], load_sem.at[1, slot]
+            w_down.at[:, :, :, :, column_tile(tile, TILE)], tall_buf.at[slot], load_sem.at[1, slot]
         )
 
     def tile_saves(tile, slot):
@@ -190,16 +192,13 @@
             pltpu.make_async_copy(
                 pre_buf.at[slot], pre_out.at[:, column_tile(tile)], tile_sem.at[0, slot]
             ),
-            pltpu.make_async_copy(
-                act_buf.at[slot], act_out.at[:, column_tile(tile)], tile_sem.at[1, slot]
-            ),
         ]
 
     def wide_tile(slot):
         return wide_buf[slot].reshape(D, HALF)
 
     def tall_tile(slot):
-        return tall_buf[slot].reshape(HALF, D)
+        return tall_buf[slot].reshape(FF, TILE)
 
     def loads(at, run):
         slot = lax.rem(at, 2)
@@ -215,7 +214,10 @@
         @pl.when(within(at, 18, 8))
         def _():
             run(wide_load(w_up, at - 18, slot))
-            run(tall_load(at - 18, slot))
+
+        @pl.when(within(at, 26, 4))
+        def _():
+            run(tall_load(at - 26, slot))
 
     def modulated(source, target, piece):
         def rows_of(block, carry):
@@ -306,26 +308,28 @@
                 pre_buf[slot, rows, :] = pre
                 inner = jnp.tanh(GELU_IN * (pre + GELU_CUBE * pre * pre * pre))
                 active = (0.5 * pre * (1.0 + inner)).astype(bf)
-                act_buf[slot, rows, :] = active
-                part = dot_nn(active, tall_tile(slot))
-
-                @pl.when(tile == 0)
-                def _():
-                    down_buf[rows, :] = part + bias_ref[:, 8 * D : 9 * D]
-
-                @pl.when(tile > 0)
-                def _():
-                    down_buf[rows, :] += part
+                act_buf[rows, column_tile(tile)] = active
 
             for copy in tile_saves(tile, slot):
                 copy.start()
 
-        @pl.when(at == FORWARD_STEPS - 1)
-        def _():
+        @pl.when(at == 26)
+        def _():
+            saves[8].start()
+
+        @pl.when(within(at, 26, 4))
+        def _():
+            cols = column_tile(at - 26, TILE)
+            bias_cols = column_tile(at - 26 + 32, TILE)
             for image in range(images):
                 rows = pl.ds(image * toks, toks)
-                gate = mod_ref[mod_at + 10 + image : mod_at + 11 + image, :]
-                x_two_buf[rows, :] = x_one_buf[rows, :] + gate * down_buf[rows, :]
+                down = dot_nn(act_buf[rows, :], tall_tile(slot)) + bias_ref[:, bias_cols]
+                down_buf[rows, cols] = down
+                gate = mod_ref[mod_at + 10 + image : mod_at + 11 + image, cols]
+                x_two_buf[rows, cols] = x_one_buf[rows, cols] + gate * down
+
+        @pl.when(at == FORWARD_STEPS - 1)
+        def _():
             saves[6].start()
             saves[7].start()
 
@@ -363,14 +367,14 @@
         pltpu.VMEM((toks, D), f32),
         pltpu.VMEM((toks, D), bf),
         pltpu.VMEM((2, toks, HALF), f32),
-        pltpu.VMEM((2, toks, HALF), bf),
+        pltpu.VMEM((toks, FF), bf),
         pltpu.VMEM((toks, D), f32),
         pltpu.VMEM((toks, D), f32),
         pltpu.VMEM((2, 4, 2, 2, 64, HALF), bf),
-        pltpu.VMEM((2, 2, 256, D), bf),
+        pltpu.VMEM((2, 4, 2, 2, 256, TILE), bf),
         pltpu.SemaphoreType.DMA((2, 2)),
         pltpu.SemaphoreType.DMA((2, 2)),
-        pltpu.SemaphoreType.DMA((8,)),
+        pltpu.SemaphoreType.DMA((9,)),
     ]
 
 
@@ -807,24 +811,23 @@
         pl.semaphore_signal(barrier, inc=1, device_id=peer, device_id_type=MESH)
     pl.semaphore_wait(barrier, 2 + lines)
 
-    def places(kind, unit):
+    def views(kind, unit):
         at = unit - firsts[kind]
         if kind % 4 == 3:
-            return pl.multiple_of(at * 64, 64), 0
-        return 0, pl.multiple_of(at * D, D)
-
-    def span(first, begin, size):
-        return pl.ds(pl.multiple_of(first + begin, 128), size)
+            cols = column_tile(at, TILE)
+            mine = pl.ds(pl.multiple_of(seq * SHARED_ROWS, 16), SHARED_ROWS)
+            rest = pl.ds(2 * SHARED_ROWS, PARTS * 64 - 2 * SHARED_ROWS)
+            return (mine, cols), (rest, cols), (slice(None), cols)
+        first = pl.multiple_of(at * D, D)
+        halved = pl.ds(first, SHARED)
+        rest = pl.ds(pl.multiple_of(first + SHARED, 128), D - SHARED)
+        mine = pl.ds(pl.multiple_of(seq * 32, 32), 32)
+        return (mine, halved), (slice(None), rest), (slice(None), pl.ds(first, D))
 
     def copies(stage, kind, unit):
         slot = unit
         own, every = pairs[kind]
-        row, first = places(kind, unit)
-        rows = pl.ds(row, 64)
-        mine = pl.ds(pl.multiple_of(row + seq * 32, 32), 32)
-        halved = span(first, 0, SHARED)
-        rest = span(first, SHARED, D - SHARED)
-        whole = span(first, 0, D)
+        shared, rest, whole = views(kind, unit)
 
         def remote(source, target, sems, peer):
             return pltpu.make_async_remote_copy(
@@ -841,18 +844,18 @@
 
         if stage == 0:
             return [
-                remote(own.at[band, cols], every.at[zed, why, core, band, cols], sems, peer)
-                for band, cols, kinds in ((mine, halved, zp_sem), (rows, rest, zq_sem))
+                remote(own.at[view], every.at[(zed, why, core) + view], sems, peer)
+                for view, kinds in ((shared, zp_sem), (rest, zq_sem))
                 for sems, peer in [(kinds.at[slot, at], z_peers[at]) for at in range(lines - 1)]
             ]
         if stage == 1:
             return [
-                same(every.at[:, why, core, mine, halved], yp_sem.at[slot], y_peer),
-                same(every.at[:, why, core, rows, rest], yq_sem.at[slot], y_peer),
+                same(every.at[(slice(None), why, core) + shared], yp_sem.at[slot], y_peer),
+                same(every.at[(slice(None), why, core) + rest], yq_sem.at[slot], y_peer),
             ]
         if stage == 2:
-            return [same(every.at[:, :, core, mine, halved], x_sem.at[slot], x_peer)]
-        return [same(every.at[:, :, core, rows, whole], core_sem.at[slot], core_peer)]
+            return [same(every.at[(slice(None), slice(None), core) + shared], x_sem.at[slot], x_peer)]
+        return [same(every.at[(slice(None), slice(None), core) + whole], core_sem.at[slot], core_peer)]
 
     def each_kind(unit, run):
         ends = firsts[1:] + [total]
@@ -1026,19 +1029,19 @@
 
         @pl.when(within(at, 10, 13))
         def _():
-            run(first, 2 * (at - 10), 2 * (at - 9))
+            run(first, 5 * (at - 10) // 2, 5 * (at - 9) // 2)
 
         @pl.when(at == 23)
         def _():
             first_finish()
 
-        @pl.when(at >= 24)
-        def _():
-            run(second, 18 * (at - 24) // 7, 18 * (at - 23) // 7)
+        @pl.when(at >= 23)
+        def _():
+            run(second, 13 * (at - 23) // 4, 13 * (at - 22) // 4)
 
         return carry
 
-    lax.fori_loop(0, steps + 4, turn, 0)
+    lax.fori_loop(0, steps + 2, turn, 0)
     second_finish()
 
 
@@ -1806,18 +1809,6 @@
     return lax.psum(owned, "seq").astype(jnp.float32)
 
 
-def unit_sums(units):
-    def by_columns(some):
-        return some.transpose(2, 0, 1, 3).reshape(64, some.shape[0] * D)
-
-    return (
-        by_columns(units[9:]),
-        by_columns(units[8:9]),
-        by_columns(units[4:8]),
-        units[:4].transpose(1, 2, 0, 3).reshape(PARTS * 64, D),
-    )
-
-
 def adamw(weight, gradient, first, second, rate):
     first_new = BETA_ONE * first + (1.0 - BETA_ONE) * gradient
     second_new = BETA_TWO * second + (1.0 - BETA_TWO) * gradient * gradient
@@ -1828,6 +1819,41 @@
         first_new,
         second_new,
     )
+
+
+def unit_adamw_kernel(by_rows, grad_ref, weight_ref, first_ref, second_ref, *outs):
+    for part in range(PARTS):
+        if by_rows:
+            place = (0, slice(part * 64, part * 64 + 64), slice(None))
+        else:
+            place = (0, slice(None), slice(part * TILE, part * TILE + TILE))
+        moved = adamw(
+            weight_ref[place], grad_ref[0, part], first_ref[place], second_ref[place], RATE_MATRIX
+        )
+        for out, value in zip(outs, moved):
+            out[place] = value
+
+
+def unit_adamw(weight, units, first, second, first_unit, by_rows):
+    layers, rows, width = weight.shape
+    block = (1, rows, TILE) if by_rows else (1, rows, D)
+    spec = pl.BlockSpec(block, lambda layer, at: (layer, 0, at))
+    per_layer = units.shape[0] // layers
+    grad_spec = pl.BlockSpec(
+        (1, PARTS, 64, TILE),
+        lambda layer, at: ((layers - 1 - layer) * per_layer + first_unit + at, 0, 0, 0),
+    )
+    return pl.pallas_call(
+        functools.partial(unit_adamw_kernel, by_rows),
+        out_shape=[jax.ShapeDtypeStruct(weight.shape, jnp.float32)] * 3,
+        grid=(layers, width // block[2]),
+        in_specs=[grad_spec, spec, spec, spec],
+        out_specs=[spec] * 3,
+        compiler_params=pltpu.CompilerParams(vmem_limit_bytes=32 * 1024 * 1024),
+        cost_estimate=pl.CostEstimate(
+            flops=16 * weight.size, bytes_accessed=28 * weight.size, transcendentals=weight.size
+        ),
+    )(units, weight, first, second)
 
 
 def body(
@@ -2024,7 +2050,6 @@
             flat_in.T,
             lines,
         )
-        layer_sums = [unit_sums(units[12:]), unit_sums(units[:12])]
         d_modulation = (
             mod_all[..., : pieces * images, :]
             .reshape(dp_parts * seq_parts, pieces, images, D)
@@ -2128,26 +2153,40 @@
         ]
     )
     s_embed = jnp.concatenate([s_patch, g_freq, g_time], axis=0)
-    s_qkv = jnp.stack([layer_sums[at][0] for at in range(LAYERS)])
-    s_proj = jnp.stack([layer_sums[at][1] for at in range(LAYERS)])
-    s_up = jnp.stack([layer_sums[at][2] for at in range(LAYERS)])
-    s_down = jnp.stack([layer_sums[at][3] for at in range(LAYERS)])
     new_embed, new_first_embed, new_second_embed = adamw(
         embed_rows, s_embed, first_embed, second_embed, RATE_MATRIX
     )
     new_table, new_first_table, new_second_table = adamw(
         class_table, s_table, first_table, second_table, RATE_TABLE
     )
-    new_qkv, new_first_qkv, new_second_qkv = adamw(
-        qkv_weight, s_qkv, first_qkv, second_qkv, RATE_MATRIX
-    )
-    new_proj, new_first_proj, new_second_proj = adamw(
-        proj_weight, s_proj, first_proj, second_proj, RATE_MATRIX
-    )
-    new_up, new_first_up, new_second_up = adamw(up_weight, s_up, first_up, second_up, RATE_MATRIX)
-    new_down, new_first_down, new_second_down = adamw(
-        down_weight, s_down, first_down, second_down, RATE_MATRIX
-    )
+    if by_kernel:
+        new_qkv, new_first_qkv, new_second_qkv = unit_adamw(
+            qkv_weight, units, first_qkv, second_qkv, 9, False
+        )
+        new_proj, new_first_proj, new_second_proj = unit_adamw(
+            proj_weight, units, first_proj, second_proj, 8, False
+        )
+        new_up, new_first_up, new_second_up = unit_adamw(
+            up_weight, units, first_up, second_up, 4, False
+        )
+        new_down, new_first_down, new_second_down = unit_adamw(
+            down_weight, units, first_down, second_down, 0, True
+        )
+    else:
+        s_qkv = jnp.stack([layer_sums[at][0] for at in range(LAYERS)])
+        s_proj = jnp.stack([layer_sums[at][1] for at in range(LAYERS)])
+        s_up = jnp.stack([layer_sums[at][2] for at in range(LAYERS)])
+        s_down = jnp.stack([layer_sums[at][3] for at in range(LAYERS)])
+        new_qkv, new_first_qkv, new_second_qkv = adamw(
+            qkv_weight, s_qkv, first_qkv, second_qkv, RATE_MATRIX
+        )
+        new_proj, new_first_proj, new_second_proj = adamw(
+            proj_weight, s_proj, first_proj, second_proj, RATE_MATRIX
+        )
+        new_up, new_first_up, new_second_up = adamw(up_weight, s_up, first_up, second_up, RATE_MATRIX)
+        new_down, new_first_down, new_second_down = adamw(
+            down_weight, s_down, first_down, second_down, RATE_MATRIX
+        )
     new_cond, new_first_cond, new_second_cond = adamw(
         cond_weight, s_cond, first_cond, second_cond, RATE_MATRIX
     )

time: 766 us -> 723 us (0.944)
  local copies, waits for them, and re-layouts: 86.6 us -> 44.6 us
  other arithmetic: 40.8 us -> 27.5 us
    transpose x11 -> x0, local copies, waits for them, and re-layouts: 22.7 us -> none  [the longest x8 14.9 us: by_columns(): return some.transpose(2, 0, 1, 3).reshape(64, some.shape[0] * D)]
    another operation x13 -> x1, local copies, waits for them, and re-layouts: 18.8 us -> 0.1 us  [the longest x3 6.8 us: body(): s_up = jnp.stack([layer_sums[at][2] for at in range(LAYERS)])]
    sub x7 -> x3, other arithmetic: 18.7 us -> 2.6 us  [adamw(): weight - rate * (first_hat / (jnp.sqrt(second_hat) + EPSILON) + DECAY * w...]
    pallas_call x0 -> x4, Pallas kernels: none -> 14.5 us  [unit_adamw(): pl.pallas_call(functools.partial(unit_adamw_kernel, by_rows), out_shape=[...]
    unnamed x138 -> x112, local copies, waits for them, and re-layouts: 17.5 us -> 13 us
  transfers between devices with their start and end apart: 2 -> 2, of which waited for: 0 -> 0; matrix products, arithmetic and copies ran while one was open for 13% -> 8% of each run, Pallas kernels for 2% -> 47%
where the time goes in v6:
time: 723 us; the launch traced here: 715 us
  Pallas kernels  599 us (83%)
  local copies, waits for them, and re-layouts  44.6 us (6%)
  other arithmetic  27.5 us (4%)
  matrix products  24.9 us (3%)
  between operations  15.8 us (2%)
    pallas_call x1, Pallas kernels, whole_backward(): pl.pallas_call(functools.partial(whole_backward_kernel, lines), out_shape...  291 us
    pallas_call x1, Pallas kernels, whole_forward(): pl.pallas_call(functools.partial(whole_forward_kernel, lines), out_shape=...  266 us
    pallas_call x2, Pallas kernels, gather_small(): pl.pallas_call(functools.partial(gather_small_kernel, lines), out_shape=j...  27.3 us
    pallas_call x4, Pallas kernels, unit_adamw(): pl.pallas_call(functools.partial(unit_adamw_kernel, by_rows), out_shape=[...  14.5 us
    dot_general x8, matrix products, matdot(): return jnp.dot(left, right, preferred_element_type=jnp.float32)  14.5 us
  transfers between devices with their start and end apart: 2, of which 0 were waited for; matrix products, arithmetic and copies ran while one was open for 8% of the time, Pallas kernels for 47%

profile of v6, /device:TPU:0, one launch (start us, length us, event | category | flops | bytes accessed | tf_op | source)
XLA Modules:
  0.0 715.1 jit_solution(11085290924290696716)
XLA Ops:
  9.6 3.0 collective-permute-start
  18.2 16.3 %shard_map.527 = bf16[4,2,2,64,384]{4,3,2,1,0:T(8,128)(2,1)} custom-call(bf16[64,384]{1,0:T(8,128)(2,1)} %fusion.29.own_ref), custom_call_target="tpu_custom_call" | custom-call | bytes 3145728 | tf_op jit(solution)/shard_map/pallas_call | solution.py:1129
  36.3 3.6 convert_element_type.170
  47.5 3.1 fusion.4
  54.4 4.1 copy.183
  58.6 3.8 reshape.521.refs_8_
  64.5 3.1 bitcast_add_fusion.1.refs_10_.refs_11_
  67.7 266.4 %shard_map.528 = (bf16[4,2,2,64,3072]{4,3,2,1,0:T(8,128)(2,1)}, bf16[4,2,2,64,1024]{4,3,2,1,0:T(8,128)(2,1)}, bf16[4,2,2,64,4096]{4,3,2,1,0:T(8,128)(2,1)}, bf16...) custom-call(bf16[64,3072]{1,0:T(8,128)(2,1)} %get-tuple-element.149., ...), custom_call_target="tpu_custom_call" | custom-call | flops 25769803776 | bytes 201326592 | tf_op jit(solution)/shard_map/pallas_call | solution.py:1054
  335.8 2.1 multiply_reduce_fusion.2
  342.9 2.1 fusion.80.refs_32_
  345.0 2.6 fusion.66
  348.7 1.9 broadcast_add_fusion
  353.2 291.1 %shard_map.529 = (f32[24,4,64,256]{3,2,1,0:T(8,128)}, bf16[512,1024]{1,0:T(8,128)(2,1)}, bf16[512,4096]{1,0:T(8,128)(2,1)}, bf16[512,1024]{1,0:T(8,128)(2,1)}, b...) custom-call(f32[512,1024]{1,0:T(8,128)} %bitcast.160, ...), custom_call_target="tpu_custom_call" | custom-call | flops 55834574848 | bytes 314572800 | tf_op jit(solution)/shard_map/pallas_call | solution.py:1759
  646.0 4.9 reshape.522
  650.9 2.1 copy.185
  656.0 11.1 %shard_map.530 = bf16[4,2,2,64,128]{4,3,2,1,0:T(8,128)(2,1)} custom-call(bf16[64,128]{1,0:T(8,128)(2,1)} %pad.16.own_ref), custom_call_target="tpu_custom_call" | custom-call | bytes 1048576 | tf_op jit(solution)/shard_map/pallas_call | solution.py:1129
  667.0 2.1 convert_reduce_fusion
  670.8 2.8 copy-done
  678.6 3.7 shard_map.531
  682.3 4.8 shard_map.533
  687.3 4.8 shard_map.534
  692.0 2.1 fusion.76
  696.6 5.9 multiply_subtract_fusion
  702.6 2.2 convert_reduce_fusion.2
  (214 shorter events, 49.8 us)
Async XLA Ops:
  7.2 28.8 %copy-start.25 = (f32[35872]{0:T(1024)S(1)}, f32[35872]{0:T(1024)}, u32[]{:S(2)}) copy-start(f32[35872]{0:T(1024)} %param.61) | copy-start | bytes 430468
  7.2 695.4 %all-gather.2.cloned.1.call-start = ((), (), s32[]{:S(2)}) async-start(), calls=%async_computation | async-start | bytes 2228224 | tf_op jit(solution)/shard_map/all_gather | solution.py:2012
  9.6 54.3 %collective-permute-start = (f32[2,128,33]{1,0,2:T(2,128)S(1)}, f32[2,128,33]{1,0,2:T(2,128)S(1)}, u32[]{:S(2)}, u32[]{:S(2)}) collective-permute-start(f32[2,128,33]{1,0,2:T(2,128)S(1)} %constant_dynamic-slice_fusion.1), channel_id=1, source_target_pairs={{0,16},{16,0},{1,17},{17,1},{2,18},{18,2},{3,19},{19,3},{4,20},{20... | collective-permute-start | bytes 101384 | tf_op jit(solution)/shard_map/ppermute | solution.py:1935
  36.3 10.0 %copy-start.44 = (s32[64]{0:T(128)}, s32[64]{0:T(128)S(1)}, u32[]{:S(2)}) copy-start(s32[64]{0:T(128)S(1)} %eq.24) | copy-start | bytes 772
  47.5 5.1 copy-start.38
  47.5 15.7 %copy-start.34 = (f32[64,64]{1,0:T(8,128)}, f32[64,64]{1,0:T(8,128)S(1)}, u32[]{:S(2)}) copy-start(f32[64,64]{1,0:T(8,128)S(1)} %get-tuple-element.181) | copy-start | bytes 49156
  64.5 269.5 %copy-start.36 = (bf16[2,8,2,256]{3,1,2,0:T(8,128)(2,1)}, bf16[2,8,2,256]{3,1,2,0:T(8,128)(2,1)S(1)}, u32[]{:S(2)}) copy-start(bf16[2,8,2,256]{3,1,2,0:T(8,128)(2,1)S(1)} %copy.196) | copy-start | bytes 49156
  682.3 4.8 copy-start.3
  682.3 4.8 copy-start.8
  682.3 4.8 copy-start.9
  687.1 7.0 copy-start.24
  687.1 7.1 copy-start.37
  687.1 7.1 copy-start.42
  687.2 7.1 copy-start.43
  687.2 7.8 %copy-start.35 = (f32[64,64]{1,0:T(8,128)S(1)}, f32[64,64]{1,0:T(8,128)}, u32[]{:S(2)}) copy-start(f32[64,64]{1,0:T(8,128)} %copy-done.34) | copy-start | bytes 49156
  687.2 8.0 %copy-start.29 = (f32[1001,64]{0,1:T(8,128)S(1)}, f32[1001,64]{0,1:T(8,128)}, u32[]{:S(2)}) copy-start(f32[1001,64]{0,1:T(8,128)} %param.40) | copy-start | bytes 768772
  687.2 8.0 %copy-start.45 = (s32[64]{0:T(128)S(1)}, s32[64]{0:T(128)}, u32[]{:S(2)}) copy-start(s32[64]{0:T(128)} %copy-done.44) | copy-start | bytes 772
  687.2 8.0 %copy-start.48 = (f32[1001,64]{0,1:T(8,128)S(1)}, f32[1001,64]{0,1:T(8,128)}, u32[]{:S(2)}) copy-start(f32[1001,64]{0,1:T(8,128)} %param.41) | copy-start | bytes 768772
  687.2 8.0 %copy-start.49 = (f32[1001,64]{0,1:T(8,128)S(1)}, f32[1001,64]{0,1:T(8,128)}, u32[]{:S(2)}) copy-start(f32[1001,64]{0,1:T(8,128)} %param.42) | copy-start | bytes 768772
  687.2 9.4 %copy-start.22 = (f32[64,14336]{1,0:T(8,128)S(1)}, f32[64,14336]{1,0:T(8,128)}, u32[]{:S(2)}) copy-start(f32[64,14336]{1,0:T(8,128)} %param.55) | copy-start | bytes 11010052
  687.2 9.4 %copy-start.46 = (f32[64,14336]{1,0:T(8,128)S(1)}, f32[64,14336]{1,0:T(8,128)}, u32[]{:S(2)}) copy-start(f32[64,14336]{1,0:T(8,128)} %param.56) | copy-start | bytes 11010052
  687.3 9.4 %copy-start.47 = (f32[64,14336]{1,0:T(8,128)S(1)}, f32[64,14336]{1,0:T(8,128)}, u32[]{:S(2)}) copy-start(f32[64,14336]{1,0:T(8,128)} %param.57) | copy-start | bytes 11010052
  692.0 4.6 copy-start.20
  692.0 4.6 copy-start.39
  (30 other events, 80.6 us)
Sparse Core Ops, SparseCore 0:
  350.7 50.9 all-gather.1

commit v7 on v6

--- a/solution.py
+++ b/solution.py
@@ -95,6 +95,10 @@
     return lax.dot_general(
         left, right, (((0,), (0,)), ((), ())), preferred_element_type=jnp.float32
     )
+
+
+def wide_sum(one, other):
+    return one.astype(jnp.float32) + other.astype(jnp.float32)
 
 
 def column_tile(at, size=HALF):
@@ -956,36 +960,41 @@
         @pl.when(at == 1)
         def _():
             to_core.wait()
-            core_total[...] = partial_ref[:, :, core] + core_in[...]
+            core_total[...] = wide_sum(partial_ref[:, :, core], core_in[...]).astype(jnp.bfloat16)
             to_y.start()
 
         @pl.when(at == 4)
         def _():
             to_y.wait()
-            y_total[...] = core_total[:, why] + y_in[...]
+            y_total[...] = wide_sum(core_total[:, why], y_in[...]).astype(jnp.bfloat16)
             for copy in to_z:
                 copy.start()
 
         @pl.when(at == 8)
         def _():
-            total = y_total[zed] + bias_ref[...]
+            total = y_total[zed].astype(jnp.float32)
             for ahead, copy in enumerate(to_z):
                 copy.wait()
-                total = total + z_in[ahead]
-            mods_ref[...] = total
+                total = total + z_in[ahead].astype(jnp.float32)
+            for image in range(2):
+                for piece in range(mods_ref.shape[0] // 2):
+                    row, source = 2 * piece + image, 16 * image + piece
+                    mods_ref[row : row + 1, :] = (
+                        total[source : source + 1, :] + bias_ref[row : row + 1, :]
+                    )
 
     return step
 
 
-def modulation_scratch(lines, rows):
+def modulation_scratch(lines):
     dma = pltpu.SemaphoreType.DMA
-    f32 = jnp.float32
+    bf = jnp.bfloat16
     return [
-        pltpu.VMEM((lines, 2, rows, D), f32),
-        pltpu.VMEM((lines, 2, rows, D), f32),
-        pltpu.VMEM((lines, rows, D), f32),
-        pltpu.VMEM((lines, rows, D), f32),
-        pltpu.VMEM((lines - 1, rows, D), f32),
+        pltpu.VMEM((lines, 2, 32, D), bf),
+        pltpu.VMEM((lines, 2, 32, D), bf),
+        pltpu.VMEM((lines, 32, D), bf),
+        pltpu.VMEM((lines, 32, D), bf),
+        pltpu.VMEM((lines - 1, 32, D), bf),
         dma((2,)),
         dma((2,)),
         dma((lines - 1, 2)),
@@ -1062,7 +1071,7 @@
         in_specs=[vmem] * 14,
         out_specs=[hbm] * (8 + 2 * len(FORWARD_OUTS)) + [vmem],
         scratch_shapes=gather_scratch(lines, 2)
-        + modulation_scratch(lines, rows)
+        + modulation_scratch(lines)
         + forward_scratch(toks),
         compiler_params=pltpu.CompilerParams(
             collective_id=2, has_side_effects=True, vmem_limit_bytes=58 * 1024 * 1024
@@ -1324,9 +1333,6 @@
                 return carry
 
             lax.fori_loop(0, 2 * lines, rows, 0)
-
-    def wide_sum(one, other):
-        return one.astype(jnp.float32) + other.astype(jnp.float32)
 
     def out_copy(unit, slot):
         return pltpu.make_async_copy(out_buf.at[slot], out_ref.at[unit], out_sem.at[slot])
@@ -1967,8 +1973,7 @@
     plane_act = lax.dynamic_index_in_dim(
         cond_act.reshape(dp_parts, seq_parts, images, own_cols), seq_at, 1, keepdims=False
     ).reshape(dp_parts * images, own_cols)
-    partial = matdot(plane_act, cond_own).reshape(dp_parts, images, pieces, D)
-    partial = partial.transpose(0, 2, 1, 3).reshape(dp_parts, pieces * images, D)
+    partial = matdot(plane_act, cond_own)
     mod_bias = jnp.repeat(all_biases[3 * D : bias_base].reshape(pieces, D), images, axis=0)
 
     position = position_table(jnp.arange(tok_rows, dtype=jnp.int32), D, GRID)
@@ -1982,9 +1987,11 @@
         for at in range(LAYERS)
     ]
     if by_kernel:
+        partial = partial.astype(jnp.bfloat16).reshape(dp_parts * images, pieces, D)
+        partial = jnp.pad(partial, ((0, 0), (0, 16 - pieces), (0, 0)))
         weights_kept, saved_kept, mods = whole_forward(
             shards,
-            partial.reshape(lines, 2, 2, pieces * images, D),
+            partial.reshape(lines, 2, 2, 16 * images, D),
             mod_bias,
             stream,
             layer_bias,
@@ -1992,6 +1999,8 @@
             lines,
         )
     else:
+        partial = partial.reshape(dp_parts, images, pieces, D).transpose(0, 2, 1, 3)
+        partial = partial.reshape(dp_parts, pieces * images, D)
         mods = mod_bias + lax.psum_scatter(
             partial, "dp", scatter_dimension=0, tiled=True
         ).reshape(pieces * images, D)

time: 723 us -> 699 us (0.967)
  Pallas kernels: 599 us -> 583 us
    pallas_call x1, Pallas kernels: 266 us -> 242 us  [whole_forward(): pl.pallas_call(functools.partial(whole_forward_kernel, lines), out_shape=...]
    pallas_call x1, Pallas kernels: 291 us -> 300 us  [whole_backward(): pl.pallas_call(functools.partial(whole_backward_kernel, lines), out_shape...]
    another operation x3 -> x1, local copies, waits for them, and re-layouts: 8.05 us -> 0.1 us  [the longest x2 7.95 us: body(): partial.reshape(lines, 2, 2, pieces * images, D)]
  transfers between devices with their start and end apart: 2 -> 2, of which waited for: 0 -> 0; matrix products, arithmetic and copies ran while one was open for 8% -> 8% of each run, Pallas kernels for 47% -> 49%
where the time goes in v7:
time: 699 us; the launch traced here: 692 us
  Pallas kernels  583 us (83%)
  local copies, waits for them, and re-layouts  40.4 us (6%)
  other arithmetic  25.6 us (4%)
  matrix products  24.2 us (3%)
  between operations  15.8 us (2%)
    pallas_call x1, Pallas kernels, whole_backward(): pl.pallas_call(functools.partial(whole_backward_kernel, lines), out_shape...  300 us
    pallas_call x1, Pallas kernels, whole_forward(): pl.pallas_call(functools.partial(whole_forward_kernel, lines), out_shape=...  242 us
    pallas_call x2, Pallas kernels, gather_small(): pl.pallas_call(functools.partial(gather_small_kernel, lines), out_shape=j...  26.5 us
    pallas_call x4, Pallas kernels, unit_adamw(): pl.pallas_call(functools.partial(unit_adamw_kernel, by_rows), out_shape=[...  14.5 us
  transfers between devices with their start and end apart: 2, of which 0 were waited for; matrix products, arithmetic and copies ran while one was open for 8% of the time, Pallas kernels for 49%

profile of v7, /device:TPU:0, one launch (start us, length us, event | category | flops | bytes accessed | tf_op | source)
XLA Modules:
  0.0 692.4 jit_solution(11862301594915502774)
XLA Ops:
  9.6 3.0 collective-permute-start
  18.2 16.3 %shard_map.527 = bf16[4,2,2,64,384]{4,3,2,1,0:T(8,128)(2,1)} custom-call(bf16[64,384]{1,0:T(8,128)(2,1)} %fusion.29.own_ref), custom_call_target="tpu_custom_call" | custom-call | bytes 3145728 | tf_op jit(solution)/shard_map/pallas_call | solution.py:1138
  36.3 1.9 convert.46
  44.7 3.4 convolution_convert_fusion
  48.0 1.9 multiply_sine_fusion.1
  51.8 2.8 reshape.504
  54.6 2.4 pad.19
  58.5 3.1 bitcast_add_fusion.1.refs_10_.refs_11_
  61.6 242.1 %shard_map.528 = (bf16[4,2,2,64,3072]{4,3,2,1,0:T(8,128)(2,1)}, bf16[4,2,2,64,1024]{4,3,2,1,0:T(8,128)(2,1)}, bf16[4,2,2,64,4096]{4,3,2,1,0:T(8,128)(2,1)}, bf16...) custom-call(bf16[64,3072]{1,0:T(8,128)(2,1)} %get-tuple-element.149., ...), custom_call_target="tpu_custom_call" | custom-call | flops 25769803776 | bytes 201326592 | tf_op jit(solution)/shard_map/pallas_call | solution.py:1063
  305.6 2.1 multiply_reduce_fusion.2
  312.6 2.1 fusion.78.refs_32_
  314.8 2.6 fusion.64
  318.5 1.9 broadcast_add_fusion
  323.0 300.1 %shard_map.529 = (f32[24,4,64,256]{3,2,1,0:T(8,128)}, bf16[512,1024]{1,0:T(8,128)(2,1)}, bf16[512,4096]{1,0:T(8,128)(2,1)}, bf16[512,1024]{1,0:T(8,128)(2,1)}, b...) custom-call(f32[512,1024]{1,0:T(8,128)} %bitcast.141, ...), custom_call_target="tpu_custom_call" | custom-call | flops 55834574848 | bytes 314572800 | tf_op jit(solution)/shard_map/pallas_call | solution.py:1765
  624.8 4.9 reshape.526
  629.7 2.1 copy.164
  635.1 10.2 %shard_map.530 = bf16[4,2,2,64,128]{4,3,2,1,0:T(8,128)(2,1)} custom-call(bf16[64,128]{1,0:T(8,128)(2,1)} %pad.21.own_ref), custom_call_target="tpu_custom_call" | custom-call | bytes 1048576 | tf_op jit(solution)/shard_map/pallas_call | solution.py:1138
  645.3 2.1 convert_reduce_fusion
  648.5 2.8 copy-done
  656.3 3.7 shard_map.531
  660.0 4.8 shard_map.533
  664.9 4.8 shard_map.534
  673.9 5.9 multiply_subtract_fusion
  679.8 2.2 convert_reduce_fusion.2
  (209 shorter events, 47.5 us)
Async XLA Ops:
  7.2 28.8 %copy-start.24 = (f32[35872]{0:T(1024)S(1)}, f32[35872]{0:T(1024)}, u32[]{:S(2)}) copy-start(f32[35872]{0:T(1024)} %param.61) | copy-start | bytes 430468
  7.2 672.6 %all-gather.2.cloned.1.call-start = ((), (), s32[]{:S(2)}) async-start(), calls=%async_computation | async-start | bytes 2228224 | tf_op jit(solution)/shard_map/all_gather | solution.py:2021
  9.6 48.2 %collective-permute-start = (f32[2,128,33]{1,0,2:T(2,128)S(1)}, f32[2,128,33]{1,0,2:T(2,128)S(1)}, u32[]{:S(2)}, u32[]{:S(2)}) collective-permute-start(f32[2,128,33]{1,0,2:T(2,128)S(1)} %constant_dynamic-slice_fusion.1), channel_id=1, source_target_pairs={{0,16},{16,0},{1,17},{17,1},{2,18},{18,2},{3,19},{19,3},{4,20},{20... | collective-permute-start | bytes 101384 | tf_op jit(solution)/shard_map/ppermute | solution.py:1941
  36.3 8.1 %copy-start.42 = (s32[64]{0:T(128)}, s32[64]{0:T(128)S(1)}, u32[]{:S(2)}) copy-start(s32[64]{0:T(128)S(1)} %eq.24) | copy-start | bytes 772
  44.6 13.1 %copy-start.34 = (f32[64,64]{1,0:T(8,128)}, f32[64,64]{1,0:T(8,128)S(1)}, u32[]{:S(2)}) copy-start(f32[64,64]{1,0:T(8,128)S(1)} %get-tuple-element.181) | copy-start | bytes 49156
  51.8 5.2 slice-start
  58.5 245.3 %copy-start.36 = (bf16[2,8,2,256]{3,1,2,0:T(8,128)(2,1)}, bf16[2,8,2,256]{3,1,2,0:T(8,128)(2,1)S(1)}, u32[]{:S(2)}) copy-start(bf16[2,8,2,256]{3,1,2,0:T(8,128)(2,1)S(1)} %copy.173) | copy-start | bytes 49156
  660.0 4.8 copy-start.2
  660.0 4.8 copy-start.7
  660.0 4.8 copy-start.8
  664.8 6.6 copy-start.23
  664.8 6.7 copy-start.37
  664.8 6.7 copy-start.40
  664.8 6.7 copy-start.41
  664.8 7.4 %copy-start.29 = (f32[64,1024]{1,0:T(8,128)S(1)}, f32[64,1024]{1,0:T(8,128)}, u32[]{:S(2)}) copy-start(f32[64,1024]{1,0:T(8,128)} %copy-done.28) | copy-start | bytes 786436
  664.8 7.4 %copy-start.35 = (f32[64,64]{1,0:T(8,128)S(1)}, f32[64,64]{1,0:T(8,128)}, u32[]{:S(2)}) copy-start(f32[64,64]{1,0:T(8,128)} %copy-done.34) | copy-start | bytes 49156
  664.8 7.6 %copy-start.31 = (f32[1001,64]{0,1:T(8,128)S(1)}, f32[1001,64]{0,1:T(8,128)}, u32[]{:S(2)}) copy-start(f32[1001,64]{0,1:T(8,128)} %param.40) | copy-start | bytes 768772
  664.9 7.6 %copy-start.43 = (s32[64]{0:T(128)S(1)}, s32[64]{0:T(128)}, u32[]{:S(2)}) copy-start(s32[64]{0:T(128)} %copy-done.42) | copy-start | bytes 772
  664.9 7.6 %copy-start.46 = (f32[1001,64]{0,1:T(8,128)S(1)}, f32[1001,64]{0,1:T(8,128)}, u32[]{:S(2)}) copy-start(f32[1001,64]{0,1:T(8,128)} %param.41) | copy-start | bytes 768772
  664.9 7.6 %copy-start.47 = (f32[1001,64]{0,1:T(8,128)S(1)}, f32[1001,64]{0,1:T(8,128)}, u32[]{:S(2)}) copy-start(f32[1001,64]{0,1:T(8,128)} %param.42) | copy-start | bytes 768772
  664.9 9.0 %copy-start.20 = (bf16[8,8,14,1024]{3,1,2,0:T(8,128)(2,1)S(1)}, bf16[8,8,14,1024]{3,1,2,0:T(8,128)(2,1)}, u32[]{:S(2)}) copy-start(bf16[8,8,14,1024]{3,1,2,0:T(8,128)(2,1)} %copy-done.19) | copy-start | bytes 5505028
  664.9 9.0 %copy-start.44 = (f32[64,14336]{1,0:T(8,128)S(1)}, f32[64,14336]{1,0:T(8,128)}, u32[]{:S(2)}) copy-start(f32[64,14336]{1,0:T(8,128)} %param.56) | copy-start | bytes 11010052
  664.9 9.0 %copy-start.45 = (f32[64,14336]{1,0:T(8,128)S(1)}, f32[64,14336]{1,0:T(8,128)}, u32[]{:S(2)}) copy-start(f32[64,14336]{1,0:T(8,128)} %param.57) | copy-start | bytes 11010052
  679.8 4.4 copy-start.26
  (28 other events, 72.1 us)
Sparse Core Ops, SparseCore 0:
  320.5 56.9 all-gather.1

commit v8 on v7

--- a/solution.py
+++ b/solution.py
@@ -1703,8 +1703,13 @@
         for row in range(52, 16 * lines):
             put(row, jnp.zeros((1, D), jnp.float32))
         d_mod_ref[24:28, :] = final_rows[...]
-        d_mod_ref[28:32, :] = jnp.zeros((4, D), jnp.float32)
-        mod_own[...] = d_mod_ref[...].astype(jnp.bfloat16)
+        by_image = back_scratch[5]
+        for image in range(2):
+            for piece in range(16):
+                row = 2 * piece + image
+                value = d_mod_ref[row : row + 1, :] if piece < 14 else jnp.zeros((1, D), jnp.float32)
+                by_image[16 * image + piece : 16 * image + piece + 1, :] = value
+        mod_own[...] = by_image[:32, :].astype(jnp.bfloat16)
 
     def back(at, carry):
         @pl.when(at < BACKWARD_STEPS)
@@ -2059,12 +2064,7 @@
             flat_in.T,
             lines,
         )
-        d_modulation = (
-            mod_all[..., : pieces * images, :]
-            .reshape(dp_parts * seq_parts, pieces, images, D)
-            .transpose(0, 2, 1, 3)
-            .reshape(everyone, cond_cols)
-        )
+        d_modulation = mod_all.reshape(everyone, 16 * D)[:, :cond_cols]
         flat = flat.reshape(64, D)
         d_bias_mod = column_sum(d_modulation)
         d_bias_patch = flat[18]

time: 699 us -> 695 us (level)
  transfers between devices with their start and end apart: 2 -> 2, of which waited for: 0 -> 0; matrix products, arithmetic and copies ran while one was open for 8% -> 7% of each run, Pallas kernels for 49% -> 50%
where the time goes in v8:
time: 695 us; the launch traced here: 688 us
  Pallas kernels  583 us (84%)
  local copies, waits for them, and re-layouts  35.3 us (5%)
  matrix products  26.7 us (4%)
  other arithmetic  23.9 us (3%)
  between operations  15.8 us (2%)
    pallas_call x1, Pallas kernels, whole_backward(): pl.pallas_call(functools.partial(whole_backward_kernel, lines), out_shape...  300 us
    pallas_call x1, Pallas kernels, whole_forward(): pl.pallas_call(functools.partial(whole_forward_kernel, lines), out_shape=...  242 us
    pallas_call x2, Pallas kernels, gather_small(): pl.pallas_call(functools.partial(gather_small_kernel, lines), out_shape=j...  26.5 us
    pallas_call x4, Pallas kernels, unit_adamw(): pl.pallas_call(functools.partial(unit_adamw_kernel, by_rows), out_shape=[...  14.6 us
  transfers between devices with their start and end apart: 2, of which 0 were waited for; matrix products, arithmetic and copies ran while one was open for 7% of the time, Pallas kernels for 50%

profile of v8, /device:TPU:0, one launch (start us, length us, event | category | flops | bytes accessed | tf_op | source)
XLA Modules:
  0.0 688.2 jit_solution(8266718936924309920)
XLA Ops:
  9.6 3.0 collective-permute-start
  18.2 16.3 %shard_map.527 = bf16[4,2,2,64,384]{4,3,2,1,0:T(8,128)(2,1)} custom-call(bf16[64,384]{1,0:T(8,128)(2,1)} %fusion.32.own_ref), custom_call_target="tpu_custom_call" | custom-call | bytes 3145728 | tf_op jit(solution)/shard_map/pallas_call | solution.py:1138
  36.3 1.9 convert.46
  44.7 3.4 convolution_convert_fusion
  48.0 1.9 multiply_sine_fusion.1
  51.8 2.8 reshape.500
  54.5 2.4 pad.19
  58.5 3.1 bitcast_add_fusion.1.refs_10_.refs_11_
  61.6 242.2 %shard_map.528 = (bf16[4,2,2,64,3072]{4,3,2,1,0:T(8,128)(2,1)}, bf16[4,2,2,64,1024]{4,3,2,1,0:T(8,128)(2,1)}, bf16[4,2,2,64,4096]{4,3,2,1,0:T(8,128)(2,1)}, bf16...) custom-call(bf16[64,3072]{1,0:T(8,128)(2,1)} %get-tuple-element.149., ...), custom_call_target="tpu_custom_call" | custom-call | flops 25769803776 | bytes 201326592 | tf_op jit(solution)/shard_map/pallas_call | solution.py:1063
  303.8 1.8 reduce_sum.107
  305.6 2.1 multiply_reduce_fusion.2
  312.7 2.1 fusion.81.refs_32_
  314.8 2.6 fusion.67
  318.5 1.9 broadcast_add_fusion
  323.0 300.3 %shard_map.529 = (f32[24,4,64,256]{3,2,1,0:T(8,128)}, bf16[512,1024]{1,0:T(8,128)(2,1)}, bf16[512,4096]{1,0:T(8,128)(2,1)}, bf16[512,1024]{1,0:T(8,128)(2,1)}, b...) custom-call(f32[512,1024]{1,0:T(8,128)} %bitcast.131, ...), custom_call_target="tpu_custom_call" | custom-call | flops 55834574848 | bytes 314572800 | tf_op jit(solution)/shard_map/pallas_call | solution.py:1770
  624.9 4.2 reshape.513
  629.1 3.2 fusion.38
  632.9 10.2 %shard_map.530 = bf16[4,2,2,64,128]{4,3,2,1,0:T(8,128)(2,1)} custom-call(bf16[64,128]{1,0:T(8,128)(2,1)} %pad.21.own_ref), custom_call_target="tpu_custom_call" | custom-call | bytes 1048576 | tf_op jit(solution)/shard_map/pallas_call | solution.py:1138
  644.2 2.8 copy-done
  652.0 3.7 shard_map.531
  655.7 4.8 shard_map.533
  660.6 4.8 shard_map.534
  669.8 5.8 multiply_subtract_fusion
  675.7 2.2 convert_reduce_fusion.2
  (202 shorter events, 43.1 us)
Async XLA Ops:
  7.2 28.8 %copy-start.22 = (f32[35872]{0:T(1024)S(1)}, f32[35872]{0:T(1024)}, u32[]{:S(2)}) copy-start(f32[35872]{0:T(1024)} %param.61) | copy-start | bytes 430468
  7.2 668.5 %all-gather.2.cloned.1.call-start = ((), (), s32[]{:S(2)}) async-start(), calls=%async_computation | async-start | bytes 2228224 | tf_op jit(solution)/shard_map/all_gather | solution.py:2026
  9.6 48.2 %collective-permute-start = (f32[2,128,33]{1,0,2:T(2,128)S(1)}, f32[2,128,33]{1,0,2:T(2,128)S(1)}, u32[]{:S(2)}, u32[]{:S(2)}) collective-permute-start(f32[2,128,33]{1,0,2:T(2,128)S(1)} %constant_dynamic-slice_fusion.1), channel_id=1, source_target_pairs={{0,16},{16,0},{1,17},{17,1},{2,18},{18,2},{3,19},{19,3},{4,20},{20... | collective-permute-start | bytes 101384 | tf_op jit(solution)/shard_map/ppermute | solution.py:1946
  36.3 8.1 %copy-start.40 = (s32[64]{0:T(128)}, s32[64]{0:T(128)S(1)}, u32[]{:S(2)}) copy-start(s32[64]{0:T(128)S(1)} %eq.24) | copy-start | bytes 772
  44.6 13.1 %copy-start.32 = (f32[64,64]{1,0:T(8,128)}, f32[64,64]{1,0:T(8,128)S(1)}, u32[]{:S(2)}) copy-start(f32[64,64]{1,0:T(8,128)S(1)} %get-tuple-element.181) | copy-start | bytes 49156
  51.8 5.2 slice-start
  58.5 3.1 copy-start.36
  58.5 245.3 %copy-start.34 = (bf16[2,8,2,256]{3,1,2,0:T(8,128)(2,1)}, bf16[2,8,2,256]{3,1,2,0:T(8,128)(2,1)S(1)}, u32[]{:S(2)}) copy-start(bf16[2,8,2,256]{3,1,2,0:T(8,128)(2,1)S(1)} %copy.163) | copy-start | bytes 49156
  308.6 3.1 copy-start.37
  652.0 3.7 copy-start.5
  652.0 3.7 copy-start.6
  655.7 4.8 copy-start.2
  655.7 4.8 copy-start.7
  655.7 4.8 copy-start.8
  660.5 6.4 copy-start.21
  660.5 6.5 copy-start.16
  660.6 9.2 %copy-start.42 = (f32[64,14336]{1,0:T(8,128)S(1)}, f32[64,14336]{1,0:T(8,128)}, u32[]{:S(2)}) copy-start(f32[64,14336]{1,0:T(8,128)} %param.56) | copy-start | bytes 11010052
  660.6 9.2 %copy-start.43 = (f32[64,14336]{1,0:T(8,128)S(1)}, f32[64,14336]{1,0:T(8,128)}, u32[]{:S(2)}) copy-start(f32[64,14336]{1,0:T(8,128)} %param.57) | copy-start | bytes 11010052
  675.6 3.3 copy-start.23
  675.6 3.3 copy-start.30
  675.6 3.3 copy-start.31
  675.6 4.4 copy-start.20
  675.6 4.4 copy-start.24
  675.6 4.4 copy-start.25
  (26 other events, 57.9 us)
Sparse Core Ops, SparseCore 0:
  320.5 57.1 all-gather.1
